TPU v7x, 32 devices: a whole 2x2x4 slice. The times are simulated.
32 devices in a mesh: groups: 2 (over y), dp: 8 (over z, x), seq: 2 (over core).
Axes of the slice: x: 2, y: 2, z: 4, core: 2. Of those that a mesh axis runs over, the one named last changes fastest.
Arguments:
- query_rows: bfloat16 [6144, 1280], P(('groups', 'dp', 'seq')), parts along dimension 0, may hold values from -8 to 8
- key_rows: bfloat16 [6144, 1280], P(('groups', 'dp', 'seq')), parts along dimension 0, may hold values from -8 to 8
- value_rows: bfloat16 [6144, 1280], P(('groups', 'dp', 'seq')), parts along dimension 0, may hold values from -6 to 6
- grad_hosted: bfloat16 [8192, 1280], P(('groups', 'dp', 'seq')), parts along dimension 0, may hold values from -6 to 6
- image_grid: int32 [16, 2, 2], P('groups'), parts along dimension 0, may hold values from 8 to 16, as said below
- destination: int32 [16, 2], P('groups'), parts along dimension 0, may hold values from 0 to 7, as said below
Outputs:
- hosted_out: bfloat16 [8192, 1280], P(('groups', 'dp', 'seq')), parts along dimension 0
- grad_query: bfloat16 [6144, 1280], P(('groups', 'dp', 'seq')), parts along dimension 0
- grad_key: bfloat16 [6144, 1280], P(('groups', 'dp', 'seq')), parts along dimension 0
- grad_value: bfloat16 [6144, 1280], P(('groups', 'dp', 'seq')), parts along dimension 0
There are 2 independent parts, one for each index of `groups`. A program takes and returns all parts, laid end to end along the dimension named above; each array names one. Nothing has to cross between parts.
Inputs may be any that keep to these rules, and one draw needn't show every extreme that they name: `image_grid`: a rank's images together hold at most 384 patches; some rank lists an image of 16 x 16 patches and exactly 384 patches in all. `destination`: each column is a permutation of the ranks: every rank hosts exactly one image of each list position.
All inputs are finite; a program needn't handle non-finite values.
Results may differ from a plain program's by a relative error of at most 0.012.
The roundings to bfloat16 on the way count: a program that leaves them out, or rounds other values in their place, can miss the bound.
Values may be sent and summed in bfloat16 or wider, within the bound.
No kernel may reach another device: no remote copies, remote signals or barrier semaphores. Data moves between devices by JAX's collectives and lax.ppermute only.
A program may use at most 64 MiB of HBM per device.

v0:
```python
import jax
import jax.numpy as jnp
from jax import lax
from jax.sharding import PartitionSpec as P

HEAD_DIM = 80


def head_forward(query_head, key_head, value_head, allowed, live_rows):
    inv_root = HEAD_DIM ** (-0.5)
    scores = (
        jnp.einsum("qd,kd->qk", query_head, key_head, preferred_element_type=jnp.float32) * inv_root
    )
    scores = jnp.where(allowed, scores, -1e30)
    row_max = jnp.max(scores, axis=1, keepdims=True)
    weights = jnp.exp(scores - row_max)
    probabilities = weights / jnp.sum(weights, axis=1, keepdims=True)
    probabilities = jnp.where(live_rows[:, None], probabilities, 0.0)
    probs_bf = probabilities.astype(jnp.bfloat16)
    attended = jnp.dot(probs_bf, value_head, preferred_element_type=jnp.float32).astype(
        jnp.bfloat16
    )
    return (attended, probabilities, probs_bf)


def head_backward(query_head, key_head, value_head, grad_head, attended, probabilities, probs_bf):
    inv_root = HEAD_DIM ** (-0.5)
    grad_probs = jnp.einsum("qd,kd->qk", grad_head, value_head, preferred_element_type=jnp.float32)
    row_dot = jnp.sum(grad_head.astype(jnp.float32) * attended.astype(jnp.float32), axis=1)
    grad_scores = (probabilities * (grad_probs - row_dot[:, None]) * inv_root).astype(jnp.bfloat16)
    grad_query = jnp.dot(grad_scores, key_head, preferred_element_type=jnp.float32).astype(
        jnp.bfloat16
    )
    grad_key = jnp.einsum(
        "qk,qd->kd", grad_scores, query_head, preferred_element_type=jnp.float32
    ).astype(jnp.bfloat16)
    grad_value = jnp.einsum(
        "qk,qd->kd", probs_bf, grad_head, preferred_element_type=jnp.float32
    ).astype(jnp.bfloat16)
    return (grad_query, grad_key, grad_value)


def head_first(matrix, heads_here):
    return jnp.transpose(matrix.reshape(matrix.shape[0], heads_here, HEAD_DIM), (1, 0, 2))


def rows_first(tensor):
    return jnp.transpose(tensor, (1, 0, 2)).reshape(
        tensor.shape[1], tensor.shape[0] * tensor.shape[2]
    )


def key_masks(row_keys):
    allowed = (row_keys[:, None] == row_keys[None, :]) & (row_keys[None, :] >= 0)
    return (allowed, row_keys >= 0)


def both_passes(pieces, heads_here):
    query_blk, key_blk, value_blk, grad_blk, row_keys = pieces
    allowed, live_rows = key_masks(row_keys)

    def one_head(head_pieces):
        query_head, key_head, value_head, grad_head = head_pieces
        attended, probabilities, probs_bf = head_forward(
            query_head, key_head, value_head, allowed, live_rows
        )
        grad_query, grad_key, grad_value = head_backward(
            query_head, key_head, value_head, grad_head, attended, probabilities, probs_bf
        )
        return (attended, grad_query, grad_key, grad_value)

    results = lax.map(
        one_head,
        (
            head_first(query_blk, heads_here),
            head_first(key_blk, heads_here),
            head_first(value_blk, heads_here),
            head_first(grad_blk, heads_here),
        ),
    )
    return tuple((rows_first(result) for result in results))


def take_rows(source_rows, row_index):
    padded = jnp.concatenate(
        [source_rows, jnp.zeros((1, source_rows.shape[1]), source_rows.dtype)], axis=0
    )
    return padded[row_index]


def collect(entry, destination, slot_ids):
    picked = entry[slot_ids[None, :], destination]
    total = picked[:, 0]
    total = total + picked[:, 1]
    return total


def local(query_rows, key_rows, value_rows, grad_hosted, image_grid, destination):
    dp_size = lax.axis_size("dp")
    my_rank = lax.axis_index("dp")
    query_heads, key_heads, value_heads, grad_heads = (
        lax.all_to_all(query_rows, "seq", split_axis=1, concat_axis=0, tiled=True),
        lax.all_to_all(key_rows, "seq", split_axis=1, concat_axis=0, tiled=True),
        lax.all_to_all(value_rows, "seq", split_axis=1, concat_axis=0, tiled=True),
        lax.all_to_all(grad_hosted, "seq", split_axis=1, concat_axis=0, tiled=True),
    )
    buffer_rows = query_heads.shape[0]
    head_width = query_heads.shape[1]
    host_rows = grad_heads.shape[0]
    image_count = destination.shape[1]
    slot_rows = host_rows // image_count
    block_part = buffer_rows // dp_size
    heads_here = head_width // HEAD_DIM
    lengths = image_grid[:, :, 0] * image_grid[:, :, 1]
    starts = jnp.cumsum(lengths, axis=1) - lengths
    rank_ids = jnp.arange(dp_size, dtype=jnp.int32)
    slot_ids = jnp.arange(image_count, dtype=jnp.int32)
    source = jnp.sum(
        jnp.where(destination[None, :, :] == rank_ids[:, None, None], rank_ids[None, :, None], 0),
        axis=1,
    )
    source_lists = jnp.transpose(source)
    my_sources = lax.dynamic_index_in_dim(source, my_rank, 0, keepdims=False)
    chosen = my_sources[:, None] == rank_ids[None, :]
    slot_start = jnp.sum(jnp.where(chosen, jnp.transpose(starts), 0), axis=1)
    slot_length = jnp.sum(jnp.where(chosen, jnp.transpose(lengths), 0), axis=1)
    offsets = jnp.arange(slot_rows, dtype=jnp.int32)
    in_slot = offsets[None, :] < slot_length[:, None]
    gather_index = jnp.where(
        in_slot,
        slot_ids[:, None] * buffer_rows + slot_start[:, None] + offsets[None, :],
        image_count * buffer_rows,
    ).reshape(host_rows)
    hosted_keys = jnp.where(in_slot, slot_ids[:, None], -1).reshape(host_rows)
    row_ids = jnp.arange(buffer_rows, dtype=jnp.int32)
    relative = row_ids[None, :] - slot_start[:, None]
    in_image = (relative >= 0) & (relative < slot_length[:, None])
    return_index = jnp.where(in_image, slot_ids[:, None] * slot_rows + relative, host_rows).reshape(
        image_count * buffer_rows
    )
    spread_shape = (dp_size, block_part, head_width)
    route_shape = (image_count, dp_size, block_part, head_width)

    def to_hosts_layout(routed):
        return take_rows(routed.reshape(image_count * buffer_rows, head_width), gather_index)

    def from_hosts_layout(host_field):
        return take_rows(host_field, return_index).reshape(route_shape)

    spread_query, spread_key, spread_value = (
        lax.all_to_all(
            query_heads.reshape(spread_shape), "dp", split_axis=0, concat_axis=0, tiled=True
        ),
        lax.all_to_all(
            key_heads.reshape(spread_shape), "dp", split_axis=0, concat_axis=0, tiled=True
        ),
        lax.all_to_all(
            value_heads.reshape(spread_shape), "dp", split_axis=0, concat_axis=0, tiled=True
        ),
    )
    routed_query, routed_key, routed_value = (
        lax.all_to_all(spread_query[source_lists], "dp", split_axis=1, concat_axis=1, tiled=True),
        lax.all_to_all(spread_key[source_lists], "dp", split_axis=1, concat_axis=1, tiled=True),
        lax.all_to_all(spread_value[source_lists], "dp", split_axis=1, concat_axis=1, tiled=True),
    )
    got_query = to_hosts_layout(routed_query)
    got_key = to_hosts_layout(routed_key)
    got_value = to_hosts_layout(routed_value)
    block_count = host_rows // host_rows

    def in_blocks(matrix):
        return matrix.reshape(block_count, host_rows, head_width)

    def block_passes(pieces):
        return both_passes(pieces, heads_here)

    results = lax.map(
        block_passes,
        (
            in_blocks(got_query),
            in_blocks(got_key),
            in_blocks(got_value),
            in_blocks(grad_heads),
            hosted_keys.reshape(block_count, host_rows),
        ),
    )
    hosted_out = results[0].reshape(host_rows, head_width)
    back_query = from_hosts_layout(results[1].reshape(host_rows, head_width))
    back_key = from_hosts_layout(results[2].reshape(host_rows, head_width))
    back_value = from_hosts_layout(results[3].reshape(host_rows, head_width))
    entry_query, entry_key, entry_value = (
        lax.all_to_all(back_query, "dp", split_axis=1, concat_axis=1, tiled=True),
        lax.all_to_all(back_key, "dp", split_axis=1, concat_axis=1, tiled=True),
        lax.all_to_all(back_value, "dp", split_axis=1, concat_axis=1, tiled=True),
    )
    home_query, home_key, home_value = (
        lax.all_to_all(
            collect(entry_query, destination, slot_ids),
            "dp",
            split_axis=0,
            concat_axis=0,
            tiled=True,
        ),
        lax.all_to_all(
            collect(entry_key, destination, slot_ids), "dp", split_axis=0, concat_axis=0, tiled=True
        ),
        lax.all_to_all(
            collect(entry_value, destination, slot_ids),
            "dp",
            split_axis=0,
            concat_axis=0,
            tiled=True,
        ),
    )
    grad_query = home_query.reshape(buffer_rows, head_width)
    grad_key = home_key.reshape(buffer_rows, head_width)
    grad_value = home_value.reshape(buffer_rows, head_width)
    hosted_half, grad_query, grad_key, grad_value = (
        lax.all_to_all(hosted_out, "seq", split_axis=0, concat_axis=1, tiled=True),
        lax.all_to_all(grad_query, "seq", split_axis=0, concat_axis=1, tiled=True),
        lax.all_to_all(grad_key, "seq", split_axis=0, concat_axis=1, tiled=True),
        lax.all_to_all(grad_value, "seq", split_axis=0, concat_axis=1, tiled=True),
    )
    return (hosted_half, grad_query, grad_key, grad_value)


def solution(mesh):
    placed = (
        P(("groups", "dp", "seq"), None),
        P(("groups", "dp", "seq"), None),
        P(("groups", "dp", "seq"), None),
        P(("groups", "dp", "seq"), None),
        P("groups", None, None),
        P("groups", None),
    )
    return jax.shard_map(
        local,
        mesh=mesh,
        in_specs=placed,
        out_specs=(
            P(("groups", "dp", "seq"), None),
            P(("groups", "dp", "seq"), None),
            P(("groups", "dp", "seq"), None),
            P(("groups", "dp", "seq"), None),
        ),
        check_vma=False,
    )
```

profile of v0, /device:TPU:0, one launch (start us, length us, event | category | flops | bytes accessed | tf_op | source)
XLA Modules:
  0.0 398.6 jit_solution(6762479599671775281)
XLA Ops:
  0.6 1.9 copy.166
  2.5 3.6 all-to-all-start
  7.8 4.1 %all_to_all.200 = bf16[192,2,640]{2,0,1:T(8,128)(2,1)S(1)} all-to-all(bf16[192,2,640]{2,0,1:T(8,128)(2,1)S(1)} %bitcast.217), channel_id=1, replica_groups=mesh['groups'=2,'dp'=8,'seq'=2] {'seq'}, dimensions={1} | all-to-all | bytes 983040 | tf_op jit(solution)/shard_map/all_to_all | solution.py:103
  11.9 4.9 %all_to_all.201 = bf16[192,2,640]{2,0,1:T(8,128)(2,1)} all-to-all(bf16[192,2,640]{2,0,1:T(8,128)(2,1)S(1)} %bitcast.216), channel_id=1, replica_groups=mesh['groups'=2,'dp'=8,'seq'=2] {'seq'}, dimensions={1} | all-to-all | bytes 983040 | tf_op jit(solution)/shard_map/all_to_all | solution.py:104
  16.8 5.0 %all_to_all.202 = bf16[256,2,640]{0,2,1:T(8,128)(2,1)} all-to-all(bf16[256,2,640]{0,2,1:T(8,128)(2,1)S(1)} %bitcast.208), channel_id=1, replica_groups=mesh['groups'=2,'dp'=8,'seq'=2] {'seq'}, dimensions={1} | all-to-all | bytes 1310720 | tf_op jit(solution)/shard_map/all_to_all | solution.py:105
  21.8 21.1 %all_to_all.203 = bf16[8,48,640]{2,1,0:T(8,128)(2,1)S(1)} all-to-all(bf16[8,48,640]{2,1,0:T(8,128)(2,1)S(1)} %bitcast.211), channel_id=1, replica_groups=mesh['groups'=2,'dp'=8,'seq'=2] {'dp'}, dimensions={0} | all-to-all | bytes 983040 | tf_op jit(solution)/shard_map/all_to_all | solution.py:151
  42.9 16.9 %all_to_all.204 = bf16[8,48,640]{2,1,0:T(8,128)(2,1)S(1)} all-to-all(bf16[8,48,640]{2,1,0:T(8,128)(2,1)S(1)} %bitcast.218), channel_id=1, replica_groups=mesh['groups'=2,'dp'=8,'seq'=2] {'dp'}, dimensions={0} | all-to-all | bytes 983040 | tf_op jit(solution)/shard_map/all_to_all | solution.py:154
  59.8 3.7 all-to-all-start.7
  65.6 11.3 %all-to-all-done.7 = bf16[8,48,640]{2,1,0:T(8,128)(2,1)S(1)} async-done(((bf16[8,48,640]{2,1,0:T(8,128)(2,1)}), bf16[8,48,640]{2,1,0:T(8,128)(2,1)S(1)}, u32[]{:S(2)}, u32[]{:S(2)}) %all-to-all-start.7) | async-done | bytes 491552 | tf_op jit(solution)/shard_map/all_to_all | solution.py:157
  77.0 3.6 all-to-all-start.2
  82.4 22.5 %all-to-all-done.2 = bf16[2,8,48,640]{3,2,0,1:T(8,128)(2,1)S(1)} async-done(((bf16[2,8,48,640]{3,2,0,1:T(8,128)(2,1)}), bf16[2,8,48,640]{3,2,0,1:T(8,128)(2,1)S(1)}, u32[]{:S(2)}, u32[]{:S(2)}) %all-to-all-start.2) | async-done | bytes 983072 | tf_op jit(solution)/shard_map/all_to_all | solution.py:162
  104.9 4.2 %all-to-all-start.5 = ((bf16[2,8,48,640]{3,2,0,1:T(8,128)(2,1)}), bf16[2,8,48,640]{3,2,0,1:T(8,128)(2,1)}, u32[]{:S(2)}, u32[]{:S(2)}) async-start(bf16[2,8,48,640]{3,2,0,1:T(8,128)(2,1)} %copy.122), calls=%async_computation.5 | async-start | bytes 1966080 | tf_op jit(solution)/shard_map/all_to_all | solution.py:163
  110.9 22.2 %all-to-all-done.5 = bf16[2,8,48,640]{3,2,0,1:T(8,128)(2,1)} async-done(((bf16[2,8,48,640]{3,2,0,1:T(8,128)(2,1)}), bf16[2,8,48,640]{3,2,0,1:T(8,128)(2,1)}, u32[]{:S(2)}, u32[]{:S(2)}) %all-to-all-start.5) | async-done | bytes 983072 | tf_op jit(solution)/shard_map/all_to_all | solution.py:163
  133.1 3.6 all-to-all-start.8
  139.5 2.0 gather_fusion.1
  144.1 2.0 gather_fusion.3
  146.4 14.7 %all-to-all-done.8 = bf16[2,8,48,640]{3,2,0,1:T(8,128)(2,1)S(1)} async-done(((bf16[2,8,48,640]{3,2,0,1:T(8,128)(2,1)}), bf16[2,8,48,640]{3,2,0,1:T(8,128)(2,1)S(1)}, u32[]{:S(2)}, u32[]{:S(2)}) %all-to-all-start.8) | async-done | bytes 983072 | tf_op jit(solution)/shard_map/all_to_all | solution.py:164
  161.2 2.0 gather_fusion.5
  164.8 72.1 %while.30 = (s32[]{:T(128)}, bf16[8,512,80]{1,2,0:T(8,128)(2,1)S(1)}, bf16[8,512,80]{1,2,0:T(8,128)(2,1)S(1)}, bf16[8,512,80]{1,2,0:T(8,128)(2,1)}, bf16[8,512,8...) while((s32[]{:T(128)}, ...), condition=%wide.region_8.9_spmd.clone, body=%wide.region_4.8_spmd.clone.sunk | while | flops 257753088 | bytes 8088201 | solution.py:72
  166.4 1.8 fusion.82
  175.4 1.9 fusion.82
  184.5 1.9 fusion.82
  193.5 1.8 fusion.82
  202.5 1.9 fusion.82
  211.5 1.8 fusion.82
  220.6 1.8 fusion.82
  229.6 1.8 fusion.82
  237.3 2.8 gather_fusion.6
  242.2 5.0 %all_to_all.205 = bf16[2,256,640]{2,1,0:T(8,128)(2,1)} all-to-all(bf16[2,256,640]{2,1,0:T(8,128)(2,1)S(1)} %copy.134), channel_id=1, replica_groups=mesh['groups'=2,'dp'=8,'seq'=2] {'seq'}, dimensions={0} | all-to-all | bytes 1310720 | tf_op jit(solution)/shard_map/all_to_all | solution.py:219
  247.2 3.9 all-to-all-start.11
  251.5 2.8 gather_fusion.8
  255.3 20.5 %all-to-all-done.11 = bf16[2,8,48,640]{3,2,0,1:T(8,128)(2,1)S(1)} async-done(((bf16[2,8,48,640]{3,2,0,1:T(8,128)(2,1)}), bf16[2,8,48,640]{3,2,0,1:T(8,128)(2,1)S(1)}, u32[]{:S(2)}, u32[]{:S(2)}) %all-to-all-start.11) | async-done | bytes 983072 | tf_op jit(solution)/shard_map/all_to_all | solution.py:192
  275.8 3.6 all-to-all-start.14
  279.8 3.4 gather_fusion.10
  283.2 2.2 copy.144
  285.4 18.5 %all-to-all-done.14 = bf16[2,8,48,640]{3,2,0,1:T(8,128)(2,1)S(1)} async-done(((bf16[2,8,48,640]{3,2,0,1:T(8,128)(2,1)}), bf16[2,8,48,640]{3,2,0,1:T(8,128)(2,1)S(1)}, u32[]{:S(2)}, u32[]{:S(2)}) %all-to-all-start.14) | async-done | bytes 983072 | tf_op jit(solution)/shard_map/all_to_all | solution.py:193
  303.9 4.2 %all-to-all-start.17 = ((bf16[2,8,48,640]{3,2,0,1:T(8,128)(2,1)}), bf16[2,8,48,640]{3,2,0,1:T(8,128)(2,1)}, u32[]{:S(2)}, u32[]{:S(2)}) async-start(bf16[2,8,48,640]{3,2,0,1:T(8,128)(2,1)} %copy.144), calls=%async_computation.17 | async-start | bytes 1966080 | tf_op jit(solution)/shard_map/all_to_all | solution.py:194
  309.9 22.5 %all-to-all-done.17 = bf16[2,8,48,640]{3,2,0,1:T(8,128)(2,1)} async-done(((bf16[2,8,48,640]{3,2,0,1:T(8,128)(2,1)}), bf16[2,8,48,640]{3,2,0,1:T(8,128)(2,1)}, u32[]{:S(2)}, u32[]{:S(2)}) %all-to-all-start.17) | async-done | bytes 983072 | tf_op jit(solution)/shard_map/all_to_all | solution.py:194
  332.5 3.5 all-to-all-start.12
  337.5 12.3 %all-to-all-done.12 = bf16[8,48,640]{2,1,0:T(8,128)(2,1)S(1)} async-done(((bf16[8,48,640]{2,1,0:T(8,128)(2,1)}), bf16[8,48,640]{2,1,0:T(8,128)(2,1)S(1)}, u32[]{:S(2)}, u32[]{:S(2)}) %all-to-all-start.12) | async-done | bytes 491552 | tf_op jit(solution)/shard_map/all_to_all | solution.py:197
  349.8 4.1 %all_to_all.206 = bf16[2,192,640]{2,1,0:T(8,128)(2,1)S(1)} all-to-all(bf16[2,192,640]{2,1,0:T(8,128)(2,1)S(1)} %bitcast.214), channel_id=1, replica_groups=mesh['groups'=2,'dp'=8,'seq'=2] {'seq'}, dimensions={0} | all-to-all | bytes 983040 | tf_op jit(solution)/shard_map/all_to_all | solution.py:220
  353.9 3.6 all-to-all-start.15
  357.5 1.9 gather_fusion.11
  360.3 11.4 %all-to-all-done.15 = bf16[8,48,640]{2,1,0:T(8,128)(2,1)S(1)} async-done(((bf16[8,48,640]{2,1,0:T(8,128)(2,1)}), bf16[8,48,640]{2,1,0:T(8,128)(2,1)S(1)}, u32[]{:S(2)}, u32[]{:S(2)}) %all-to-all-start.15) | async-done | bytes 491552 | tf_op jit(solution)/shard_map/all_to_all | solution.py:204
  371.7 4.1 %all_to_all.207 = bf16[2,192,640]{2,1,0:T(8,128)(2,1)S(1)} all-to-all(bf16[2,192,640]{2,1,0:T(8,128)(2,1)S(1)} %bitcast.213), channel_id=1, replica_groups=mesh['groups'=2,'dp'=8,'seq'=2] {'seq'}, dimensions={0} | all-to-all | bytes 983040 | tf_op jit(solution)/shard_map/all_to_all | solution.py:221
  375.8 3.7 all-to-all-start.18
  382.5 11.2 %all-to-all-done.18 = bf16[8,48,640]{2,1,0:T(8,128)(2,1)S(1)} async-done(((bf16[8,48,640]{2,1,0:T(8,128)(2,1)}), bf16[8,48,640]{2,1,0:T(8,128)(2,1)S(1)}, u32[]{:S(2)}, u32[]{:S(2)}) %all-to-all-start.18) | async-done | bytes 491552 | tf_op jit(solution)/shard_map/all_to_all | solution.py:207
  393.7 4.1 %all_to_all.208 = bf16[2,192,640]{2,1,0:T(8,128)(2,1)S(1)} all-to-all(bf16[2,192,640]{2,1,0:T(8,128)(2,1)S(1)} %bitcast.212), channel_id=1, replica_groups=mesh['groups'=2,'dp'=8,'seq'=2] {'seq'}, dimensions={0} | all-to-all | bytes 983040 | tf_op jit(solution)/shard_map/all_to_all | solution.py:222
  (170 shorter events, 83.6 us)
Async XLA Ops:
  2.5 3.6 copy-start.7
  2.5 5.3 %all-to-all-start = ((bf16[192,2,640]{2,0,1:T(8,128)(2,1)}), bf16[192,2,640]{2,0,1:T(8,128)(2,1)S(1)}, u32[]{:S(2)}, u32[]{:S(2)}) async-start(bf16[192,2,640]{2,0,1:T(8,128)(2,1)} %bitcast.160), calls=%async_computation | async-start | bytes 983040 | tf_op jit(solution)/shard_map/all_to_all | solution.py:102
  6.1 1.0 copy-start.8
  6.2 1.2 copy-start.2
  59.8 3.7 copy-start.9
  59.8 17.1 %all-to-all-start.7 = ((bf16[8,48,640]{2,1,0:T(8,128)(2,1)}), bf16[8,48,640]{2,1,0:T(8,128)(2,1)S(1)}, u32[]{:S(2)}, u32[]{:S(2)}) async-start(bf16[8,48,640]{2,1,0:T(8,128)(2,1)} %bitcast.18), calls=%async_computation.7 | async-start | bytes 983040 | tf_op jit(solution)/shard_map/all_to_all | solution.py:157
  77.0 27.9 %all-to-all-start.2 = ((bf16[2,8,48,640]{3,2,0,1:T(8,128)(2,1)}), bf16[2,8,48,640]{3,2,0,1:T(8,128)(2,1)S(1)}, u32[]{:S(2)}, u32[]{:S(2)}) async-start(bf16[2,8,48,640]{3,2,0,1:T(8,128)(2,1)} %copy.118), calls=%async_computation.2 | async-start | bytes 1966080 | tf_op jit(solution)/shard_map/all_to_all | solution.py:162
  104.9 28.3 %all-to-all-start.5 = ((bf16[2,8,48,640]{3,2,0,1:T(8,128)(2,1)}), bf16[2,8,48,640]{3,2,0,1:T(8,128)(2,1)}, u32[]{:S(2)}, u32[]{:S(2)}) async-start(bf16[2,8,48,640]{3,2,0,1:T(8,128)(2,1)} %copy.122), calls=%async_computation.5 | async-start | bytes 1966080 | tf_op jit(solution)/shard_map/all_to_all | solution.py:163
  110.9 25.8 %copy-start.10 = (s32[8,2,2]{0,2,1:T(2,128)S(1)}, s32[8,2,2]{0,2,1:T(2,128)}, u32[]{:S(2)}) copy-start(s32[8,2,2]{0,2,1:T(2,128)} %param.12) | copy-start | bytes 388
  110.9 26.4 %copy-start = (bf16[256,2,640]{0,2,1:T(8,128)(2,1)S(1)}, bf16[256,2,640]{0,2,1:T(8,128)(2,1)}, u32[]{:S(2)}) copy-start(bf16[256,2,640]{0,2,1:T(8,128)(2,1)} %all_to_all.202) | copy-start | bytes 1966084
  133.1 27.9 %all-to-all-start.8 = ((bf16[2,8,48,640]{3,2,0,1:T(8,128)(2,1)}), bf16[2,8,48,640]{3,2,0,1:T(8,128)(2,1)S(1)}, u32[]{:S(2)}, u32[]{:S(2)}) async-start(bf16[2,8,48,640]{3,2,0,1:T(8,128)(2,1)} %copy.126), calls=%async_computation.8 | async-start | bytes 1966080 | tf_op jit(solution)/shard_map/all_to_all | solution.py:164
  163.3 1.1 copy-start.3
  163.3 1.5 copy-start.4
  247.2 3.9 copy-start.5
  247.2 28.6 %all-to-all-start.11 = ((bf16[2,8,48,640]{3,2,0,1:T(8,128)(2,1)}), bf16[2,8,48,640]{3,2,0,1:T(8,128)(2,1)S(1)}, u32[]{:S(2)}, u32[]{:S(2)}) async-start(bf16[2,8,48,640]{3,2,0,1:T(8,128)(2,1)} %copy.137), calls=%async_computation.11 | async-start | bytes 1966080 | tf_op jit(solution)/shard_map/all_to_all | solution.py:192
  255.3 24.1 %copy-start.6 = (bf16[8,512,80]{1,2,0:T(8,128)(2,1)S(1)}, bf16[8,512,80]{1,2,0:T(8,128)(2,1)}, u32[]{:S(2)}) copy-start(bf16[8,512,80]{1,2,0:T(8,128)(2,1)} %get-tuple-element.97) | copy-start | bytes 1966084
  275.8 28.2 %all-to-all-start.14 = ((bf16[2,8,48,640]{3,2,0,1:T(8,128)(2,1)}), bf16[2,8,48,640]{3,2,0,1:T(8,128)(2,1)S(1)}, u32[]{:S(2)}, u32[]{:S(2)}) async-start(bf16[2,8,48,640]{3,2,0,1:T(8,128)(2,1)} %copy.141), calls=%async_computation.14 | async-start | bytes 1966080 | tf_op jit(solution)/shard_map/all_to_all | solution.py:193
  303.9 28.5 %all-to-all-start.17 = ((bf16[2,8,48,640]{3,2,0,1:T(8,128)(2,1)}), bf16[2,8,48,640]{3,2,0,1:T(8,128)(2,1)}, u32[]{:S(2)}, u32[]{:S(2)}) async-start(bf16[2,8,48,640]{3,2,0,1:T(8,128)(2,1)} %copy.144), calls=%async_computation.17 | async-start | bytes 1966080 | tf_op jit(solution)/shard_map/all_to_all | solution.py:194
  332.5 17.3 %all-to-all-start.12 = ((bf16[8,48,640]{2,1,0:T(8,128)(2,1)}), bf16[8,48,640]{2,1,0:T(8,128)(2,1)S(1)}, u32[]{:S(2)}, u32[]{:S(2)}) async-start(bf16[8,48,640]{2,1,0:T(8,128)(2,1)} %fusion.42), calls=%async_computation.12 | async-start | bytes 983040 | tf_op jit(solution)/shard_map/all_to_all | solution.py:197
  353.9 17.8 %all-to-all-start.15 = ((bf16[8,48,640]{2,1,0:T(8,128)(2,1)}), bf16[8,48,640]{2,1,0:T(8,128)(2,1)S(1)}, u32[]{:S(2)}, u32[]{:S(2)}) async-start(bf16[8,48,640]{2,1,0:T(8,128)(2,1)} %fusion.41), calls=%async_computation.15 | async-start | bytes 983040 | tf_op jit(solution)/shard_map/all_to_all | solution.py:204
  375.8 3.8 copy-start.1
  375.8 17.9 %all-to-all-start.18 = ((bf16[8,48,640]{2,1,0:T(8,128)(2,1)}), bf16[8,48,640]{2,1,0:T(8,128)(2,1)S(1)}, u32[]{:S(2)}, u32[]{:S(2)}) async-start(bf16[8,48,640]{2,1,0:T(8,128)(2,1)} %fusion.40), calls=%async_computation.18 | async-start | bytes 983040 | tf_op jit(solution)/shard_map/all_to_all | solution.py:207
where the time goes:
time: 402 us; the launch traced here: 399 us
  waiting for transfers between devices  167 us (42%)
  blocking collectives  69.3 us (17%)
  matrix products  62.1 us (15%)
  local copies, waits for them, and re-layouts  44.2 us (11%)
  starting transfers between devices  41.4 us (10%)
  other arithmetic  12.8 us (3%)
    all_to_all x1, waiting for transfers between devices, local(): lax.all_to_all(back_value, 'dp', split_axis=1, concat_axis=1, tiled=True)  22.5 us
    all_to_all x1, waiting for transfers between devices, local(): lax.all_to_all(spread_query[source_lists], 'dp', split_axis=1, concat_axi...  22.5 us
    all_to_all x1, waiting for transfers between devices, local(): lax.all_to_all(spread_key[source_lists], 'dp', split_axis=1, concat_axis=...  22.2 us
    all_to_all x1, blocking collectives, local(): lax.all_to_all(query_heads.reshape(spread_shape), 'dp', split_axis=0, con...  21.1 us
    all_to_all x1, waiting for transfers between devices, local(): lax.all_to_all(back_query, 'dp', split_axis=1, concat_axis=1, tiled=True)  20.5 us
    all_to_all x1, waiting for transfers between devices, local(): lax.all_to_all(back_key, 'dp', split_axis=1, concat_axis=1, tiled=True)  18.5 us
    gather x9, local copies, waits for them, and re-layouts, take_rows(): return padded[row_index]  17.5 us
    all_to_all x1, blocking collectives, local(): lax.all_to_all(key_heads.reshape(spread_shape), 'dp', split_axis=0, conca...  16.9 us
  transfers between devices with their start and end apart: 11, of which 11 were waited for; matrix products, arithmetic and copies ran while one was open for 9% of the time, Pallas kernels for 0%

commit v1 on v0

v1 whole, which is shorter than its diff:
```python
import functools

import jax
import jax.numpy as jnp
from jax import lax
from jax.experimental import pallas as pl
from jax.experimental.pallas import tpu as pltpu
from jax.sharding import PartitionSpec as P

HEAD_DIM = 80
VMEM_BYTES = 48 * 1024 * 1024


def image_place(grid_ref, rank, slot):
    start = jnp.int32(0)
    length = jnp.int32(0)
    for image in range(grid_ref.shape[1]):
        patches = grid_ref[rank, image, 0] * grid_ref[rank, image, 1]
        start = start + jnp.where(image < slot, patches, 0)
        length = jnp.where(image == slot, patches, length)
    return start, length


def row_pick(slot_rows, part_rows, first, start, length, transposed=False):
    shape = (part_rows, slot_rows) if transposed else (slot_rows, part_rows)
    offset = lax.broadcasted_iota(jnp.int32, shape, 1 if transposed else 0)
    row = lax.broadcasted_iota(jnp.int32, shape, 0 if transposed else 1) + first
    return jnp.where((row == start + offset) & (offset < length), 1.0, 0.0).astype(jnp.bfloat16)


def dot(a, b, a_dim, b_dim):
    return lax.dot_general(
        a, b, (((a_dim,), (b_dim,)), ((), ())), preferred_element_type=jnp.float32
    )


def forward_kernel(
    grid_ref, q_own, q_far, k_own, k_far, v_own, v_far, q_img, k_img, v_img, out_ref, lse_ref
):
    rank = lax.axis_index("dp")
    slot = lax.axis_index("seq")
    start, length = image_place(grid_ref, rank, slot)
    slot_rows, width = out_ref.shape
    part_rows = q_own.shape[0]
    heads = width // HEAD_DIM
    inv_root = HEAD_DIM**-0.5
    pick_own = row_pick(slot_rows, part_rows, slot * part_rows, start, length)
    pick_far = row_pick(slot_rows, part_rows, (1 - slot) * part_rows, start, length)
    for own, far, image in ((q_own, q_far, q_img), (k_own, k_far, k_img), (v_own, v_far, v_img)):
        image[...] = (dot(pick_own, own[...], 1, 0) + dot(pick_far, far[...], 1, 0)).astype(
            image.dtype
        )
    key_ids = lax.broadcasted_iota(jnp.int32, (1, slot_rows), 1)
    key_bias = jnp.where(key_ids < length, 0.0, -1e30)
    row_ids = lax.broadcasted_iota(jnp.int32, (slot_rows, 1), 0)
    live = row_ids < length
    lane = lax.broadcasted_iota(jnp.int32, lse_ref.shape, 1)
    lse_all = jnp.zeros(lse_ref.shape, jnp.float32)
    for head in range(heads):
        cols = slice(head * HEAD_DIM, (head + 1) * HEAD_DIM)
        scores = dot(q_img[:, cols], k_img[:, cols], 1, 1) * inv_root + key_bias
        row_max = jnp.max(scores, axis=1, keepdims=True)
        weights = jnp.exp(scores - row_max)
        total = jnp.sum(weights, axis=1, keepdims=True)
        probs = (weights * (1.0 / total)).astype(jnp.bfloat16)
        attended = dot(probs, v_img[:, cols], 1, 0)
        out_ref[:, cols] = jnp.where(live, attended, 0.0).astype(out_ref.dtype)
        lse_all = jnp.where(lane == head, row_max + jnp.log(total), lse_all)
    lse_ref[...] = lse_all


def backward_kernel(
    grid_ref, q_img, k_img, v_img, out_ref, lse_ref, g_ref, *outs_and_scratch
):
    own_refs = outs_and_scratch[:3]
    far_refs = outs_and_scratch[3:6]
    g_img, dq_img, dk_img, dv_img = outs_and_scratch[6:]
    rank = lax.axis_index("dp")
    slot = lax.axis_index("seq")
    start, length = image_place(grid_ref, rank, slot)
    slot_rows, width = out_ref.shape
    part_rows = own_refs[0].shape[0]
    heads = width // HEAD_DIM
    inv_root = HEAD_DIM**-0.5
    row_ids = lax.broadcasted_iota(jnp.int32, (slot_rows, 1), 0)
    live = row_ids < length
    g_rows = g_ref[...].reshape(slot_rows, width)
    g_img[...] = jnp.where(live, g_rows, jnp.zeros_like(g_rows))
    key_ids = lax.broadcasted_iota(jnp.int32, (1, slot_rows), 1)
    key_bias = jnp.where(key_ids < length, 0.0, -1e30)
    for head in range(heads):
        cols = slice(head * HEAD_DIM, (head + 1) * HEAD_DIM)
        q, k, v, g = q_img[:, cols], k_img[:, cols], v_img[:, cols], g_img[:, cols]
        scores = dot(q, k, 1, 1) * inv_root + key_bias
        probs = jnp.exp(scores - lse_ref[:, head : head + 1])
        probs_bf = probs.astype(jnp.bfloat16)
        grad_probs = dot(g, v, 1, 1)
        row_dot = jnp.sum(
            g.astype(jnp.float32) * out_ref[:, cols].astype(jnp.float32), axis=1, keepdims=True
        )
        grad_scores = (probs * (grad_probs - row_dot) * inv_root).astype(jnp.bfloat16)
        dq_img[:, cols] = dot(grad_scores, k, 1, 0).astype(dq_img.dtype)
        dk_img[:, cols] = dot(grad_scores, q, 0, 0).astype(dk_img.dtype)
        dv_img[:, cols] = dot(probs_bf, g, 0, 0).astype(dv_img.dtype)
    put_own = row_pick(slot_rows, part_rows, slot * part_rows, start, length, True)
    put_far = row_pick(slot_rows, part_rows, (1 - slot) * part_rows, start, length, True)
    for image, own, far in zip((dq_img, dk_img, dv_img), own_refs, far_refs):
        own[...] = dot(put_own, image[...], 1, 0).astype(own.dtype)
        far[...] = dot(put_far, image[...], 1, 0).astype(far.dtype)


def middle_kernel(dest_ref, g_ref, o_ref, out_ref, g_sem, o_sem):
    slot = lax.axis_index("seq")
    ranks, block = g_ref.shape[:2]
    copies = []
    for rank in range(ranks):
        copies.append(
            pltpu.make_async_copy(
                g_ref.at[dest_ref[rank, slot]], out_ref.at[rank, pl.ds(0, block)], g_sem.at[rank]
            )
        )
        copies.append(
            pltpu.make_async_copy(
                o_ref.at[pl.ds(rank * block, block)],
                out_ref.at[rank, pl.ds(block, block)],
                o_sem.at[rank],
            )
        )
    for copy in copies:
        copy.start()
    for copy in copies:
        copy.wait()


def last_kernel(dest_ref, in_ref, out_ref, sem):
    slot = lax.axis_index("seq")
    ranks, block = out_ref.shape[:2]
    copies = []
    for rank in range(ranks):
        copies.append(
            pltpu.make_async_copy(
                in_ref.at[rank, pl.ds(block, block)], out_ref.at[dest_ref[rank, slot]], sem.at[rank]
            )
        )
    for copy in copies:
        copy.start()
    for copy in copies:
        copy.wait()


SMEM = pl.BlockSpec(memory_space=pltpu.SMEM)
VMEM = pl.BlockSpec(memory_space=pltpu.VMEM)
ANY = pl.BlockSpec(memory_space=pl.ANY)


def bf16(*shape):
    return jax.ShapeDtypeStruct(shape, jnp.bfloat16)


def local(query_rows, key_rows, value_rows, grad_hosted, image_grid, destination):
    ranks = lax.axis_size("dp")
    slot = lax.axis_index("seq")
    part_rows, width = query_rows.shape
    slot_rows = grad_hosted.shape[0]
    heads = width // HEAD_DIM
    block = slot_rows // ranks
    by_kernel = block % 16 == 0
    flops = 2 * slot_rows * slot_rows * width
    params = pltpu.CompilerParams(vmem_limit_bytes=VMEM_BYTES)

    def swap(x):
        return lax.ppermute(x, "seq", [(0, 1), (1, 0)])

    def spread(x):
        return lax.all_to_all(x, "dp", 0, 0, tiled=True)

    grad_spread = spread(grad_hosted.reshape(ranks, block, width))

    pairs = []
    for rows in (query_rows, key_rows, value_rows):
        pairs += [rows, swap(rows)]
    q_img, k_img, v_img, attended, lse = pl.pallas_call(
        forward_kernel,
        out_shape=[bf16(slot_rows, width)] * 4
        + [jax.ShapeDtypeStruct((slot_rows, 128), jnp.float32)],
        in_specs=[SMEM] + [VMEM] * 6,
        out_specs=[VMEM] * 5,
        compiler_params=params,
        cost_estimate=pl.CostEstimate(
            flops=5 * flops, bytes_accessed=6 * 2 * slot_rows * width, transcendentals=slot_rows * slot_rows * heads
        ),
        name="attend",
    )(image_grid, *pairs)

    if by_kernel:
        both = pl.pallas_call(
            middle_kernel,
            out_shape=bf16(ranks, 2 * block, width),
            in_specs=[SMEM, ANY, ANY],
            out_specs=ANY,
            scratch_shapes=[pltpu.SemaphoreType.DMA((ranks,)), pltpu.SemaphoreType.DMA((ranks,))],
            name="order_by_lister",
        )(destination, grad_spread, attended)
    else:
        dest = lax.dynamic_index_in_dim(destination, slot, 1, keepdims=False)
        both = jnp.concatenate(
            [grad_spread[dest], attended.reshape(ranks, block, width)], axis=1
        )
    both = spread(both)

    if by_kernel:
        host_order = pl.pallas_call(
            last_kernel,
            out_shape=bf16(ranks, block, width),
            in_specs=[SMEM, ANY],
            out_specs=ANY,
            scratch_shapes=[pltpu.SemaphoreType.DMA((ranks,))],
            name="order_by_host",
        )(destination, both)
        grad_slot = both
        grad_spec = pl.BlockSpec((ranks, block, width), lambda i: (0, 0, 0))
    else:
        rank_ids = jnp.arange(ranks, dtype=jnp.int32)
        source = jnp.sum(
            jnp.where(dest[None, :] == rank_ids[:, None], rank_ids[None, :], 0), axis=1
        )
        host_order = both[source, block:]
        grad_slot = both[:, :block].reshape(1, slot_rows, width)
        grad_spec = pl.BlockSpec((1, slot_rows, width), lambda i: (0, 0, 0))
    hosted_out = spread(host_order).reshape(slot_rows, width)

    def whole(*shape):
        return pl.BlockSpec(shape, lambda i: (0,) * len(shape))

    grads = pl.pallas_call(
        backward_kernel,
        grid=(1,),
        out_shape=[bf16(part_rows, width)] * 6,
        in_specs=[SMEM]
        + [whole(slot_rows, width)] * 4
        + [whole(slot_rows, 128), grad_spec],
        out_specs=[whole(part_rows, width)] * 6,
        scratch_shapes=[pltpu.VMEM((slot_rows, width), jnp.bfloat16)] * 4,
        compiler_params=params,
        cost_estimate=pl.CostEstimate(
            flops=9 * flops, bytes_accessed=11 * 2 * slot_rows * width, transcendentals=slot_rows * slot_rows * heads
        ),
        name="attend_back",
    )(image_grid, q_img, k_img, v_img, attended, lse, grad_slot)
    grad_query, grad_key, grad_value = (
        own + swap(far) for own, far in zip(grads[:3], grads[3:])
    )
    return hosted_out, grad_query, grad_key, grad_value


def solution(mesh):
    rows = P(("groups", "dp", "seq"), None)
    return jax.shard_map(
        local,
        mesh=mesh,
        in_specs=(rows, rows, rows, rows, P("groups", None, None), P("groups", None)),
        out_specs=(rows,) * 4,
        check_vma=False,
    )
```

time: 402 us -> 148 us (0.37)
  waiting for transfers between devices: 167 us -> 4.91 us
  Pallas kernels: 0 us -> 84.6 us
  matrix products: 62.1 us -> 0 us
  local copies, waits for them, and re-layouts: 44.2 us -> 5.18 us
  blocking collectives: 69.3 us -> 36.6 us
  starting transfers between devices: 41.4 us -> 12.4 us
  other arithmetic: 12.8 us -> 2.69 us
    all_to_all x11 -> x2, waiting for transfers between devices: 167 us -> 1.52 us  [spread(): return lax.all_to_all(x, 'dp', 0, 0, tiled=True)]
    pallas_call x0 -> x4, Pallas kernels: none -> 84.6 us  [the longest x1 41.7 us: local(): pl.pallas_call(middle_kernel, out_shape=bf16(ranks, 2 * block, width), in...]
    dot_general x48 -> x0, matrix products: 62.1 us -> none  [the longest x8 14.8 us: head_backward(): jnp.einsum('qk,qd->kd', probs_bf, grad_head, preferred_element_type=jnp.f...]
    all_to_all x9 -> x1, blocking collectives: 69.3 us -> 36.6 us  [spread(): return lax.all_to_all(x, 'dp', 0, 0, tiled=True)]
    all_to_all x11 -> x2, starting transfers between devices: 41.4 us -> 11.1 us  [spread(): return lax.all_to_all(x, 'dp', 0, 0, tiled=True)]
    gather x18 -> x0, local copies, waits for them, and re-layouts: 26.1 us -> none  [the longest x9 17.5 us: take_rows(): return padded[row_index]]
    reduce_sum x18 -> x0, other arithmetic: 9.41 us -> none  [the longest x8 7.51 us: head_backward(): jnp.sum(grad_head.astype(jnp.float32) * attended.astype(jnp.float32), axi...]
    all_to_all x13 -> x0, local copies, waits for them, and re-layouts: 7.87 us -> none  [the longest x1 1.85 us: local(): lax.all_to_all(query_rows, 'seq', split_axis=1, concat_axis=0, tiled=True)]
  transfers between devices with their start and end apart: 11 -> 8, of which waited for: 11 -> 6; matrix products, arithmetic and copies ran while one was open for 9% -> 2% of each run, Pallas kernels for 0% -> 14%
where the time goes in v1:
time: 148 us; the launch traced here: 147 us
  Pallas kernels  84.6 us (57%)
  blocking collectives  36.6 us (25%)
  starting transfers between devices  12.4 us (8%)
  local copies, waits for them, and re-layouts  5.18 us (4%)
  waiting for transfers between devices  4.91 us (3%)
  other arithmetic  2.69 us (2%)
    pallas_call x1, Pallas kernels, local(): pl.pallas_call(middle_kernel, out_shape=bf16(ranks, 2 * block, width), in...  41.7 us
    all_to_all x1, blocking collectives, spread(): return lax.all_to_all(x, 'dp', 0, 0, tiled=True)  36.6 us
    pallas_call x1, Pallas kernels, local(): pl.pallas_call(last_kernel, out_shape=bf16(ranks, block, width), in_specs...  21.9 us
    pallas_call x1, Pallas kernels, local(): pl.pallas_call(backward_kernel, grid=(1,), out_shape=[bf16(part_rows, wid...  11.8 us
    all_to_all x2, starting transfers between devices, spread(): return lax.all_to_all(x, 'dp', 0, 0, tiled=True)  11.1 us
    pallas_call x1, Pallas kernels, local(): pl.pallas_call(forward_kernel, out_shape=[bf16(slot_rows, width)] * 4 + [...  9.23 us
    unnamed x25, local copies, waits for them, and re-layouts  5.18 us
    ppermute x6, waiting for transfers between devices, swap(): return lax.ppermute(x, 'seq', [(0, 1), (1, 0)])  3.39 us
  transfers between devices with their start and end apart: 8, of which 6 were waited for; matrix products, arithmetic and copies ran while one was open for 2% of the time, Pallas kernels for 14%

profile of v1, /device:TPU:0, one launch (start us, length us, event | category | flops | bytes accessed | tf_op | source)
XLA Modules:
  0.0 147.1 jit_solution(15518254551247237457)
XLA Ops:
  0.6 0.0 copy-start.2
  0.6 0.0 copy-start.3
  0.7 0.0 copy-start.10
  0.7 0.0 copy-start.9
  0.7 7.4 %all-to-all-start = ((bf16[8,32,1280]{2,1,0:T(8,128)(2,1)}), bf16[8,32,1280]{2,1,0:T(8,128)(2,1)}, u32[]{:S(2)}, u32[]{:S(2)}) async-start(bf16[8,32,1280]{2,1,0:T(8,128)(2,1)} %bitcast.3), calls=%async_computation | async-start | bytes 1310720 | tf_op jit(solution)/shard_map/all_to_all | solution.py:175
  8.1 0.0 copy-done.2
  8.1 0.1 collective-permute-start
  8.2 0.0 copy-done.3
  8.2 0.5 collective-permute-start.1
  8.7 0.1 collective-permute-start.2
  8.7 0.0 copy-done.10
  8.7 0.7 copy.12.dest_ref
  9.4 0.0 copy-done.9
  9.4 0.1 copy.10.grid_ref
  9.5 0.5 collective-permute-done.q_far
  10.0 1.4 collective-permute-done.1.k_far
  11.4 0.2 collective-permute-done.2.v_far
  11.6 0.0 copy-start.4
  11.6 1.0 copy-done.4
  12.7 9.2 %attend.1 = (bf16[256,1280]{1,0:T(8,128)(2,1)S(1)}, bf16[256,1280]{1,0:T(8,128)(2,1)S(1)}, bf16[256,1280]{1,0:T(8,128)(2,1)S(1)}, bf16[256,1280]{1,0:T(8,128)(2,1)S(1)}, f32[256,128]{1,0:T(8,128)S(1)}) custom-call(s32[8,2,2]{2,1,0:T(2,128)S(1)} %copy.10.grid_ref, bf16[192,1280]{1,0:T(8,128)(2,1)S(1)} %copy-done.2, ...), custom_call_target="tpu_custom_call" | custom-call | flops 838860800 | bytes 3932160 | tf_op jit(solution)/shard_map/attend/pallas_call | solution.py:182
  21.9 0.0 copy-start
  21.9 0.8 copy-done
  22.7 0.0 copy-start.5
  22.7 0.8 copy-done.5
  23.6 0.0 copy-start.7
  23.6 0.8 copy-done.7
  24.4 1.1 all-to-all-done.g_ref
  25.5 41.7 %order_by_lister.1 = bf16[8,64,1280]{2,1,0:T(8,128)(2,1)} custom-call(s32[8,2]{1,0:T(8,128)} %copy.12.dest_ref, bf16[8,32,1280]{2,1,0:T(8,128)(2,1)} %all-to-all-done.g_ref, bf16[256,1280]{1,0:T(8,128)(2,1)} %copy-done), custom_call_target="tpu_custom_call" | custom-call | tf_op jit(solution)/shard_map/order_by_lister/pallas_call | solution.py:196
  67.2 36.6 %all_to_all.15.in_ref.g_ref = bf16[8,64,1280]{2,1,0:T(8,128)(2,1)} all-to-all(bf16[8,64,1280]{2,1,0:T(8,128)(2,1)} %order_by_lister.1), channel_id=1, replica_groups=mesh['groups'=2,'dp'=8,'seq'=2] {'dp'}, dimensions={0} | all-to-all | bytes 2621440 | tf_op jit(solution)/shard_map/all_to_all | solution.py:175
  103.8 0.0 copy-start.1
  103.8 0.0 copy-start.6
  103.8 21.9 %order_by_host.1 = bf16[8,32,1280]{2,1,0:T(8,128)(2,1)} custom-call(s32[8,2]{1,0:T(8,128)} %copy.12.dest_ref, bf16[8,64,1280]{2,1,0:T(8,128)(2,1)} %all_to_all.15.in_ref.g_ref), custom_call_target="tpu_custom_call" | custom-call | tf_op jit(solution)/shard_map/order_by_host/pallas_call | solution.py:212
  125.7 3.7 %all-to-all-start.2 = ((bf16[8,32,1280]{2,1,0:T(8,128)(2,1)}), bf16[8,32,1280]{2,1,0:T(8,128)(2,1)S(1)}, u32[]{:S(2)}, u32[]{:S(2)}) async-start(bf16[8,32,1280]{2,1,0:T(8,128)(2,1)} %order_by_host.1), calls=%async_computation.2 | async-start | bytes 1310720 | tf_op jit(solution)/shard_map/all_to_all | solution.py:175
  129.4 0.0 copy-done.1
  129.4 0.0 copy-done.6
  129.4 0.0 copy-done.8
  129.5 11.8 %attend_back.1 = (bf16[192,1280]{1,0:T(8,128)(2,1)S(1)}, bf16[192,1280]{1,0:T(8,128)(2,1)S(1)}, bf16[192,1280]{1,0:T(8,128)(2,1)S(1)}, bf16[192,1280]{1,0:T(8,12...) custom-call(s32[8,2,2]{2,1,0:T(2,128)S(1)} %copy.10.grid_ref, ...), custom_call_target="tpu_custom_call" | custom-call | flops 1509949440 | bytes 7208960 | tf_op jit(solution)/shard_map/attend_back/pallas_call | solution.py:235
  141.2 0.1 collective-permute-start.3
  141.3 0.5 collective-permute-start.4
  141.8 0.1 collective-permute-start.5
  141.9 1.3 collective-permute-done.3
  143.2 0.9 add.9
  144.1 0.0 collective-permute-done.4
  144.1 0.9 add.10
  144.9 0.0 collective-permute-done.5
  145.0 0.9 add.11
  145.8 0.5 all-to-all-done.2
  146.3 0.8 copy.15
  (1 shorter events, 0.0 us)
Async XLA Ops:
  0.6 7.4 %copy-start.2 = (bf16[192,1280]{1,0:T(8,128)(2,1)S(1)}, bf16[192,1280]{1,0:T(8,128)(2,1)}, u32[]{:S(2)}) copy-start(bf16[192,1280]{1,0:T(8,128)(2,1)} %q_own.1) | copy-start | bytes 1474564
  0.6 7.5 %copy-start.3 = (bf16[192,1280]{1,0:T(8,128)(2,1)S(1)}, bf16[192,1280]{1,0:T(8,128)(2,1)}, u32[]{:S(2)}) copy-start(bf16[192,1280]{1,0:T(8,128)(2,1)} %k_own.1) | copy-start | bytes 1474564
  0.7 8.1 %copy-start.10 = (s32[8,2]{0,1:T(2,128)S(1)}, s32[8,2]{0,1:T(2,128)}, u32[]{:S(2)}) copy-start(s32[8,2]{0,1:T(2,128)} %param.11) | copy-start | bytes 196
  0.7 8.8 %copy-start.9 = (s32[8,2,2]{0,2,1:T(2,128)S(1)}, s32[8,2,2]{0,2,1:T(2,128)}, u32[]{:S(2)}) copy-start(s32[8,2,2]{0,2,1:T(2,128)} %param.10) | copy-start | bytes 388
  0.7 24.8 %all-to-all-start = ((bf16[8,32,1280]{2,1,0:T(8,128)(2,1)}), bf16[8,32,1280]{2,1,0:T(8,128)(2,1)}, u32[]{:S(2)}, u32[]{:S(2)}) async-start(bf16[8,32,1280]{2,1,0:T(8,128)(2,1)} %bitcast.3), calls=%async_computation | async-start | bytes 1310720 | tf_op jit(solution)/shard_map/all_to_all | solution.py:175
  8.1 1.9 %collective-permute-start = (bf16[192,1280]{1,0:T(8,128)(2,1)S(1)}, bf16[192,1280]{1,0:T(8,128)(2,1)S(1)}, u32[]{:S(2)}, u32[]{:S(2)}) collective-permute-start(bf16[192,1280]{1,0:T(8,128)(2,1)S(1)} %copy-done.2), channel_id=1, source_target_pairs={{0,1},{1,0},{2,3},{3,2},{4,5},{5,4},{6,7},{7,6},{8,9},{9,8},{10,11... | collective-permute-start | bytes 1474568 | tf_op jit(solution)/shard_map/ppermute | solution.py:172
  8.2 3.2 %collective-permute-start.1 = (bf16[192,1280]{1,0:T(8,128)(2,1)S(1)}, bf16[192,1280]{1,0:T(8,128)(2,1)S(1)}, u32[]{:S(2)}, u32[]{:S(2)}) collective-permute-start(bf16[192,1280]{1,0:T(8,128)(2,1)S(1)} %copy-done.3), channel_id=1, source_target_pairs={{0,1},{1,0},{2,3},{3,2},{4,5},{5,4},{6,7},{7,6},{8,9},{9,8},{10,11... | collective-permute-start | bytes 1474568 | tf_op jit(solution)/shard_map/ppermute | solution.py:172
  8.7 3.0 %collective-permute-start.2 = (bf16[192,1280]{1,0:T(8,128)(2,1)}, bf16[192,1280]{1,0:T(8,128)(2,1)S(1)}, u32[]{:S(2)}, u32[]{:S(2)}) collective-permute-start(bf16[192,1280]{1,0:T(8,128)(2,1)} %v_own.1), channel_id=1, source_target_pairs={{0,1},{1,0},{2,3},{3,2},{4,5},{5,4},{6,7},{7,6},{8,9},{9,8},{10,11... | collective-permute-start | bytes 1474568 | tf_op jit(solution)/shard_map/ppermute | solution.py:172
  11.6 1.0 copy-start.4
  21.9 0.8 copy-start
  22.7 0.8 copy-start.5
  23.6 0.8 copy-start.7
  103.8 25.6 %copy-start.1 = (bf16[256,1280]{1,0:T(8,128)(2,1)S(1)}, bf16[256,1280]{1,0:T(8,128)(2,1)}, u32[]{:S(2)}) copy-start(bf16[256,1280]{1,0:T(8,128)(2,1)} %copy-done) | copy-start | bytes 1966084
  103.8 25.7 %copy-start.6 = (bf16[256,1280]{1,0:T(8,128)(2,1)S(1)}, bf16[256,1280]{1,0:T(8,128)(2,1)}, u32[]{:S(2)}) copy-start(bf16[256,1280]{1,0:T(8,128)(2,1)} %copy-done.5) | copy-start | bytes 1966084
  103.8 25.7 %copy-start.8 = (bf16[256,1280]{1,0:T(8,128)(2,1)S(1)}, bf16[256,1280]{1,0:T(8,128)(2,1)}, u32[]{:S(2)}) copy-start(bf16[256,1280]{1,0:T(8,128)(2,1)} %copy-done.7) | copy-start | bytes 1966084
  125.7 20.6 %all-to-all-start.2 = ((bf16[8,32,1280]{2,1,0:T(8,128)(2,1)}), bf16[8,32,1280]{2,1,0:T(8,128)(2,1)S(1)}, u32[]{:S(2)}, u32[]{:S(2)}) async-start(bf16[8,32,1280]{2,1,0:T(8,128)(2,1)} %order_by_host.1), calls=%async_computation.2 | async-start | bytes 1310720 | tf_op jit(solution)/shard_map/all_to_all | solution.py:175
  141.2 1.9 %collective-permute-start.3 = (bf16[192,1280]{1,0:T(8,128)(2,1)S(1)}, bf16[192,1280]{1,0:T(8,128)(2,1)S(1)}, u32[]{:S(2)}, u32[]{:S(2)}) collective-permute-start(bf16[192,1280]{1,0:T(8,128)(2,1)S(1)} %get-tuple-element.21), channel_id=1, source_target_pairs={{0,1},{1,0},{2,3},{3,2},{4,5},{5,4},{6,7},{7,6},{8,9},{9,8},{10,11... | collective-permute-start | bytes 1474568 | tf_op jit(solution)/shard_map/ppermute | solution.py:172
  141.3 2.7 %collective-permute-start.4 = (bf16[192,1280]{1,0:T(8,128)(2,1)S(1)}, bf16[192,1280]{1,0:T(8,128)(2,1)S(1)}, u32[]{:S(2)}, u32[]{:S(2)}) collective-permute-start(bf16[192,1280]{1,0:T(8,128)(2,1)S(1)} %get-tuple-element.23), channel_id=1, source_target_pairs={{0,1},{1,0},{2,3},{3,2},{4,5},{5,4},{6,7},{7,6},{8,9},{9,8},{10,11... | collective-permute-start | bytes 1474568 | tf_op jit(solution)/shard_map/ppermute | solution.py:172
  141.8 3.2 %collective-permute-start.5 = (bf16[192,1280]{1,0:T(8,128)(2,1)S(1)}, bf16[192,1280]{1,0:T(8,128)(2,1)S(1)}, u32[]{:S(2)}, u32[]{:S(2)}) collective-permute-start(bf16[192,1280]{1,0:T(8,128)(2,1)S(1)} %get-tuple-element.25), channel_id=1, source_target_pairs={{0,1},{1,0},{2,3},{3,2},{4,5},{5,4},{6,7},{7,6},{8,9},{9,8},{10,11... | collective-permute-start | bytes 1474568 | tf_op jit(solution)/shard_map/ppermute | solution.py:172

commit v2 on v1

--- a/solution.py
+++ b/solution.py
@@ -1,5 +1,3 @@
-import functools
-
 import jax
 import jax.numpy as jnp
 from jax import lax
@@ -109,48 +107,22 @@
         far[...] = dot(put_far, image[...], 1, 0).astype(far.dtype)
 
 
-def middle_kernel(dest_ref, g_ref, o_ref, out_ref, g_sem, o_sem):
+def middle_kernel(dest_ref, g_ref, o_ref, out_ref):
     slot = lax.axis_index("seq")
     ranks, block = g_ref.shape[:2]
-    copies = []
     for rank in range(ranks):
-        copies.append(
-            pltpu.make_async_copy(
-                g_ref.at[dest_ref[rank, slot]], out_ref.at[rank, pl.ds(0, block)], g_sem.at[rank]
-            )
-        )
-        copies.append(
-            pltpu.make_async_copy(
-                o_ref.at[pl.ds(rank * block, block)],
-                out_ref.at[rank, pl.ds(block, block)],
-                o_sem.at[rank],
-            )
-        )
-    for copy in copies:
-        copy.start()
-    for copy in copies:
-        copy.wait()
-
-
-def last_kernel(dest_ref, in_ref, out_ref, sem):
-    slot = lax.axis_index("seq")
-    ranks, block = out_ref.shape[:2]
-    copies = []
-    for rank in range(ranks):
-        copies.append(
-            pltpu.make_async_copy(
-                in_ref.at[rank, pl.ds(block, block)], out_ref.at[dest_ref[rank, slot]], sem.at[rank]
-            )
-        )
-    for copy in copies:
-        copy.start()
-    for copy in copies:
-        copy.wait()
+        out_ref[rank, :block] = g_ref[dest_ref[rank, slot]]
+        out_ref[rank, block:] = o_ref[rank * block : (rank + 1) * block]
+
+
+def last_kernel(dest_ref, in_ref, out_ref):
+    slot = lax.axis_index("seq")
+    for rank in range(out_ref.shape[0]):
+        out_ref[dest_ref[rank, slot]] = in_ref[rank]
 
 
 SMEM = pl.BlockSpec(memory_space=pltpu.SMEM)
 VMEM = pl.BlockSpec(memory_space=pltpu.VMEM)
-ANY = pl.BlockSpec(memory_space=pl.ANY)
 
 
 def bf16(*shape):
@@ -196,9 +168,8 @@
         both = pl.pallas_call(
             middle_kernel,
             out_shape=bf16(ranks, 2 * block, width),
-            in_specs=[SMEM, ANY, ANY],
-            out_specs=ANY,
-            scratch_shapes=[pltpu.SemaphoreType.DMA((ranks,)), pltpu.SemaphoreType.DMA((ranks,))],
+            in_specs=[SMEM, VMEM, VMEM],
+            out_specs=VMEM,
             name="order_by_lister",
         )(destination, grad_spread, attended)
     else:
@@ -211,10 +182,10 @@
     if by_kernel:
         host_order = pl.pallas_call(
             last_kernel,
+            grid=(1,),
             out_shape=bf16(ranks, block, width),
-            in_specs=[SMEM, ANY],
-            out_specs=ANY,
-            scratch_shapes=[pltpu.SemaphoreType.DMA((ranks,))],
+            in_specs=[SMEM, pl.BlockSpec((ranks, block, width), lambda i: (0, 1, 0))],
+            out_specs=pl.BlockSpec((ranks, block, width), lambda i: (0, 0, 0)),
             name="order_by_host",
         )(destination, both)
         grad_slot = both

time: 148 us -> 88.6 us (0.60)
  Pallas kernels: 84.6 us -> 25.6 us
    pallas_call x1, Pallas kernels: 41.7 us -> 2.43 us  [local(): pl.pallas_call(middle_kernel, out_shape=bf16(ranks, 2 * block, width), in...]
    pallas_call x1, Pallas kernels: 21.9 us -> 2.14 us  [local(): pl.pallas_call(last_kernel, grid=(1,), out_shape=bf16(ranks, block, width...]
  transfers between devices with their start and end apart: 8 -> 8, of which waited for: 6 -> 6; matrix products, arithmetic and copies ran while one was open for 2% -> 4% of each run, Pallas kernels for 14% -> 24%
where the time goes in v2:
time: 88.6 us; the launch traced here: 88.1 us
  blocking collectives  36.6 us (41%)
  Pallas kernels  25.6 us (29%)
  starting transfers between devices  12.4 us (14%)
  local copies, waits for them, and re-layouts  5.18 us (6%)
  waiting for transfers between devices  4.91 us (6%)
  other arithmetic  2.69 us (3%)
    all_to_all x1, blocking collectives, spread(): return lax.all_to_all(x, 'dp', 0, 0, tiled=True)  36.6 us
    pallas_call x1, Pallas kernels, local(): pl.pallas_call(backward_kernel, grid=(1,), out_shape=[bf16(part_rows, wid...  11.8 us
    all_to_all x2, starting transfers between devices, spread(): return lax.all_to_all(x, 'dp', 0, 0, tiled=True)  11.1 us
    pallas_call x1, Pallas kernels, local(): pl.pallas_call(forward_kernel, out_shape=[bf16(slot_rows, width)] * 4 + [...  9.23 us
    unnamed x25, local copies, waits for them, and re-layouts  5.18 us
    ppermute x6, waiting for transfers between devices, swap(): return lax.ppermute(x, 'seq', [(0, 1), (1, 0)])  3.39 us
    add x3, other arithmetic, local(): own + swap(far)  2.69 us
    pallas_call x1, Pallas kernels, local(): pl.pallas_call(middle_kernel, out_shape=bf16(ranks, 2 * block, width), in...  2.43 us
  transfers between devices with their start and end apart: 8, of which 6 were waited for; matrix products, arithmetic and copies ran while one was open for 4% of the time, Pallas kernels for 24%

profile of v2, /device:TPU:0, one launch (start us, length us, event | category | flops | bytes accessed | tf_op | source)
XLA Modules:
  0.0 88.1 jit_solution(17563174588379703263)
XLA Ops:
  0.6 0.0 copy-start.2
  0.6 0.0 copy-start.3
  0.7 0.0 copy-start.10
  0.7 0.0 copy-start.9
  0.7 7.4 %all-to-all-start = ((bf16[8,32,1280]{2,1,0:T(8,128)(2,1)}), bf16[8,32,1280]{2,1,0:T(8,128)(2,1)}, u32[]{:S(2)}, u32[]{:S(2)}) async-start(bf16[8,32,1280]{2,1,0:T(8,128)(2,1)} %bitcast.3), calls=%async_computation | async-start | bytes 1310720 | tf_op jit(solution)/shard_map/all_to_all | solution.py:147
  8.1 0.0 copy-done.2
  8.1 0.1 collective-permute-start
  8.2 0.0 copy-done.3
  8.2 0.5 collective-permute-start.1
  8.7 0.1 collective-permute-start.2
  8.7 0.0 copy-done.10
  8.7 0.7 copy.12.dest_ref
  9.4 0.0 copy-done.9
  9.4 0.1 copy.10.grid_ref
  9.5 0.5 collective-permute-done.q_far
  10.0 1.4 %collective-permute-done.1.k_far = bf16[192,1280]{1,0:T(8,128)(2,1)S(1)} collective-permute-done((bf16[192,1280]{1,0:T(8,128)(2,1)S(1)}, bf16[192,1280]{1,0:T(8,128)(2,1)S(1)}, u32[]{:S(2)}, u32[]{:S(2)}) %collective-permute-start.1) | collective-permute-done | bytes 491552 | tf_op jit(solution)/shard_map/ppermute | solution.py:144
  11.4 0.2 collective-permute-done.2.v_far
  11.6 0.0 copy-start.4
  11.6 1.0 %copy-done.4 = bf16[192,1280]{1,0:T(8,128)(2,1)S(1)} copy-done((bf16[192,1280]{1,0:T(8,128)(2,1)S(1)}, bf16[192,1280]{1,0:T(8,128)(2,1)}, u32[]{:S(2)}) %copy-start.4) | copy-done | bytes 491544
  12.7 9.2 %attend.1 = (bf16[256,1280]{1,0:T(8,128)(2,1)S(1)}, bf16[256,1280]{1,0:T(8,128)(2,1)S(1)}, bf16[256,1280]{1,0:T(8,128)(2,1)S(1)}, bf16[256,1280]{1,0:T(8,128)(2,1)S(1)}, f32[256,128]{1,0:T(8,128)S(1)}) custom-call(s32[8,2,2]{2,1,0:T(2,128)S(1)} %copy.10.grid_ref, bf16[192,1280]{1,0:T(8,128)(2,1)S(1)} %copy-done.2, ...), custom_call_target="tpu_custom_call" | custom-call | flops 838860800 | bytes 3932160 | tf_op jit(solution)/shard_map/attend/pallas_call | solution.py:154
  21.9 0.0 copy-start
  21.9 0.8 copy-done
  22.7 0.0 copy-start.5
  22.7 0.8 copy-done.5
  23.6 0.0 copy-start.7
  23.6 0.8 copy-done.7
  24.4 1.1 %all-to-all-done.g_ref = bf16[8,32,1280]{2,1,0:T(8,128)(2,1)} async-done(((bf16[8,32,1280]{2,1,0:T(8,128)(2,1)}), bf16[8,32,1280]{2,1,0:T(8,128)(2,1)}, u32[]{:S(2)}, u32[]{:S(2)}) %all-to-all-start) | async-done | bytes 655392 | tf_op jit(solution)/shard_map/all_to_all | solution.py:147
  25.5 2.4 %order_by_lister.1 = bf16[8,64,1280]{2,1,0:T(8,128)(2,1)} custom-call(s32[8,2]{1,0:T(8,128)} %copy.12.dest_ref, bf16[8,32,1280]{2,1,0:T(8,128)(2,1)} %all-to-all-done.g_ref, bf16[256,1280]{1,0:T(8,128)(2,1)} %copy-done), custom_call_target="tpu_custom_call" | custom-call | tf_op jit(solution)/shard_map/order_by_lister/pallas_call | solution.py:168
  27.9 36.6 %all_to_all.15.in_ref.g_ref = bf16[8,64,1280]{2,1,0:T(8,128)(2,1)} all-to-all(bf16[8,64,1280]{2,1,0:T(8,128)(2,1)} %order_by_lister.1), channel_id=1, replica_groups=mesh['groups'=2,'dp'=8,'seq'=2] {'dp'}, dimensions={0} | all-to-all | bytes 2621440 | tf_op jit(solution)/shard_map/all_to_all | solution.py:147
  64.5 0.0 copy-start.1
  64.5 0.0 copy-start.6
  64.5 2.1 %order_by_host.1 = bf16[8,32,1280]{2,1,0:T(8,128)(2,1)} custom-call(s32[8,2]{1,0:T(8,128)} %copy.12.dest_ref, bf16[8,64,1280]{2,1,0:T(8,128)(2,1)} %all_to_all.15.in_ref.g_ref), custom_call_target="tpu_custom_call" | custom-call | tf_op jit(solution)/shard_map/order_by_host/pallas_call | solution.py:183
  66.7 3.7 %all-to-all-start.2 = ((bf16[8,32,1280]{2,1,0:T(8,128)(2,1)}), bf16[8,32,1280]{2,1,0:T(8,128)(2,1)S(1)}, u32[]{:S(2)}, u32[]{:S(2)}) async-start(bf16[8,32,1280]{2,1,0:T(8,128)(2,1)} %order_by_host.1), calls=%async_computation.2 | async-start | bytes 1310720 | tf_op jit(solution)/shard_map/all_to_all | solution.py:147
  70.4 0.0 copy-done.1
  70.4 0.0 copy-done.6
  70.4 0.0 copy-done.8
  70.4 11.8 %attend_back.1 = (bf16[192,1280]{1,0:T(8,128)(2,1)S(1)}, bf16[192,1280]{1,0:T(8,128)(2,1)S(1)}, bf16[192,1280]{1,0:T(8,128)(2,1)S(1)}, bf16[192,1280]{1,0:T(8,12...) custom-call(s32[8,2,2]{2,1,0:T(2,128)S(1)} %copy.10.grid_ref, ...), custom_call_target="tpu_custom_call" | custom-call | flops 1509949440 | bytes 7208960 | tf_op jit(solution)/shard_map/attend_back/pallas_call | solution.py:206
  82.2 0.1 collective-permute-start.3
  82.3 0.5 collective-permute-start.4
  82.8 0.1 collective-permute-start.5
  82.8 1.3 %collective-permute-done.3 = bf16[192,1280]{1,0:T(8,128)(2,1)S(1)} collective-permute-done((bf16[192,1280]{1,0:T(8,128)(2,1)S(1)}, bf16[192,1280]{1,0:T(8,128)(2,1)S(1)}, u32[]{:S(2)}, u32[]{:S(2)}) %collective-permute-start.3) | collective-permute-done | bytes 491552 | tf_op jit(solution)/shard_map/ppermute | solution.py:144
  84.1 0.9 %add.9 = bf16[192,1280]{1,0:T(8,128)(2,1)} add(bf16[192,1280]{1,0:T(8,128)(2,1)S(1)} %get-tuple-element.20, bf16[192,1280]{1,0:T(8,128)(2,1)S(1)} %collective-permute-done.3) | non-fusion elementwise | flops 245760 | bytes 1474560 | tf_op jit(solution)/shard_map/add | solution.py:222
  85.0 0.0 collective-permute-done.4
  85.0 0.9 %add.10 = bf16[192,1280]{1,0:T(8,128)(2,1)} add(bf16[192,1280]{1,0:T(8,128)(2,1)S(1)} %get-tuple-element.22, bf16[192,1280]{1,0:T(8,128)(2,1)S(1)} %collective-permute-done.4) | non-fusion elementwise | flops 245760 | bytes 1474560 | tf_op jit(solution)/shard_map/add | solution.py:222
  85.9 0.0 collective-permute-done.5
  85.9 0.9 %add.11 = bf16[192,1280]{1,0:T(8,128)(2,1)} add(bf16[192,1280]{1,0:T(8,128)(2,1)S(1)} %get-tuple-element.24, bf16[192,1280]{1,0:T(8,128)(2,1)S(1)} %collective-permute-done.5) | non-fusion elementwise | flops 245760 | bytes 1474560 | tf_op jit(solution)/shard_map/add | solution.py:222
  86.8 0.5 all-to-all-done.2
  87.3 0.8 copy.15
  (1 shorter events, 0.0 us)
Async XLA Ops:
  0.6 7.4 %copy-start.2 = (bf16[192,1280]{1,0:T(8,128)(2,1)S(1)}, bf16[192,1280]{1,0:T(8,128)(2,1)}, u32[]{:S(2)}) copy-start(bf16[192,1280]{1,0:T(8,128)(2,1)} %q_own.1) | copy-start | bytes 1474564
  0.6 7.5 %copy-start.3 = (bf16[192,1280]{1,0:T(8,128)(2,1)S(1)}, bf16[192,1280]{1,0:T(8,128)(2,1)}, u32[]{:S(2)}) copy-start(bf16[192,1280]{1,0:T(8,128)(2,1)} %k_own.1) | copy-start | bytes 1474564
  0.7 8.1 %copy-start.10 = (s32[8,2]{0,1:T(2,128)S(1)}, s32[8,2]{0,1:T(2,128)}, u32[]{:S(2)}) copy-start(s32[8,2]{0,1:T(2,128)} %param.11) | copy-start | bytes 196
  0.7 8.8 %copy-start.9 = (s32[8,2,2]{0,2,1:T(2,128)S(1)}, s32[8,2,2]{0,2,1:T(2,128)}, u32[]{:S(2)}) copy-start(s32[8,2,2]{0,2,1:T(2,128)} %param.10) | copy-start | bytes 388
  0.7 24.8 %all-to-all-start = ((bf16[8,32,1280]{2,1,0:T(8,128)(2,1)}), bf16[8,32,1280]{2,1,0:T(8,128)(2,1)}, u32[]{:S(2)}, u32[]{:S(2)}) async-start(bf16[8,32,1280]{2,1,0:T(8,128)(2,1)} %bitcast.3), calls=%async_computation | async-start | bytes 1310720 | tf_op jit(solution)/shard_map/all_to_all | solution.py:147
  8.1 1.9 %collective-permute-start = (bf16[192,1280]{1,0:T(8,128)(2,1)S(1)}, bf16[192,1280]{1,0:T(8,128)(2,1)S(1)}, u32[]{:S(2)}, u32[]{:S(2)}) collective-permute-start(bf16[192,1280]{1,0:T(8,128)(2,1)S(1)} %copy-done.2), channel_id=1, source_target_pairs={{0,1},{1,0},{2,3},{3,2},{4,5},{5,4},{6,7},{7,6},{8,9},{9,8},{10,11... | collective-permute-start | bytes 1474568 | tf_op jit(solution)/shard_map/ppermute | solution.py:144
  8.2 3.2 %collective-permute-start.1 = (bf16[192,1280]{1,0:T(8,128)(2,1)S(1)}, bf16[192,1280]{1,0:T(8,128)(2,1)S(1)}, u32[]{:S(2)}, u32[]{:S(2)}) collective-permute-start(bf16[192,1280]{1,0:T(8,128)(2,1)S(1)} %copy-done.3), channel_id=1, source_target_pairs={{0,1},{1,0},{2,3},{3,2},{4,5},{5,4},{6,7},{7,6},{8,9},{9,8},{10,11... | collective-permute-start | bytes 1474568 | tf_op jit(solution)/shard_map/ppermute | solution.py:144
  8.7 3.0 %collective-permute-start.2 = (bf16[192,1280]{1,0:T(8,128)(2,1)}, bf16[192,1280]{1,0:T(8,128)(2,1)S(1)}, u32[]{:S(2)}, u32[]{:S(2)}) collective-permute-start(bf16[192,1280]{1,0:T(8,128)(2,1)} %v_own.1), channel_id=1, source_target_pairs={{0,1},{1,0},{2,3},{3,2},{4,5},{5,4},{6,7},{7,6},{8,9},{9,8},{10,11... | collective-permute-start | bytes 1474568 | tf_op jit(solution)/shard_map/ppermute | solution.py:144
  11.6 1.0 %copy-start.4 = (bf16[192,1280]{1,0:T(8,128)(2,1)S(1)}, bf16[192,1280]{1,0:T(8,128)(2,1)}, u32[]{:S(2)}) copy-start(bf16[192,1280]{1,0:T(8,128)(2,1)} %v_own.1) | copy-start | bytes 1474564
  21.9 0.8 copy-start
  22.7 0.8 copy-start.5
  23.6 0.8 copy-start.7
  64.5 5.9 %copy-start.1 = (bf16[256,1280]{1,0:T(8,128)(2,1)S(1)}, bf16[256,1280]{1,0:T(8,128)(2,1)}, u32[]{:S(2)}) copy-start(bf16[256,1280]{1,0:T(8,128)(2,1)} %copy-done) | copy-start | bytes 1966084
  64.5 5.9 %copy-start.6 = (bf16[256,1280]{1,0:T(8,128)(2,1)S(1)}, bf16[256,1280]{1,0:T(8,128)(2,1)}, u32[]{:S(2)}) copy-start(bf16[256,1280]{1,0:T(8,128)(2,1)} %copy-done.5) | copy-start | bytes 1966084
  64.5 5.9 %copy-start.8 = (bf16[256,1280]{1,0:T(8,128)(2,1)S(1)}, bf16[256,1280]{1,0:T(8,128)(2,1)}, u32[]{:S(2)}) copy-start(bf16[256,1280]{1,0:T(8,128)(2,1)} %copy-done.7) | copy-start | bytes 1966084
  66.7 20.6 %all-to-all-start.2 = ((bf16[8,32,1280]{2,1,0:T(8,128)(2,1)}), bf16[8,32,1280]{2,1,0:T(8,128)(2,1)S(1)}, u32[]{:S(2)}, u32[]{:S(2)}) async-start(bf16[8,32,1280]{2,1,0:T(8,128)(2,1)} %order_by_host.1), calls=%async_computation.2 | async-start | bytes 1310720 | tf_op jit(solution)/shard_map/all_to_all | solution.py:147
  82.2 1.9 %collective-permute-start.3 = (bf16[192,1280]{1,0:T(8,128)(2,1)S(1)}, bf16[192,1280]{1,0:T(8,128)(2,1)S(1)}, u32[]{:S(2)}, u32[]{:S(2)}) collective-permute-start(bf16[192,1280]{1,0:T(8,128)(2,1)S(1)} %get-tuple-element.21), channel_id=1, source_target_pairs={{0,1},{1,0},{2,3},{3,2},{4,5},{5,4},{6,7},{7,6},{8,9},{9,8},{10,11... | collective-permute-start | bytes 1474568 | tf_op jit(solution)/shard_map/ppermute | solution.py:144
  82.3 2.7 %collective-permute-start.4 = (bf16[192,1280]{1,0:T(8,128)(2,1)S(1)}, bf16[192,1280]{1,0:T(8,128)(2,1)S(1)}, u32[]{:S(2)}, u32[]{:S(2)}) collective-permute-start(bf16[192,1280]{1,0:T(8,128)(2,1)S(1)} %get-tuple-element.23), channel_id=1, source_target_pairs={{0,1},{1,0},{2,3},{3,2},{4,5},{5,4},{6,7},{7,6},{8,9},{9,8},{10,11... | collective-permute-start | bytes 1474568 | tf_op jit(solution)/shard_map/ppermute | solution.py:144
  82.8 3.2 %collective-permute-start.5 = (bf16[192,1280]{1,0:T(8,128)(2,1)S(1)}, bf16[192,1280]{1,0:T(8,128)(2,1)S(1)}, u32[]{:S(2)}, u32[]{:S(2)}) collective-permute-start(bf16[192,1280]{1,0:T(8,128)(2,1)S(1)} %get-tuple-element.25), channel_id=1, source_target_pairs={{0,1},{1,0},{2,3},{3,2},{4,5},{5,4},{6,7},{7,6},{8,9},{9,8},{10,11... | collective-permute-start | bytes 1474568 | tf_op jit(solution)/shard_map/ppermute | solution.py:144

commit v3 on v2

v3 whole, which is shorter than its diff:
```python
import jax
import jax.numpy as jnp
from jax import lax
from jax.experimental import pallas as pl
from jax.experimental.pallas import tpu as pltpu
from jax.sharding import PartitionSpec as P


HEAD_DIM = 80
STRIP = 256
STEPS = (0, 7, 1, 2, 5, 3, 4, 6)
LARGE = pltpu.CompilerParams(vmem_limit_bytes=12 * 1024 * 1024)
SMALL = pltpu.CompilerParams(vmem_limit_bytes=6 * 1024 * 1024)
SMEM = pl.BlockSpec(memory_space=pltpu.SMEM)
VMEM = pl.BlockSpec(memory_space=pltpu.VMEM)
HBM = pl.BlockSpec(memory_space=pltpu.HBM)


def dot(a, b, a_dim, b_dim):
    return lax.dot_general(
        a, b, (((a_dim,), (b_dim,)), ((), ())), preferred_element_type=jnp.float32
    )


def one_hot(condition):
    return jnp.where(condition, 1.0, 0.0).astype(jnp.bfloat16)


def iota(shape, dim):
    return lax.broadcasted_iota(jnp.int32, shape, dim)


def strips(width):
    return [slice(at, at + STRIP) for at in range(0, width, STRIP)]


def length_of(grid_ref, rank, image):
    return grid_ref[image, 0, rank] * grid_ref[image, 1, rank]


def image_place(grid_ref, rank, slot):
    start = jnp.int32(0)
    length = jnp.int32(0)
    for image in range(grid_ref.shape[0]):
        patches = length_of(grid_ref, rank, image)
        start = start + jnp.where(image < slot, patches, 0)
        length = jnp.where(image == slot, patches, length)
    return start, length


def row_pick(slot_rows, part_rows, first, start, length, transposed=False):
    shape = (part_rows, slot_rows) if transposed else (slot_rows, part_rows)
    offset = iota(shape, 1 if transposed else 0)
    row = iota(shape, 0 if transposed else 1) + first
    return one_hot((row == start + offset) & (offset < length))


def eye(n):
    return one_hot(iota((n, n), 0) == iota((n, n), 1))


def turn(identity, block):
    return dot(identity, block, 1, 1)


def block_of(to, rows):
    return pl.ds(pl.multiple_of(to * rows, rows), rows)


def to_lister_kernel(dest_ref, attended_ref, in_ref, *out_refs):
    rank = lax.axis_index("dp")
    slot = lax.axis_index("seq")
    rows = in_ref.shape[1]
    for step, out_ref in zip(STEPS, out_refs):
        out_ref[:rows] = in_ref[dest_ref[slot, rank ^ step]]
        out_ref[rows:] = attended_ref[block_of(rank ^ step, rows), :]


def to_host_kernel(dest_ref, *refs):
    rank = lax.axis_index("dp")
    slot = lax.axis_index("seq")
    in_refs, (out_ref, grad_ref) = refs[:-2], refs[-2:]
    rows = out_ref.shape[1]
    for step, in_ref in zip(STEPS, in_refs):
        out_ref[dest_ref[slot, rank ^ step]] = in_ref[rows:]
        grad_ref[block_of(rank ^ step, rows), :] = in_ref[:rows]


def store_kernel(in_ref, hbm_ref, sems):
    rows = in_ref.shape[1]
    stores = [
        pltpu.make_async_copy(
            in_ref.at[index], hbm_ref.at[pl.ds(index * rows, rows)], sems.at[index]
        )
        for index in range(in_ref.shape[0])
    ]
    for store in stores:
        store.start()
    for store in stores:
        store.wait()


def join_kernel(*refs):
    hbm_refs, vmem_refs, sems = refs[6:9], refs[9:12], refs[12]
    stores = [
        pltpu.make_async_copy(vmem, hbm, sems.at[index])
        for index, (vmem, hbm) in enumerate(zip(vmem_refs, hbm_refs))
    ]
    for own, far, vmem, store in zip(refs[:3], refs[3:6], vmem_refs, stores):
        vmem[...] = own[...] + far[...]
        store.start()
    for store in stores:
        store.wait()


def forward_kernel(grid_ref, *refs):
    rows, (k_img, v_img, qt_ref, ot_ref, lse_ref), refs = refs[:6], refs[6:11], refs[11:]
    out_ref, q_img, vt_ref = refs
    rank = lax.axis_index("dp")
    slot = lax.axis_index("seq")
    start, length = image_place(grid_ref, rank, slot)
    slot_rows, width = k_img.shape
    part_rows = rows[0].shape[0]
    inv_root = HEAD_DIM**-0.5
    pick_own = row_pick(slot_rows, part_rows, slot * part_rows, start, length)
    pick_far = row_pick(slot_rows, part_rows, (1 - slot) * part_rows, start, length)
    for own, far, image in zip(rows[0::2], rows[1::2], (q_img, k_img, v_img)):
        image[...] = (dot(pick_own, own[...], 1, 0) + dot(pick_far, far[...], 1, 0)).astype(
            image.dtype
        )
    identity = eye(slot_rows)
    for part in strips(width):
        qt_ref[part] = turn(identity, q_img[:, part]).astype(qt_ref.dtype)
        vt_ref[part] = turn(identity, v_img[:, part]).astype(vt_ref.dtype)
    key_bias = jnp.where(iota((slot_rows, 1), 0) < length, 0.0, -1e30)
    live = iota((1, slot_rows), 1) < length
    for head in range(width // HEAD_DIM):
        part = slice(head * HEAD_DIM, (head + 1) * HEAD_DIM)
        scores = dot(k_img[:, part], qt_ref[part], 1, 0) * inv_root + key_bias
        top = jnp.max(scores, axis=0, keepdims=True)
        weights = jnp.exp(scores - top)
        total = jnp.sum(weights, axis=0, keepdims=True)
        probs = (weights * jnp.where(live, 1.0 / total, 0.0)).astype(jnp.bfloat16)
        ot_ref[part] = dot(vt_ref[part], probs, 1, 0).astype(ot_ref.dtype)
        lse_ref[head : head + 1] = top + jnp.log(total)
    for part in strips(width):
        out_ref[:, part] = turn(identity, ot_ref[part]).astype(out_ref.dtype)


def backward_kernel(grid_ref, *refs):
    (k_img, v_img, qt_ref, ot_ref, lse_ref), refs = refs[:5], refs[5:]
    g_img, own_refs, far_refs, (gt_ref, kt_ref, *grad_refs) = refs[0], refs[1:4], refs[4:7], refs[7:]
    rank = lax.axis_index("dp")
    slot = lax.axis_index("seq")
    start, length = image_place(grid_ref, rank, slot)
    slot_rows, width = k_img.shape
    part_rows = own_refs[0].shape[0]
    inv_root = HEAD_DIM**-0.5
    identity = eye(slot_rows)
    live = iota((1, slot_rows), 1) < length
    for part in strips(width):
        gt_ref[part] = jnp.where(live, turn(identity, g_img[:, part]), 0.0).astype(gt_ref.dtype)
        kt_ref[part] = turn(identity, k_img[:, part]).astype(kt_ref.dtype)
    key_bias = jnp.where(iota((slot_rows, 1), 0) < length, 0.0, -1e30)
    dq_ref, dk_ref, dv_ref = grad_refs
    for head in range(width // HEAD_DIM):
        part = slice(head * HEAD_DIM, (head + 1) * HEAD_DIM)
        qt, gt = qt_ref[part], gt_ref[part]
        scores = dot(k_img[:, part], qt, 1, 0) * inv_root + key_bias
        probs = jnp.exp(scores - lse_ref[head : head + 1])
        grad_probs = dot(v_img[:, part], gt, 1, 0)
        row_dot = jnp.sum(
            gt.astype(jnp.float32) * ot_ref[part].astype(jnp.float32), axis=0, keepdims=True
        )
        grad_scores = (probs * (grad_probs - row_dot) * inv_root).astype(jnp.bfloat16)
        dq_ref[part] = dot(kt_ref[part], grad_scores, 1, 0).astype(dq_ref.dtype)
        dk_ref[part] = dot(qt, grad_scores, 1, 1).astype(dk_ref.dtype)
        dv_ref[part] = dot(gt, probs.astype(jnp.bfloat16), 1, 1).astype(dv_ref.dtype)
    put_own = row_pick(slot_rows, part_rows, slot * part_rows, start, length, True)
    put_far = row_pick(slot_rows, part_rows, (1 - slot) * part_rows, start, length, True)
    for grad, own, far in zip(grad_refs, own_refs, far_refs):
        own[...] = dot(put_own, grad[...], 1, 1).astype(own.dtype)
        far[...] = dot(put_far, grad[...], 1, 1).astype(far.dtype)


def bf16(*shape):
    return jax.ShapeDtypeStruct(shape, jnp.bfloat16)


def table(x):
    return jax.ShapeDtypeStruct(x.shape, x.dtype)


def local(query_rows, key_rows, value_rows, grad_hosted, image_grid, destination):
    ranks = lax.axis_size("dp")
    slot = lax.axis_index("seq")
    image_grid = jnp.transpose(image_grid, (1, 2, 0))
    destination = jnp.transpose(destination)
    part_rows, width = query_rows.shape
    slot_rows = grad_hosted.shape[0]
    heads = width // HEAD_DIM
    block = slot_rows // ranks
    by_pairs = ranks == len(STEPS) and block % 16 == 0
    flops = 2 * slot_rows * slot_rows * width
    exps = slot_rows * slot_rows * heads

    def swap(x):
        return lax.ppermute(x, "seq", [(0, 1), (1, 0)])

    def call(kernel, ins, outs, params, name, scratch=(), work=0, out_spec=VMEM, sems=0):
        return pl.pallas_call(
            kernel,
            out_shape=outs,
            in_specs=[SMEM if x.dtype == jnp.int32 else VMEM for x in ins],
            out_specs=[out_spec] * len(outs),
            scratch_shapes=[pltpu.VMEM(shape, jnp.bfloat16) for shape in scratch]
            + [pltpu.SemaphoreType.DMA((sems,))] * (sems > 0),
            compiler_params=params,
            cost_estimate=pl.CostEstimate(
                flops=work * flops + 1,
                bytes_accessed=sum(x.size * x.dtype.itemsize for x in (*ins, *outs)),
                transcendentals=exps if work else 0,
            ),
            name=name,
        )(*ins)

    def spread(x):
        return lax.all_to_all(x, "dp", 0, 0, tiled=True)

    def exchange(blocks):
        return [
            lax.ppermute(x, "dp", [(rank, rank ^ step) for rank in range(ranks)]) if step else x
            for step, x in zip(STEPS, blocks)
        ]

    rows = []
    for x in (query_rows, key_rows, value_rows):
        rows += [x, swap(x)]
    grad_spread = spread(grad_hosted.reshape(ranks, block, width))
    k_img, v_img, q_turned, out_turned, lse, attended = call(
        forward_kernel,
        (image_grid, *rows),
        [bf16(slot_rows, width)] * 2
        + [bf16(width, slot_rows)] * 2
        + [jax.ShapeDtypeStruct((heads, slot_rows), jnp.float32)]
        + [bf16(slot_rows, width)],
        LARGE,
        "attend",
        scratch=[(slot_rows, width), (width, slot_rows)],
        work=2,
    )
    if by_pairs:
        messages = call(
            to_lister_kernel,
            (destination, attended, grad_spread),
            [bf16(2 * block, width)] * ranks,
            SMALL,
            "to_lister",
        )
        host_order, grad_slot = call(
            to_host_kernel,
            (destination, *exchange(messages)),
            [bf16(ranks, block, width), bf16(slot_rows, width)],
            SMALL,
            "to_host",
        )
        (hosted_out,) = call(
            store_kernel,
            (spread(host_order),),
            [bf16(slot_rows, width)],
            SMALL,
            "store",
            out_spec=HBM,
            sems=ranks,
        )
    else:
        dest = lax.dynamic_index_in_dim(destination, slot, 0, keepdims=False)
        rank_ids = jnp.arange(ranks, dtype=jnp.int32)
        source = jnp.sum(
            jnp.where(dest[None, :] == rank_ids[:, None], rank_ids[None, :], 0), axis=1
        )
        both = spread(
            jnp.concatenate([grad_spread[dest], attended.reshape(ranks, block, width)], axis=1)
        )
        grad_slot = both[:, :block].reshape(slot_rows, width)
        hosted_out = spread(both[source, block:]).reshape(slot_rows, width)
    grads = call(
        backward_kernel,
        (image_grid, k_img, v_img, q_turned, out_turned, lse, grad_slot),
        [bf16(part_rows, width)] * 6,
        LARGE,
        "attend_back",
        scratch=[(width, slot_rows)] * 5,
        work=5,
    )
    grad_query, grad_key, grad_value = call(
        join_kernel,
        (*grads[:3], *(swap(x) for x in grads[3:])),
        [bf16(part_rows, width)] * 3,
        SMALL,
        "join",
        scratch=[(part_rows, width)] * 3,
        out_spec=HBM,
        sems=3,
    )
    return hosted_out, grad_query, grad_key, grad_value


def solution(mesh):
    rows = P(("groups", "dp", "seq"), None)
    return jax.shard_map(
        local,
        mesh=mesh,
        in_specs=(rows, rows, rows, rows, P("groups", None, None), P("groups", None)),
        out_specs=(rows,) * 4,
        check_vma=False,
    )
```

time: 88.6 us -> 81.2 us (0.916)
  blocking collectives: 36.6 us -> 0 us
  waiting for transfers between devices: 4.91 us -> 27.9 us
  starting transfers between devices: 12.4 us -> 26.6 us
  Pallas kernels: 25.6 us -> 18.7 us
  other arithmetic: 2.69 us -> 0 us
  local copies, waits for them, and re-layouts: 5.18 us -> 6.58 us
    all_to_all x1 -> x0, blocking collectives: 36.6 us -> none  [spread(): return lax.all_to_all(x, 'dp', 0, 0, tiled=True)]
    ppermute x0 -> x7, waiting for transfers between devices: none -> 15.8 us  [exchange(): lax.ppermute(x, 'dp', [(rank, rank ^ step) for rank in range(ranks)])]
    ppermute x0 -> x7, starting transfers between devices: none -> 12.3 us  [exchange(): lax.ppermute(x, 'dp', [(rank, rank ^ step) for rank in range(ranks)])]
    pallas_call x4 -> x6, Pallas kernels: 25.6 us -> 18.7 us  [call(): pl.pallas_call(kernel, out_shape=outs, in_specs=[SMEM if x.dtype == jnp.i...]
    all_to_all x2, waiting for transfers between devices: 1.52 us -> 6.49 us  [spread(): return lax.all_to_all(x, 'dp', 0, 0, tiled=True)]
    add x3 -> x0, other arithmetic: 2.69 us -> none  [local(): own + swap(far)]
    ppermute x6, waiting for transfers between devices: 3.39 us -> 5.56 us  [swap(): return lax.ppermute(x, 'seq', [(0, 1), (1, 0)])]
    all_to_all x2, starting transfers between devices: 11.1 us -> 13 us  [spread(): return lax.all_to_all(x, 'dp', 0, 0, tiled=True)]
  transfers between devices with their start and end apart: 8 -> 15, of which waited for: 6 -> 12; matrix products, arithmetic and copies ran while one was open for 4% -> 0% of each run, Pallas kernels for 24% -> 19%
where the time goes in v3:
time: 81.2 us; the launch traced here: 80.7 us
  waiting for transfers between devices  27.9 us (34%)
  starting transfers between devices  26.6 us (33%)
  Pallas kernels  18.7 us (23%)
  local copies, waits for them, and re-layouts  6.58 us (8%)
  between operations  0.92 us (1%)
    pallas_call x6, Pallas kernels, call(): pl.pallas_call(kernel, out_shape=outs, in_specs=[SMEM if x.dtype == jnp.i...  18.7 us
    ppermute x7, waiting for transfers between devices, exchange(): lax.ppermute(x, 'dp', [(rank, rank ^ step) for rank in range(ranks)])  15.8 us
    all_to_all x2, starting transfers between devices, spread(): return lax.all_to_all(x, 'dp', 0, 0, tiled=True)  13 us
    ppermute x7, starting transfers between devices, exchange(): lax.ppermute(x, 'dp', [(rank, rank ^ step) for rank in range(ranks)])  12.3 us
    unnamed x22, local copies, waits for them, and re-layouts  6.58 us
    all_to_all x2, waiting for transfers between devices, spread(): return lax.all_to_all(x, 'dp', 0, 0, tiled=True)  6.49 us
    ppermute x6, waiting for transfers between devices, swap(): return lax.ppermute(x, 'seq', [(0, 1), (1, 0)])  5.56 us
  transfers between devices with their start and end apart: 15, of which 12 were waited for; matrix products, arithmetic and copies ran while one was open for 0% of the time, Pallas kernels for 19%

profile of v3, /device:TPU:0, one launch (start us, length us, event | category | flops | bytes accessed | tf_op | source)
XLA Modules:
  0.0 80.7 jit_solution(10443013969865348808)
XLA Ops:
  0.6 0.0 copy-start.4
  0.6 0.0 copy-start.6
  0.7 0.0 copy-start.9
  0.7 7.4 %all-to-all-start = ((bf16[8,32,1280]{2,1,0:T(8,128)(2,1)}), bf16[8,32,1280]{2,1,0:T(8,128)(2,1)S(1)}, u32[]{:S(2)}, u32[]{:S(2)}) async-start(bf16[8,32,1280]{2,1,0:T(8,128)(2,1)} %bitcast.7), calls=%async_computation | async-start | bytes 1310720 | tf_op jit(solution)/shard_map/all_to_all | solution.py:228
  8.1 0.1 collective-permute-start
  8.2 0.5 collective-permute-start.1
  8.6 0.1 collective-permute-start.2
  8.7 1.3 %collective-permute-done.refs_1_ = bf16[192,1280]{1,0:T(8,128)(2,1)S(1)} collective-permute-done((bf16[192,1280]{1,0:T(8,128)(2,1)S(1)}, bf16[192,1280]{1,0:T(8,128)(2,1)S(1)}, u32[]{:S(2)}, u32[]{:S(2)}) %collective-permute-start) | collective-permute-done | bytes 491552 | tf_op jit(solution)/shard_map/ppermute | solution.py:208
  10.0 1.4 %collective-permute-done.1.refs_3_ = bf16[192,1280]{1,0:T(8,128)(2,1)S(1)} collective-permute-done((bf16[192,1280]{1,0:T(8,128)(2,1)S(1)}, bf16[192,1280]{1,0:T(8,128)(2,1)S(1)}, u32[]{:S(2)}, u32[]{:S(2)}) %collective-permute-start.1) | collective-permute-done | bytes 491552 | tf_op jit(solution)/shard_map/ppermute | solution.py:208
  11.4 0.2 collective-permute-done.2.refs_5_
  11.6 0.0 copy-done.9
  11.6 1.0 %copy-done.5 = bf16[192,1280]{1,0:T(8,128)(2,1)S(1)} copy-done((bf16[192,1280]{1,0:T(8,128)(2,1)S(1)}, bf16[192,1280]{1,0:T(8,128)(2,1)}, u32[]{:S(2)}) %copy-start.5) | copy-done | bytes 491544
  12.6 1.0 %copy-done.7 = bf16[192,1280]{1,0:T(8,128)(2,1)S(1)} copy-done((bf16[192,1280]{1,0:T(8,128)(2,1)S(1)}, bf16[192,1280]{1,0:T(8,128)(2,1)}, u32[]{:S(2)}) %copy-start.7) | copy-done | bytes 491544
  13.7 1.0 %copy-done.8 = bf16[192,1280]{1,0:T(8,128)(2,1)S(1)} copy-done((bf16[192,1280]{1,0:T(8,128)(2,1)S(1)}, bf16[192,1280]{1,0:T(8,128)(2,1)}, u32[]{:S(2)}) %copy-start.8) | copy-done | bytes 491544
  14.7 7.4 %attend.1 = (bf16[256,1280]{1,0:T(8,128)(2,1)S(1)}, bf16[256,1280]{1,0:T(8,128)(2,1)S(1)}, bf16[1280,256]{1,0:T(8,128)(2,1)S(1)}, bf16[1280,256]{1,0:T(8,128)(2,...) custom-call(s32[2,2,8]{2,1,0:T(2,128)S(1)} %bitcast.3, bf16[192,1280]{1,0:T(8,128)(2,1)S(1)} %copy-done.5, ...), custom_call_target="tpu_custom_call" | custom-call | flops 335544320 | bytes 6242432 | tf_op jit(solution)/shard_map/attend/pallas_call | solution.py:211
  22.1 0.8 %copy-done = bf16[1280,256]{1,0:T(8,128)(2,1)} copy-done((bf16[1280,256]{1,0:T(8,128)(2,1)}, bf16[1280,256]{1,0:T(8,128)(2,1)S(1)}, u32[]{:S(2)}) %copy-start) | copy-done | bytes 655384
  23.0 2.4 %all-to-all-done.in_ref = bf16[8,32,1280]{2,1,0:T(8,128)(2,1)S(1)} async-done(((bf16[8,32,1280]{2,1,0:T(8,128)(2,1)}), bf16[8,32,1280]{2,1,0:T(8,128)(2,1)S(1)}, u32[]{:S(2)}, u32[]{:S(2)}) %all-to-all-start) | async-done | bytes 655392 | tf_op jit(solution)/shard_map/all_to_all | solution.py:228
  25.4 0.7 copy-done.10
  26.0 0.6 to_lister.1
  26.7 2.4 %collective-permute-start.3 = (bf16[64,1280]{1,0:T(8,128)(2,1)S(1)}, bf16[64,1280]{1,0:T(8,128)(2,1)S(1)}, u32[]{:S(2)}, u32[]{:S(2)}) collective-permute-start(bf16[64,1280]{1,0:T(8,128)(2,1)S(1)} %get-tuple-element.31), channel_id=1, source_target_pairs={{0,14},{2,12},{4,10},{6,8},{8,6},{10,4},{12,2},{14,0},{1,15},{3,13... | collective-permute-start | bytes 491528 | tf_op jit(solution)/shard_map/ppermute | solution.py:232
  29.1 0.5 collective-permute-start.4
  29.6 0.0 collective-permute-start.5
  29.6 3.9 %collective-permute-start.6 = (bf16[64,1280]{1,0:T(8,128)(2,1)S(1)}, bf16[64,1280]{1,0:T(8,128)(2,1)S(1)}, u32[]{:S(2)}, u32[]{:S(2)}) collective-permute-start(bf16[64,1280]{1,0:T(8,128)(2,1)S(1)} %get-tuple-element.34), channel_id=1, source_target_pairs={{0,10},{2,8},{4,14},{6,12},{8,2},{10,0},{12,6},{14,4},{1,11},{3,9}... | collective-permute-start | bytes 491528 | tf_op jit(solution)/shard_map/ppermute | solution.py:232
  33.5 0.0 collective-permute-start.7
  33.5 3.0 %collective-permute-done.3.refs_1_ = bf16[64,1280]{1,0:T(8,128)(2,1)S(1)} collective-permute-done((bf16[64,1280]{1,0:T(8,128)(2,1)S(1)}, bf16[64,1280]{1,0:T(8,128)(2,1)S(1)}, u32[]{:S(2)}, u32[]{:S(2)}) %collective-permute-start.3) | collective-permute-done | bytes 163872 | tf_op jit(solution)/shard_map/ppermute | solution.py:232
  36.5 2.2 %collective-permute-start.8 = (bf16[64,1280]{1,0:T(8,128)(2,1)S(1)}, bf16[64,1280]{1,0:T(8,128)(2,1)S(1)}, u32[]{:S(2)}, u32[]{:S(2)}) collective-permute-start(bf16[64,1280]{1,0:T(8,128)(2,1)S(1)} %get-tuple-element.36), channel_id=1, source_target_pairs={{0,8},{2,10},{4,12},{6,14},{8,0},{10,2},{12,4},{14,6},{1,9},{3,11}... | collective-permute-start | bytes 491528 | tf_op jit(solution)/shard_map/ppermute | solution.py:232
  38.7 0.3 collective-permute-done.4.refs_2_
  39.0 3.3 %collective-permute-start.9 = (bf16[64,1280]{1,0:T(8,128)(2,1)S(1)}, bf16[64,1280]{1,0:T(8,128)(2,1)S(1)}, u32[]{:S(2)}, u32[]{:S(2)}) collective-permute-start(bf16[64,1280]{1,0:T(8,128)(2,1)S(1)} %get-tuple-element.37), channel_id=1, source_target_pairs={{0,12},{2,14},{4,8},{6,10},{8,4},{10,6},{12,0},{14,2},{1,13},{3,15... | collective-permute-start | bytes 491528 | tf_op jit(solution)/shard_map/ppermute | solution.py:232
  42.3 0.0 collective-permute-done.5.refs_3_
  42.3 4.8 %collective-permute-done.6.refs_4_ = bf16[64,1280]{1,0:T(8,128)(2,1)S(1)} collective-permute-done((bf16[64,1280]{1,0:T(8,128)(2,1)S(1)}, bf16[64,1280]{1,0:T(8,128)(2,1)S(1)}, u32[]{:S(2)}, u32[]{:S(2)}) %collective-permute-start.6) | collective-permute-done | bytes 163872 | tf_op jit(solution)/shard_map/ppermute | solution.py:232
  47.0 0.0 collective-permute-done.7.refs_5_
  47.0 7.8 %collective-permute-done.8.refs_6_ = bf16[64,1280]{1,0:T(8,128)(2,1)S(1)} collective-permute-done((bf16[64,1280]{1,0:T(8,128)(2,1)S(1)}, bf16[64,1280]{1,0:T(8,128)(2,1)S(1)}, u32[]{:S(2)}, u32[]{:S(2)}) %collective-permute-start.8) | collective-permute-done | bytes 163872 | tf_op jit(solution)/shard_map/ppermute | solution.py:232
  54.8 0.0 collective-permute-done.9.refs_7_
  54.8 1.5 %to_host.1 = (bf16[8,32,1280]{2,1,0:T(8,128)(2,1)}, bf16[256,1280]{1,0:T(8,128)(2,1)S(1)}) custom-call(s32[2,8]{1,0:T(2,128)S(1)} %bitcast.6, bf16[64,1280]{1,0:T(8,128)(2,1)S(1)} %get-tuple-element.30.refs_0_, bf16[64,1280]{1,0:T(8,128)(2,1)S(1)} %collective-permute-done.3.refs_1_, bf16[64,1280]{1,0:T(8,128)(2,1)S(1)} %collective-permute-done.4.refs_2_, ...), custom_call_target="tpu_custom_call" | custom-call | flops 1 | bytes 2621504 | tf_op jit(solution)/shard_map/to_host/pallas_call | solution.py:211
  56.3 0.9 %copy-done.2 = bf16[256,1280]{1,0:T(8,128)(2,1)} copy-done((bf16[256,1280]{1,0:T(8,128)(2,1)}, bf16[256,1280]{1,0:T(8,128)(2,1)S(1)}, u32[]{:S(2)}) %copy-start.2) | copy-done | bytes 655384
  57.2 5.6 %all-to-all-start.1 = ((bf16[8,32,1280]{2,1,0:T(8,128)(2,1)}), bf16[8,32,1280]{2,1,0:T(8,128)(2,1)S(1)}, u32[]{:S(2)}, u32[]{:S(2)}) async-start(bf16[8,32,1280]{2,1,0:T(8,128)(2,1)} %get-tuple-element.38), calls=%async_computation.1 | async-start | bytes 1310720 | tf_op jit(solution)/shard_map/all_to_all | solution.py:228
  62.8 0.0 copy-done.1
  62.8 1.1 %copy-done.3 = bf16[256,1280]{1,0:T(8,128)(2,1)S(1)} copy-done((bf16[256,1280]{1,0:T(8,128)(2,1)S(1)}, bf16[256,1280]{1,0:T(8,128)(2,1)}, u32[]{:S(2)}) %copy-start.3) | copy-done | bytes 655384
  63.9 7.1 %attend_back.1 = (bf16[192,1280]{1,0:T(8,128)(2,1)S(1)}, bf16[192,1280]{1,0:T(8,128)(2,1)S(1)}, bf16[192,1280]{1,0:T(8,128)(2,1)S(1)}, bf16[192,1280]{1,0:T(8,12...) custom-call(s32[2,2,8]{2,1,0:T(2,128)S(1)} %bitcast.4, ...), custom_call_target="tpu_custom_call" | custom-call | flops 838860800 | bytes 6242432 | tf_op jit(solution)/shard_map/attend_back/pallas_call | solution.py:211
  71.0 0.1 collective-permute-start.10
  71.1 0.5 collective-permute-start.11
  71.6 0.1 collective-permute-start.12
  71.6 1.3 %collective-permute-done.10.refs_3_ = bf16[192,1280]{1,0:T(8,128)(2,1)S(1)} collective-permute-done((bf16[192,1280]{1,0:T(8,128)(2,1)S(1)}, bf16[192,1280]{1,0:T(8,128)(2,1)S(1)}, u32[]{:S(2)}, u32[]{:S(2)}) %collective-permute-start.10) | collective-permute-done | bytes 491552 | tf_op jit(solution)/shard_map/ppermute | solution.py:208
  72.9 0.7 collective-permute-done.11.refs_4_
  73.6 0.7 collective-permute-done.12.refs_5_
  74.3 1.2 %join.1 = (bf16[192,1280]{1,0:T(8,128)(2,1)}, bf16[192,1280]{1,0:T(8,128)(2,1)}, bf16[192,1280]{1,0:T(8,128)(2,1)}) custom-call(bf16[192,1280]{1,0:T(8,128)(2,1)S(1)} %get-tuple-element.45.refs_0_, bf16[192,1280]{1,0:T(8,128)(2,1)S(1)} %get-tuple-element.46.refs_1_, bf16[192,1280]{1,0:T(8,128)(2,1)S(1)} %get-tuple-element.47.refs_2_, ...), custom_call_target="tpu_custom_call" | custom-call | flops 1 | bytes 4423680 | tf_op jit(solution)/shard_map/join/pallas_call | solution.py:211
  75.5 4.1 %all-to-all-done.1.in_ref = bf16[8,32,1280]{2,1,0:T(8,128)(2,1)S(1)} async-done(((bf16[8,32,1280]{2,1,0:T(8,128)(2,1)}), bf16[8,32,1280]{2,1,0:T(8,128)(2,1)S(1)}, u32[]{:S(2)}, u32[]{:S(2)}) %all-to-all-start.1) | async-done | bytes 655392 | tf_op jit(solution)/shard_map/all_to_all | solution.py:228
  79.6 0.9 %store.1 = bf16[256,1280]{1,0:T(8,128)(2,1)} custom-call(bf16[8,32,1280]{2,1,0:T(8,128)(2,1)S(1)} %all-to-all-done.1.in_ref), custom_call_target="tpu_custom_call" | custom-call | flops 1 | bytes 1310720 | tf_op jit(solution)/shard_map/store/pallas_call | solution.py:211
  (10 shorter events, 0.0 us)
Async XLA Ops:
  0.6 7.4 %copy-start.4 = (bf16[192,1280]{1,0:T(8,128)(2,1)S(1)}, bf16[192,1280]{1,0:T(8,128)(2,1)}, u32[]{:S(2)}) copy-start(bf16[192,1280]{1,0:T(8,128)(2,1)} %refs_0_.1) | copy-start | bytes 1474564
  0.6 7.5 %copy-start.6 = (bf16[192,1280]{1,0:T(8,128)(2,1)S(1)}, bf16[192,1280]{1,0:T(8,128)(2,1)}, u32[]{:S(2)}) copy-start(bf16[192,1280]{1,0:T(8,128)(2,1)} %refs_2_.1) | copy-start | bytes 1474564
  0.7 11.0 %copy-start.9 = (s32[8,2,2]{0,2,1:T(2,128)S(1)}, s32[8,2,2]{0,2,1:T(2,128)}, u32[]{:S(2)}) copy-start(s32[8,2,2]{0,2,1:T(2,128)} %param.10) | copy-start | bytes 388
  0.7 24.7 %all-to-all-start = ((bf16[8,32,1280]{2,1,0:T(8,128)(2,1)}), bf16[8,32,1280]{2,1,0:T(8,128)(2,1)S(1)}, u32[]{:S(2)}, u32[]{:S(2)}) async-start(bf16[8,32,1280]{2,1,0:T(8,128)(2,1)} %bitcast.7), calls=%async_computation | async-start | bytes 1310720 | tf_op jit(solution)/shard_map/all_to_all | solution.py:228
  8.1 1.9 %collective-permute-start = (bf16[192,1280]{1,0:T(8,128)(2,1)S(1)}, bf16[192,1280]{1,0:T(8,128)(2,1)S(1)}, u32[]{:S(2)}, u32[]{:S(2)}) collective-permute-start(bf16[192,1280]{1,0:T(8,128)(2,1)S(1)} %copy-done.4), channel_id=1, source_target_pairs={{0,1},{1,0},{2,3},{3,2},{4,5},{5,4},{6,7},{7,6},{8,9},{9,8},{10,11... | collective-permute-start | bytes 1474568 | tf_op jit(solution)/shard_map/ppermute | solution.py:208
  8.2 3.2 %collective-permute-start.1 = (bf16[192,1280]{1,0:T(8,128)(2,1)S(1)}, bf16[192,1280]{1,0:T(8,128)(2,1)S(1)}, u32[]{:S(2)}, u32[]{:S(2)}) collective-permute-start(bf16[192,1280]{1,0:T(8,128)(2,1)S(1)} %copy-done.6), channel_id=1, source_target_pairs={{0,1},{1,0},{2,3},{3,2},{4,5},{5,4},{6,7},{7,6},{8,9},{9,8},{10,11... | collective-permute-start | bytes 1474568 | tf_op jit(solution)/shard_map/ppermute | solution.py:208
  8.6 3.0 %collective-permute-start.2 = (bf16[192,1280]{1,0:T(8,128)(2,1)}, bf16[192,1280]{1,0:T(8,128)(2,1)S(1)}, u32[]{:S(2)}, u32[]{:S(2)}) collective-permute-start(bf16[192,1280]{1,0:T(8,128)(2,1)} %refs_4_.1), channel_id=1, source_target_pairs={{0,1},{1,0},{2,3},{3,2},{4,5},{5,4},{6,7},{7,6},{8,9},{9,8},{10,11... | collective-permute-start | bytes 1474568 | tf_op jit(solution)/shard_map/ppermute | solution.py:208
  11.6 1.0 %copy-start.5 = (bf16[192,1280]{1,0:T(8,128)(2,1)S(1)}, bf16[192,1280]{1,0:T(8,128)(2,1)}, u32[]{:S(2)}) copy-start(bf16[192,1280]{1,0:T(8,128)(2,1)} %refs_0_.1) | copy-start | bytes 1474564
  12.6 1.0 %copy-start.7 = (bf16[192,1280]{1,0:T(8,128)(2,1)S(1)}, bf16[192,1280]{1,0:T(8,128)(2,1)}, u32[]{:S(2)}) copy-start(bf16[192,1280]{1,0:T(8,128)(2,1)} %refs_2_.1) | copy-start | bytes 1474564
  13.7 1.0 %copy-start.8 = (bf16[192,1280]{1,0:T(8,128)(2,1)S(1)}, bf16[192,1280]{1,0:T(8,128)(2,1)}, u32[]{:S(2)}) copy-start(bf16[192,1280]{1,0:T(8,128)(2,1)} %refs_4_.1) | copy-start | bytes 1474564
  22.1 0.8 %copy-start = (bf16[1280,256]{1,0:T(8,128)(2,1)}, bf16[1280,256]{1,0:T(8,128)(2,1)S(1)}, u32[]{:S(2)}) copy-start(bf16[1280,256]{1,0:T(8,128)(2,1)S(1)} %get-tuple-element.42.refs_3_) | copy-start | bytes 1966084
  25.4 0.7 copy-start.10
  26.7 9.8 %collective-permute-start.3 = (bf16[64,1280]{1,0:T(8,128)(2,1)S(1)}, bf16[64,1280]{1,0:T(8,128)(2,1)S(1)}, u32[]{:S(2)}, u32[]{:S(2)}) collective-permute-start(bf16[64,1280]{1,0:T(8,128)(2,1)S(1)} %get-tuple-element.31), channel_id=1, source_target_pairs={{0,14},{2,12},{4,10},{6,8},{8,6},{10,4},{12,2},{14,0},{1,15},{3,13... | collective-permute-start | bytes 491528 | tf_op jit(solution)/shard_map/ppermute | solution.py:232
  29.1 9.9 %collective-permute-start.4 = (bf16[64,1280]{1,0:T(8,128)(2,1)S(1)}, bf16[64,1280]{1,0:T(8,128)(2,1)S(1)}, u32[]{:S(2)}, u32[]{:S(2)}) collective-permute-start(bf16[64,1280]{1,0:T(8,128)(2,1)S(1)} %get-tuple-element.32), channel_id=1, source_target_pairs={{0,2},{2,0},{4,6},{6,4},{8,10},{10,8},{12,14},{14,12},{1,3},{3,1},... | collective-permute-start | bytes 491528 | tf_op jit(solution)/shard_map/ppermute | solution.py:232
  29.6 12.7 %collective-permute-start.5 = (bf16[64,1280]{1,0:T(8,128)(2,1)S(1)}, bf16[64,1280]{1,0:T(8,128)(2,1)S(1)}, u32[]{:S(2)}, u32[]{:S(2)}) collective-permute-start(bf16[64,1280]{1,0:T(8,128)(2,1)S(1)} %get-tuple-element.33), channel_id=1, source_target_pairs={{0,4},{2,6},{4,0},{6,2},{8,12},{10,14},{12,8},{14,10},{1,5},{3,7},... | collective-permute-start | bytes 491528 | tf_op jit(solution)/shard_map/ppermute | solution.py:232
  29.6 17.4 %collective-permute-start.6 = (bf16[64,1280]{1,0:T(8,128)(2,1)S(1)}, bf16[64,1280]{1,0:T(8,128)(2,1)S(1)}, u32[]{:S(2)}, u32[]{:S(2)}) collective-permute-start(bf16[64,1280]{1,0:T(8,128)(2,1)S(1)} %get-tuple-element.34), channel_id=1, source_target_pairs={{0,10},{2,8},{4,14},{6,12},{8,2},{10,0},{12,6},{14,4},{1,11},{3,9}... | collective-permute-start | bytes 491528 | tf_op jit(solution)/shard_map/ppermute | solution.py:232
  33.5 13.5 %collective-permute-start.7 = (bf16[64,1280]{1,0:T(8,128)(2,1)S(1)}, bf16[64,1280]{1,0:T(8,128)(2,1)S(1)}, u32[]{:S(2)}, u32[]{:S(2)}) collective-permute-start(bf16[64,1280]{1,0:T(8,128)(2,1)S(1)} %get-tuple-element.35), channel_id=1, source_target_pairs={{0,6},{2,4},{4,2},{6,0},{8,14},{10,12},{12,10},{14,8},{1,7},{3,5},... | collective-permute-start | bytes 491528 | tf_op jit(solution)/shard_map/ppermute | solution.py:232
  36.5 18.3 %collective-permute-start.8 = (bf16[64,1280]{1,0:T(8,128)(2,1)S(1)}, bf16[64,1280]{1,0:T(8,128)(2,1)S(1)}, u32[]{:S(2)}, u32[]{:S(2)}) collective-permute-start(bf16[64,1280]{1,0:T(8,128)(2,1)S(1)} %get-tuple-element.36), channel_id=1, source_target_pairs={{0,8},{2,10},{4,12},{6,14},{8,0},{10,2},{12,4},{14,6},{1,9},{3,11}... | collective-permute-start | bytes 491528 | tf_op jit(solution)/shard_map/ppermute | solution.py:232
  39.0 15.8 %collective-permute-start.9 = (bf16[64,1280]{1,0:T(8,128)(2,1)S(1)}, bf16[64,1280]{1,0:T(8,128)(2,1)S(1)}, u32[]{:S(2)}, u32[]{:S(2)}) collective-permute-start(bf16[64,1280]{1,0:T(8,128)(2,1)S(1)} %get-tuple-element.37), channel_id=1, source_target_pairs={{0,12},{2,14},{4,8},{6,10},{8,4},{10,6},{12,0},{14,2},{1,13},{3,15... | collective-permute-start | bytes 491528 | tf_op jit(solution)/shard_map/ppermute | solution.py:232
  56.3 0.9 %copy-start.2 = (bf16[256,1280]{1,0:T(8,128)(2,1)}, bf16[256,1280]{1,0:T(8,128)(2,1)S(1)}, u32[]{:S(2)}) copy-start(bf16[256,1280]{1,0:T(8,128)(2,1)S(1)} %get-tuple-element.44.refs_5_) | copy-start | bytes 1966084
  57.2 5.6 %copy-start.1 = (bf16[1280,256]{1,0:T(8,128)(2,1)S(1)}, bf16[1280,256]{1,0:T(8,128)(2,1)}, u32[]{:S(2)}) copy-start(bf16[1280,256]{1,0:T(8,128)(2,1)} %copy-done) | copy-start | bytes 1966084
  57.2 22.4 %all-to-all-start.1 = ((bf16[8,32,1280]{2,1,0:T(8,128)(2,1)}), bf16[8,32,1280]{2,1,0:T(8,128)(2,1)S(1)}, u32[]{:S(2)}, u32[]{:S(2)}) async-start(bf16[8,32,1280]{2,1,0:T(8,128)(2,1)} %get-tuple-element.38), calls=%async_computation.1 | async-start | bytes 1310720 | tf_op jit(solution)/shard_map/all_to_all | solution.py:228
  62.8 1.1 %copy-start.3 = (bf16[256,1280]{1,0:T(8,128)(2,1)S(1)}, bf16[256,1280]{1,0:T(8,128)(2,1)}, u32[]{:S(2)}) copy-start(bf16[256,1280]{1,0:T(8,128)(2,1)} %copy-done.2) | copy-start | bytes 1966084
  71.0 1.9 %collective-permute-start.10 = (bf16[192,1280]{1,0:T(8,128)(2,1)S(1)}, bf16[192,1280]{1,0:T(8,128)(2,1)S(1)}, u32[]{:S(2)}, u32[]{:S(2)}) collective-permute-start(bf16[192,1280]{1,0:T(8,128)(2,1)S(1)} %get-tuple-element.48), channel_id=1, source_target_pairs={{0,1},{1,0},{2,3},{3,2},{4,5},{5,4},{6,7},{7,6},{8,9},{9,8},{10,11... | collective-permute-start | bytes 1474568 | tf_op jit(solution)/shard_map/ppermute | solution.py:208
  71.1 2.6 %collective-permute-start.11 = (bf16[192,1280]{1,0:T(8,128)(2,1)S(1)}, bf16[192,1280]{1,0:T(8,128)(2,1)S(1)}, u32[]{:S(2)}, u32[]{:S(2)}) collective-permute-start(bf16[192,1280]{1,0:T(8,128)(2,1)S(1)} %get-tuple-element.49), channel_id=1, source_target_pairs={{0,1},{1,0},{2,3},{3,2},{4,5},{5,4},{6,7},{7,6},{8,9},{9,8},{10,11... | collective-permute-start | bytes 1474568 | tf_op jit(solution)/shard_map/ppermute | solution.py:208
  71.6 2.8 %collective-permute-start.12 = (bf16[192,1280]{1,0:T(8,128)(2,1)S(1)}, bf16[192,1280]{1,0:T(8,128)(2,1)S(1)}, u32[]{:S(2)}, u32[]{:S(2)}) collective-permute-start(bf16[192,1280]{1,0:T(8,128)(2,1)S(1)} %get-tuple-element.50), channel_id=1, source_target_pairs={{0,1},{1,0},{2,3},{3,2},{4,5},{5,4},{6,7},{7,6},{8,9},{9,8},{10,11... | collective-permute-start | bytes 1474568 | tf_op jit(solution)/shard_map/ppermute | solution.py:208

commit v4 on v3

--- a/solution.py
+++ b/solution.py
@@ -67,23 +67,22 @@
     return pl.ds(pl.multiple_of(to * rows, rows), rows)
 
 
-def to_lister_kernel(dest_ref, attended_ref, in_ref, *out_refs):
+def to_lister_kernel(dest_ref, in_ref, *out_refs):
     rank = lax.axis_index("dp")
     slot = lax.axis_index("seq")
-    rows = in_ref.shape[1]
     for step, out_ref in zip(STEPS, out_refs):
-        out_ref[:rows] = in_ref[dest_ref[slot, rank ^ step]]
-        out_ref[rows:] = attended_ref[block_of(rank ^ step, rows), :]
+        out_ref[...] = in_ref[dest_ref[slot, rank ^ step]]
 
 
 def to_host_kernel(dest_ref, *refs):
     rank = lax.axis_index("dp")
     slot = lax.axis_index("seq")
-    in_refs, (out_ref, grad_ref) = refs[:-2], refs[-2:]
+    count = len(STEPS)
+    out_ref, grad_ref = refs[-2:]
     rows = out_ref.shape[1]
-    for step, in_ref in zip(STEPS, in_refs):
-        out_ref[dest_ref[slot, rank ^ step]] = in_ref[rows:]
-        grad_ref[block_of(rank ^ step, rows), :] = in_ref[:rows]
+    for step, o_ref, g_ref in zip(STEPS, refs[:count], refs[count : 2 * count]):
+        out_ref[dest_ref[slot, rank ^ step]] = o_ref[...]
+        grad_ref[block_of(rank ^ step, rows), :] = g_ref[...]
 
 
 def store_kernel(in_ref, hbm_ref, sems):
@@ -115,7 +114,7 @@
 
 def forward_kernel(grid_ref, *refs):
     rows, (k_img, v_img, qt_ref, ot_ref, lse_ref), refs = refs[:6], refs[6:11], refs[11:]
-    out_ref, q_img, vt_ref = refs
+    out_refs, (q_img, vt_ref, out_rows) = refs[:-3], refs[-3:]
     rank = lax.axis_index("dp")
     slot = lax.axis_index("seq")
     start, length = image_place(grid_ref, rank, slot)
@@ -134,17 +133,36 @@
         vt_ref[part] = turn(identity, v_img[:, part]).astype(vt_ref.dtype)
     key_bias = jnp.where(iota((slot_rows, 1), 0) < length, 0.0, -1e30)
     live = iota((1, slot_rows), 1) < length
-    for head in range(width // HEAD_DIM):
-        part = slice(head * HEAD_DIM, (head + 1) * HEAD_DIM)
-        scores = dot(k_img[:, part], qt_ref[part], 1, 0) * inv_root + key_bias
+    parts = [slice(at, at + HEAD_DIM) for at in range(0, width, HEAD_DIM)]
+    raws = {}
+    late = []
+
+    def finish():
+        part, probs = late.pop(0)
+        ot_ref[part] = dot(vt_ref[part], probs, 1, 0).astype(ot_ref.dtype)
+
+    for head, part in enumerate(parts):
+        for other in range(head, min(head + 1 + 2, len(parts))):
+            if other not in raws:
+                raws[other] = dot(k_img[:, parts[other]], qt_ref[parts[other]], 1, 0)
+        if len(late) > 1:
+            finish()
+        scores = raws[head] * inv_root + key_bias
         top = jnp.max(scores, axis=0, keepdims=True)
         weights = jnp.exp(scores - top)
         total = jnp.sum(weights, axis=0, keepdims=True)
         probs = (weights * jnp.where(live, 1.0 / total, 0.0)).astype(jnp.bfloat16)
-        ot_ref[part] = dot(vt_ref[part], probs, 1, 0).astype(ot_ref.dtype)
         lse_ref[head : head + 1] = top + jnp.log(total)
+        late.append((part, probs))
+    while late:
+        finish()
     for part in strips(width):
-        out_ref[:, part] = turn(identity, ot_ref[part]).astype(out_ref.dtype)
+        out_rows[:, part] = turn(identity, ot_ref[part]).astype(out_rows.dtype)
+    if len(out_refs) > 1:
+        for step, out_ref in zip(STEPS, out_refs):
+            out_ref[...] = out_rows[block_of(rank ^ step, out_ref.shape[0]), :]
+    else:
+        out_refs[0][...] = out_rows[...]
 
 
 def backward_kernel(grid_ref, *refs):
@@ -163,19 +181,33 @@
         kt_ref[part] = turn(identity, k_img[:, part]).astype(kt_ref.dtype)
     key_bias = jnp.where(iota((slot_rows, 1), 0) < length, 0.0, -1e30)
     dq_ref, dk_ref, dv_ref = grad_refs
-    for head in range(width // HEAD_DIM):
-        part = slice(head * HEAD_DIM, (head + 1) * HEAD_DIM)
-        qt, gt = qt_ref[part], gt_ref[part]
-        scores = dot(k_img[:, part], qt, 1, 0) * inv_root + key_bias
-        probs = jnp.exp(scores - lse_ref[head : head + 1])
-        grad_probs = dot(v_img[:, part], gt, 1, 0)
+    parts = [slice(at, at + HEAD_DIM) for at in range(0, width, HEAD_DIM)]
+    raws = {}
+    late = []
+
+    def finish():
+        part, probs, grad_scores = late.pop(0)
+        dq_ref[part] = dot(kt_ref[part], grad_scores, 1, 0).astype(dq_ref.dtype)
+        dk_ref[part] = dot(qt_ref[part], grad_scores, 1, 1).astype(dk_ref.dtype)
+        dv_ref[part] = dot(gt_ref[part], probs, 1, 1).astype(dv_ref.dtype)
+
+    for head, part in enumerate(parts):
+        for other in range(head, min(head + 1 + 1, len(parts))):
+            if other not in raws:
+                at = parts[other]
+                raws[other] = (dot(k_img[:, at], qt_ref[at], 1, 0), dot(v_img[:, at], gt_ref[at], 1, 0))
+        if len(late) > 0:
+            finish()
+        raw, grad_probs = raws.pop(head)
+        raws[head] = None
+        probs = jnp.exp(raw * inv_root + key_bias - lse_ref[head : head + 1])
         row_dot = jnp.sum(
-            gt.astype(jnp.float32) * ot_ref[part].astype(jnp.float32), axis=0, keepdims=True
+            gt_ref[part].astype(jnp.float32) * ot_ref[part].astype(jnp.float32), axis=0, keepdims=True
         )
         grad_scores = (probs * (grad_probs - row_dot) * inv_root).astype(jnp.bfloat16)
-        dq_ref[part] = dot(kt_ref[part], grad_scores, 1, 0).astype(dq_ref.dtype)
-        dk_ref[part] = dot(qt, grad_scores, 1, 1).astype(dk_ref.dtype)
-        dv_ref[part] = dot(gt, probs.astype(jnp.bfloat16), 1, 1).astype(dv_ref.dtype)
+        late.append((part, probs.astype(jnp.bfloat16), grad_scores))
+    while late:
+        finish()
     put_own = row_pick(slot_rows, part_rows, slot * part_rows, start, length, True)
     put_far = row_pick(slot_rows, part_rows, (1 - slot) * part_rows, start, length, True)
     for grad, own, far in zip(grad_refs, own_refs, far_refs):
@@ -237,29 +269,30 @@
     for x in (query_rows, key_rows, value_rows):
         rows += [x, swap(x)]
     grad_spread = spread(grad_hosted.reshape(ranks, block, width))
-    k_img, v_img, q_turned, out_turned, lse, attended = call(
+    k_img, v_img, q_turned, out_turned, lse, *attended = call(
         forward_kernel,
         (image_grid, *rows),
         [bf16(slot_rows, width)] * 2
         + [bf16(width, slot_rows)] * 2
         + [jax.ShapeDtypeStruct((heads, slot_rows), jnp.float32)]
-        + [bf16(slot_rows, width)],
+        + ([bf16(block, width)] * ranks if by_pairs else [bf16(slot_rows, width)]),
         LARGE,
         "attend",
-        scratch=[(slot_rows, width), (width, slot_rows)],
+        scratch=[(slot_rows, width), (width, slot_rows), (slot_rows, width)],
         work=2,
     )
     if by_pairs:
+        attended = exchange(attended)
         messages = call(
             to_lister_kernel,
-            (destination, attended, grad_spread),
-            [bf16(2 * block, width)] * ranks,
+            (destination, grad_spread),
+            [bf16(block, width)] * ranks,
             SMALL,
             "to_lister",
         )
         host_order, grad_slot = call(
             to_host_kernel,
-            (destination, *exchange(messages)),
+            (destination, *attended, *exchange(messages)),
             [bf16(ranks, block, width), bf16(slot_rows, width)],
             SMALL,
             "to_host",
@@ -280,7 +313,7 @@
             jnp.where(dest[None, :] == rank_ids[:, None], rank_ids[None, :], 0), axis=1
         )
         both = spread(
-            jnp.concatenate([grad_spread[dest], attended.reshape(ranks, block, width)], axis=1)
+            jnp.concatenate([grad_spread[dest], attended[0].reshape(ranks, block, width)], axis=1)
         )
         grad_slot = both[:, :block].reshape(slot_rows, width)
         hosted_out = spread(both[source, block:]).reshape(slot_rows, width)

time: 81.2 us -> 77.4 us (0.953)
  starting transfers between devices: 26.6 us -> 35.5 us
  waiting for transfers between devices: 27.9 us -> 20.1 us
  Pallas kernels: 18.7 us -> 14 us
    ppermute x7 -> x14, starting transfers between devices: 12.3 us -> 23.2 us  [exchange(): lax.ppermute(x, 'dp', [(rank, rank ^ step) for rank in range(ranks)])]
    ppermute x7 -> x14, waiting for transfers between devices: 15.8 us -> 9.5 us  [exchange(): lax.ppermute(x, 'dp', [(rank, rank ^ step) for rank in range(ranks)])]
    pallas_call x6, Pallas kernels: 18.7 us -> 14 us  [call(): pl.pallas_call(kernel, out_shape=outs, in_specs=[SMEM if x.dtype == jnp.i...]
    all_to_all x2, starting transfers between devices: 13 us -> 10.9 us  [spread(): return lax.all_to_all(x, 'dp', 0, 0, tiled=True)]
    all_to_all x2, waiting for transfers between devices: 6.49 us -> 5.02 us  [spread(): return lax.all_to_all(x, 'dp', 0, 0, tiled=True)]
    unnamed x22 -> x26, local copies, waits for them, and re-layouts: 6.58 us -> 6.54 us
  transfers between devices with their start and end apart: 15 -> 22, of which waited for: 12 -> 12; matrix products, arithmetic and copies ran while one was open for 0% -> 0% of each run, Pallas kernels for 19% -> 15%
where the time goes in v4:
time: 77.4 us; the launch traced here: 76.9 us
  starting transfers between devices  35.5 us (46%)
  waiting for transfers between devices  20.1 us (26%)
  Pallas kernels  14 us (18%)
  local copies, waits for them, and re-layouts  6.54 us (8%)
    ppermute x14, starting transfers between devices, exchange(): lax.ppermute(x, 'dp', [(rank, rank ^ step) for rank in range(ranks)])  23.2 us
    pallas_call x6, Pallas kernels, call(): pl.pallas_call(kernel, out_shape=outs, in_specs=[SMEM if x.dtype == jnp.i...  14 us
    all_to_all x2, starting transfers between devices, spread(): return lax.all_to_all(x, 'dp', 0, 0, tiled=True)  10.9 us
    ppermute x14, waiting for transfers between devices, exchange(): lax.ppermute(x, 'dp', [(rank, rank ^ step) for rank in range(ranks)])  9.5 us
    unnamed x26, local copies, waits for them, and re-layouts  6.54 us
    ppermute x6, waiting for transfers between devices, swap(): return lax.ppermute(x, 'seq', [(0, 1), (1, 0)])  5.56 us
    all_to_all x2, waiting for transfers between devices, spread(): return lax.all_to_all(x, 'dp', 0, 0, tiled=True)  5.02 us
  transfers between devices with their start and end apart: 22, of which 12 were waited for; matrix products, arithmetic and copies ran while one was open for 0% of the time, Pallas kernels for 15%

profile of v4, /device:TPU:0, one launch (start us, length us, event | category | flops | bytes accessed | tf_op | source)
XLA Modules:
  0.0 76.9 jit_solution(14732889315727995402)
XLA Ops:
  0.7 7.4 %all-to-all-start = ((bf16[8,32,1280]{2,1,0:T(8,128)(2,1)}), bf16[8,32,1280]{2,1,0:T(8,128)(2,1)S(1)}, u32[]{:S(2)}, u32[]{:S(2)}) async-start(bf16[8,32,1280]{2,1,0:T(8,128)(2,1)} %bitcast.7), calls=%async_computation | async-start | bytes 1310720 | tf_op jit(solution)/shard_map/all_to_all | solution.py:260
  8.1 0.1 collective-permute-start
  8.2 0.5 collective-permute-start.1
  8.6 0.1 collective-permute-start.2
  8.7 1.3 %collective-permute-done.refs_1_ = bf16[192,1280]{1,0:T(8,128)(2,1)S(1)} collective-permute-done((bf16[192,1280]{1,0:T(8,128)(2,1)S(1)}, bf16[192,1280]{1,0:T(8,128)(2,1)S(1)}, u32[]{:S(2)}, u32[]{:S(2)}) %collective-permute-start) | collective-permute-done | bytes 491552 | tf_op jit(solution)/shard_map/ppermute | solution.py:240
  10.0 1.4 %collective-permute-done.1.refs_3_ = bf16[192,1280]{1,0:T(8,128)(2,1)S(1)} collective-permute-done((bf16[192,1280]{1,0:T(8,128)(2,1)S(1)}, bf16[192,1280]{1,0:T(8,128)(2,1)S(1)}, u32[]{:S(2)}, u32[]{:S(2)}) %collective-permute-start.1) | collective-permute-done | bytes 491552 | tf_op jit(solution)/shard_map/ppermute | solution.py:240
  11.4 0.2 collective-permute-done.2.refs_5_
  11.6 1.0 %copy-done.3 = bf16[192,1280]{1,0:T(8,128)(2,1)S(1)} copy-done((bf16[192,1280]{1,0:T(8,128)(2,1)S(1)}, bf16[192,1280]{1,0:T(8,128)(2,1)}, u32[]{:S(2)}) %copy-start.3) | copy-done | bytes 491544
  12.6 1.0 %copy-done.5 = bf16[192,1280]{1,0:T(8,128)(2,1)S(1)} copy-done((bf16[192,1280]{1,0:T(8,128)(2,1)S(1)}, bf16[192,1280]{1,0:T(8,128)(2,1)}, u32[]{:S(2)}) %copy-start.5) | copy-done | bytes 491544
  13.7 1.0 %copy-done.6 = bf16[192,1280]{1,0:T(8,128)(2,1)S(1)} copy-done((bf16[192,1280]{1,0:T(8,128)(2,1)S(1)}, bf16[192,1280]{1,0:T(8,128)(2,1)}, u32[]{:S(2)}) %copy-start.6) | copy-done | bytes 491544
  14.7 4.8 %attend.1 = (bf16[256,1280]{1,0:T(8,128)(2,1)S(1)}, bf16[256,1280]{1,0:T(8,128)(2,1)S(1)}, bf16[1280,256]{1,0:T(8,128)(2,1)S(1)}, bf16[1280,256]{1,0:T(8,128)(2,...) custom-call(s32[2,2,8]{2,1,0:T(2,128)S(1)} %bitcast.3, ...), custom_call_target="tpu_custom_call" | custom-call | flops 335544320 | bytes 6242432 | tf_op jit(solution)/shard_map/attend/pallas_call | solution.py:243
  19.5 0.6 copy-done.9
  20.2 0.6 copy-done.11
  20.8 4.7 %collective-permute-start.3 = (bf16[32,1280]{1,0:T(8,128)(2,1)}, bf16[32,1280]{1,0:T(8,128)(2,1)S(1)}, u32[]{:S(2)}, u32[]{:S(2)}) collective-permute-start(bf16[32,1280]{1,0:T(8,128)(2,1)} %get-tuple-element.37), channel_id=1, source_target_pairs={{0,14},{2,12},{4,10},{6,8},{8,6},{10,4},{12,2},{14,0},{1,15},{3,13... | collective-permute-start | bytes 245768 | tf_op jit(solution)/shard_map/ppermute | solution.py:264
  25.5 0.6 collective-permute-start.4
  26.0 0.0 collective-permute-start.5
  26.0 2.0 %collective-permute-start.6 = (bf16[32,1280]{1,0:T(8,128)(2,1)}, bf16[32,1280]{1,0:T(8,128)(2,1)}, u32[]{:S(2)}, u32[]{:S(2)}) collective-permute-start(bf16[32,1280]{1,0:T(8,128)(2,1)} %get-tuple-element.40), channel_id=1, source_target_pairs={{0,10},{2,8},{4,14},{6,12},{8,2},{10,0},{12,6},{14,4},{1,11},{3,9}... | collective-permute-start | bytes 245768 | tf_op jit(solution)/shard_map/ppermute | solution.py:264
  28.0 0.9 %collective-permute-start.7 = (bf16[32,1280]{1,0:T(8,128)(2,1)}, bf16[32,1280]{1,0:T(8,128)(2,1)}, u32[]{:S(2)}, u32[]{:S(2)}) collective-permute-start(bf16[32,1280]{1,0:T(8,128)(2,1)} %get-tuple-element.41), channel_id=1, source_target_pairs={{0,6},{2,4},{4,2},{6,0},{8,14},{10,12},{12,10},{14,8},{1,7},{3,5},... | collective-permute-start | bytes 245768 | tf_op jit(solution)/shard_map/ppermute | solution.py:264
  28.9 0.0 all-to-all-done.in_ref
  29.0 0.6 to_lister.1
  29.6 0.0 collective-permute-done.3.refs_1_
  29.6 0.3 copy-done.12
  29.8 2.9 %collective-permute-start.8 = (bf16[32,1280]{1,0:T(8,128)(2,1)S(1)}, bf16[32,1280]{1,0:T(8,128)(2,1)S(1)}, u32[]{:S(2)}, u32[]{:S(2)}) collective-permute-start(bf16[32,1280]{1,0:T(8,128)(2,1)S(1)} %copy-done.12), channel_id=1, source_target_pairs={{0,8},{2,10},{4,12},{6,14},{8,0},{10,2},{12,4},{14,6},{1,9},{3,11}... | collective-permute-start | bytes 245768 | tf_op jit(solution)/shard_map/ppermute | solution.py:264
  32.8 0.8 %collective-permute-start.9 = (bf16[32,1280]{1,0:T(8,128)(2,1)S(1)}, bf16[32,1280]{1,0:T(8,128)(2,1)S(1)}, u32[]{:S(2)}, u32[]{:S(2)}) collective-permute-start(bf16[32,1280]{1,0:T(8,128)(2,1)S(1)} %copy-done.10), channel_id=1, source_target_pairs={{0,12},{2,14},{4,8},{6,10},{8,4},{10,6},{12,0},{14,2},{1,13},{3,15... | collective-permute-start | bytes 245768 | tf_op jit(solution)/shard_map/ppermute | solution.py:264
  33.6 3.9 %collective-permute-start.10 = (bf16[32,1280]{1,0:T(8,128)(2,1)S(1)}, bf16[32,1280]{1,0:T(8,128)(2,1)S(1)}, u32[]{:S(2)}, u32[]{:S(2)}) collective-permute-start(bf16[32,1280]{1,0:T(8,128)(2,1)S(1)} %get-tuple-element.45), channel_id=1, source_target_pairs={{0,14},{2,12},{4,10},{6,8},{8,6},{10,4},{12,2},{14,0},{1,15},{3,13... | collective-permute-start | bytes 245768 | tf_op jit(solution)/shard_map/ppermute | solution.py:264
  37.5 0.6 collective-permute-start.11
  38.1 3.7 %collective-permute-done.8.refs_6_ = bf16[32,1280]{1,0:T(8,128)(2,1)S(1)} collective-permute-done((bf16[32,1280]{1,0:T(8,128)(2,1)S(1)}, bf16[32,1280]{1,0:T(8,128)(2,1)S(1)}, u32[]{:S(2)}, u32[]{:S(2)}) %collective-permute-start.8) | collective-permute-done | bytes 81952 | tf_op jit(solution)/shard_map/ppermute | solution.py:264
  41.8 4.5 %collective-permute-start.14 = (bf16[32,1280]{1,0:T(8,128)(2,1)S(1)}, bf16[32,1280]{1,0:T(8,128)(2,1)S(1)}, u32[]{:S(2)}, u32[]{:S(2)}) collective-permute-start(bf16[32,1280]{1,0:T(8,128)(2,1)S(1)} %get-tuple-element.49), channel_id=1, source_target_pairs={{0,6},{2,4},{4,2},{6,0},{8,14},{10,12},{12,10},{14,8},{1,7},{3,5},... | collective-permute-start | bytes 245768 | tf_op jit(solution)/shard_map/ppermute | solution.py:264
  46.3 1.8 %collective-permute-start.15 = (bf16[32,1280]{1,0:T(8,128)(2,1)S(1)}, bf16[32,1280]{1,0:T(8,128)(2,1)S(1)}, u32[]{:S(2)}, u32[]{:S(2)}) collective-permute-start(bf16[32,1280]{1,0:T(8,128)(2,1)S(1)} %get-tuple-element.50), channel_id=1, source_target_pairs={{0,8},{2,10},{4,12},{6,14},{8,0},{10,2},{12,4},{14,6},{1,9},{3,11}... | collective-permute-start | bytes 245768 | tf_op jit(solution)/shard_map/ppermute | solution.py:264
  48.1 0.6 collective-permute-start.16
  48.7 1.4 %collective-permute-done.13.refs_12_ = bf16[32,1280]{1,0:T(8,128)(2,1)S(1)} collective-permute-done((bf16[32,1280]{1,0:T(8,128)(2,1)S(1)}, bf16[32,1280]{1,0:T(8,128)(2,1)S(1)}, u32[]{:S(2)}, u32[]{:S(2)}) %collective-permute-start.13) | collective-permute-done | bytes 81952 | tf_op jit(solution)/shard_map/ppermute | solution.py:264
  50.1 0.2 collective-permute-done.14.refs_13_
  50.3 3.0 %collective-permute-done.15.refs_14_ = bf16[32,1280]{1,0:T(8,128)(2,1)S(1)} collective-permute-done((bf16[32,1280]{1,0:T(8,128)(2,1)S(1)}, bf16[32,1280]{1,0:T(8,128)(2,1)S(1)}, u32[]{:S(2)}, u32[]{:S(2)}) %collective-permute-start.15) | collective-permute-done | bytes 81952 | tf_op jit(solution)/shard_map/ppermute | solution.py:264
  53.3 1.1 %collective-permute-done.16.refs_15_ = bf16[32,1280]{1,0:T(8,128)(2,1)S(1)} collective-permute-done((bf16[32,1280]{1,0:T(8,128)(2,1)S(1)}, bf16[32,1280]{1,0:T(8,128)(2,1)S(1)}, u32[]{:S(2)}, u32[]{:S(2)}) %collective-permute-start.16) | collective-permute-done | bytes 81952 | tf_op jit(solution)/shard_map/ppermute | solution.py:264
  54.5 1.9 %to_host.1 = (bf16[8,32,1280]{2,1,0:T(8,128)(2,1)}, bf16[256,1280]{1,0:T(8,128)(2,1)S(1)}) custom-call(s32[2,8]{1,0:T(2,128)S(1)} %bitcast.6, bf16[32,1280]{1,0:T(8,128)(2,1)S(1)} %get-tuple-element.36.refs_0_, bf16[32,1280]{1,0:T(8,128)(2,1)S(1)} %collective-permute-done.3.refs_1_, bf16[32,1280]{1,0:T(8,128)(2,1)S(1)} %collective-permute-done.4.refs_2_, ...), custom_call_target="tpu_custom_call" | custom-call | flops 1 | bytes 2621504 | tf_op jit(solution)/shard_map/to_host/pallas_call | solution.py:243
  56.4 0.8 %copy-done = bf16[256,1280]{1,0:T(8,128)(2,1)} copy-done((bf16[256,1280]{1,0:T(8,128)(2,1)}, bf16[256,1280]{1,0:T(8,128)(2,1)S(1)}, u32[]{:S(2)}) %copy-start) | copy-done | bytes 655384
  57.2 3.5 %all-to-all-start.1 = ((bf16[8,32,1280]{2,1,0:T(8,128)(2,1)}), bf16[8,32,1280]{2,1,0:T(8,128)(2,1)S(1)}, u32[]{:S(2)}, u32[]{:S(2)}) async-start(bf16[8,32,1280]{2,1,0:T(8,128)(2,1)} %get-tuple-element.52), calls=%async_computation.1 | async-start | bytes 1310720 | tf_op jit(solution)/shard_map/all_to_all | solution.py:260
  60.8 1.1 %copy-done.1 = bf16[256,1280]{1,0:T(8,128)(2,1)S(1)} copy-done((bf16[256,1280]{1,0:T(8,128)(2,1)S(1)}, bf16[256,1280]{1,0:T(8,128)(2,1)}, u32[]{:S(2)}) %copy-start.1) | copy-done | bytes 655384
  61.9 4.6 %attend_back.1 = (bf16[192,1280]{1,0:T(8,128)(2,1)S(1)}, bf16[192,1280]{1,0:T(8,128)(2,1)S(1)}, bf16[192,1280]{1,0:T(8,128)(2,1)S(1)}, bf16[192,1280]{1,0:T(8,12...) custom-call(s32[2,2,8]{2,1,0:T(2,128)S(1)} %bitcast.4, ...), custom_call_target="tpu_custom_call" | custom-call | flops 838860800 | bytes 6242432 | tf_op jit(solution)/shard_map/attend_back/pallas_call | solution.py:243
  66.5 0.1 collective-permute-start.17
  66.5 0.5 collective-permute-start.18
  67.0 0.1 collective-permute-start.19
  67.1 1.3 %collective-permute-done.17.refs_3_ = bf16[192,1280]{1,0:T(8,128)(2,1)S(1)} collective-permute-done((bf16[192,1280]{1,0:T(8,128)(2,1)S(1)}, bf16[192,1280]{1,0:T(8,128)(2,1)S(1)}, u32[]{:S(2)}, u32[]{:S(2)}) %collective-permute-start.17) | collective-permute-done | bytes 491552 | tf_op jit(solution)/shard_map/ppermute | solution.py:240
  68.4 0.7 collective-permute-done.18.refs_4_
  69.1 0.7 collective-permute-done.19.refs_5_
  69.8 1.2 %join.1 = (bf16[192,1280]{1,0:T(8,128)(2,1)}, bf16[192,1280]{1,0:T(8,128)(2,1)}, bf16[192,1280]{1,0:T(8,128)(2,1)}) custom-call(bf16[192,1280]{1,0:T(8,128)(2,1)S(1)} %get-tuple-element.59.refs_0_, bf16[192,1280]{1,0:T(8,128)(2,1)S(1)} %get-tuple-element.60.refs_1_, bf16[192,1280]{1,0:T(8,128)(2,1)S(1)} %get-tuple-element.61.refs_2_, ...), custom_call_target="tpu_custom_call" | custom-call | flops 1 | bytes 4423680 | tf_op jit(solution)/shard_map/join/pallas_call | solution.py:243
  71.0 5.0 %all-to-all-done.1.in_ref = bf16[8,32,1280]{2,1,0:T(8,128)(2,1)S(1)} async-done(((bf16[8,32,1280]{2,1,0:T(8,128)(2,1)}), bf16[8,32,1280]{2,1,0:T(8,128)(2,1)S(1)}, u32[]{:S(2)}, u32[]{:S(2)}) %all-to-all-start.1) | async-done | bytes 655392 | tf_op jit(solution)/shard_map/all_to_all | solution.py:260
  76.0 0.9 %store.1 = bf16[256,1280]{1,0:T(8,128)(2,1)} custom-call(bf16[8,32,1280]{2,1,0:T(8,128)(2,1)S(1)} %all-to-all-done.1.in_ref), custom_call_target="tpu_custom_call" | custom-call | flops 1 | bytes 1310720 | tf_op jit(solution)/shard_map/store/pallas_call | solution.py:243
  (28 shorter events, 0.1 us)
Async XLA Ops:
  0.6 7.4 %copy-start.2 = (bf16[192,1280]{1,0:T(8,128)(2,1)S(1)}, bf16[192,1280]{1,0:T(8,128)(2,1)}, u32[]{:S(2)}) copy-start(bf16[192,1280]{1,0:T(8,128)(2,1)} %refs_0_.1) | copy-start | bytes 1474564
  0.6 7.5 %copy-start.4 = (bf16[192,1280]{1,0:T(8,128)(2,1)S(1)}, bf16[192,1280]{1,0:T(8,128)(2,1)}, u32[]{:S(2)}) copy-start(bf16[192,1280]{1,0:T(8,128)(2,1)} %refs_2_.1) | copy-start | bytes 1474564
  0.7 11.0 %copy-start.7 = (s32[8,2,2]{0,2,1:T(2,128)S(1)}, s32[8,2,2]{0,2,1:T(2,128)}, u32[]{:S(2)}) copy-start(s32[8,2,2]{0,2,1:T(2,128)} %param.10) | copy-start | bytes 388
  0.7 28.3 %all-to-all-start = ((bf16[8,32,1280]{2,1,0:T(8,128)(2,1)}), bf16[8,32,1280]{2,1,0:T(8,128)(2,1)S(1)}, u32[]{:S(2)}, u32[]{:S(2)}) async-start(bf16[8,32,1280]{2,1,0:T(8,128)(2,1)} %bitcast.7), calls=%async_computation | async-start | bytes 1310720 | tf_op jit(solution)/shard_map/all_to_all | solution.py:260
  8.1 1.9 %collective-permute-start = (bf16[192,1280]{1,0:T(8,128)(2,1)S(1)}, bf16[192,1280]{1,0:T(8,128)(2,1)S(1)}, u32[]{:S(2)}, u32[]{:S(2)}) collective-permute-start(bf16[192,1280]{1,0:T(8,128)(2,1)S(1)} %copy-done.2), channel_id=1, source_target_pairs={{0,1},{1,0},{2,3},{3,2},{4,5},{5,4},{6,7},{7,6},{8,9},{9,8},{10,11... | collective-permute-start | bytes 1474568 | tf_op jit(solution)/shard_map/ppermute | solution.py:240
  8.2 3.2 %collective-permute-start.1 = (bf16[192,1280]{1,0:T(8,128)(2,1)S(1)}, bf16[192,1280]{1,0:T(8,128)(2,1)S(1)}, u32[]{:S(2)}, u32[]{:S(2)}) collective-permute-start(bf16[192,1280]{1,0:T(8,128)(2,1)S(1)} %copy-done.4), channel_id=1, source_target_pairs={{0,1},{1,0},{2,3},{3,2},{4,5},{5,4},{6,7},{7,6},{8,9},{9,8},{10,11... | collective-permute-start | bytes 1474568 | tf_op jit(solution)/shard_map/ppermute | solution.py:240
  8.6 3.0 %collective-permute-start.2 = (bf16[192,1280]{1,0:T(8,128)(2,1)}, bf16[192,1280]{1,0:T(8,128)(2,1)S(1)}, u32[]{:S(2)}, u32[]{:S(2)}) collective-permute-start(bf16[192,1280]{1,0:T(8,128)(2,1)} %refs_4_.1), channel_id=1, source_target_pairs={{0,1},{1,0},{2,3},{3,2},{4,5},{5,4},{6,7},{7,6},{8,9},{9,8},{10,11... | collective-permute-start | bytes 1474568 | tf_op jit(solution)/shard_map/ppermute | solution.py:240
  11.6 1.0 %copy-start.3 = (bf16[192,1280]{1,0:T(8,128)(2,1)S(1)}, bf16[192,1280]{1,0:T(8,128)(2,1)}, u32[]{:S(2)}) copy-start(bf16[192,1280]{1,0:T(8,128)(2,1)} %refs_0_.1) | copy-start | bytes 1474564
  12.6 1.0 %copy-start.5 = (bf16[192,1280]{1,0:T(8,128)(2,1)S(1)}, bf16[192,1280]{1,0:T(8,128)(2,1)}, u32[]{:S(2)}) copy-start(bf16[192,1280]{1,0:T(8,128)(2,1)} %refs_2_.1) | copy-start | bytes 1474564
  13.7 1.0 %copy-start.6 = (bf16[192,1280]{1,0:T(8,128)(2,1)S(1)}, bf16[192,1280]{1,0:T(8,128)(2,1)}, u32[]{:S(2)}) copy-start(bf16[192,1280]{1,0:T(8,128)(2,1)} %refs_4_.1) | copy-start | bytes 1474564
  19.5 0.6 copy-start.9
  20.2 0.6 copy-start.11
  20.8 8.8 %collective-permute-start.3 = (bf16[32,1280]{1,0:T(8,128)(2,1)}, bf16[32,1280]{1,0:T(8,128)(2,1)S(1)}, u32[]{:S(2)}, u32[]{:S(2)}) collective-permute-start(bf16[32,1280]{1,0:T(8,128)(2,1)} %get-tuple-element.37), channel_id=1, source_target_pairs={{0,14},{2,12},{4,10},{6,8},{8,6},{10,4},{12,2},{14,0},{1,15},{3,13... | collective-permute-start | bytes 245768 | tf_op jit(solution)/shard_map/ppermute | solution.py:264
  25.5 7.3 %collective-permute-start.4 = (bf16[32,1280]{1,0:T(8,128)(2,1)}, bf16[32,1280]{1,0:T(8,128)(2,1)S(1)}, u32[]{:S(2)}, u32[]{:S(2)}) collective-permute-start(bf16[32,1280]{1,0:T(8,128)(2,1)} %get-tuple-element.38), channel_id=1, source_target_pairs={{0,2},{2,0},{4,6},{6,4},{8,10},{10,8},{12,14},{14,12},{1,3},{3,1},... | collective-permute-start | bytes 245768 | tf_op jit(solution)/shard_map/ppermute | solution.py:264
  26.0 7.6 %collective-permute-start.5 = (bf16[32,1280]{1,0:T(8,128)(2,1)}, bf16[32,1280]{1,0:T(8,128)(2,1)}, u32[]{:S(2)}, u32[]{:S(2)}) collective-permute-start(bf16[32,1280]{1,0:T(8,128)(2,1)} %get-tuple-element.39), channel_id=1, source_target_pairs={{0,4},{2,6},{4,0},{6,2},{8,12},{10,14},{12,8},{14,10},{1,5},{3,7},... | collective-permute-start | bytes 245768 | tf_op jit(solution)/shard_map/ppermute | solution.py:264
  26.0 11.5 %collective-permute-start.6 = (bf16[32,1280]{1,0:T(8,128)(2,1)}, bf16[32,1280]{1,0:T(8,128)(2,1)}, u32[]{:S(2)}, u32[]{:S(2)}) collective-permute-start(bf16[32,1280]{1,0:T(8,128)(2,1)} %get-tuple-element.40), channel_id=1, source_target_pairs={{0,10},{2,8},{4,14},{6,12},{8,2},{10,0},{12,6},{14,4},{1,11},{3,9}... | collective-permute-start | bytes 245768 | tf_op jit(solution)/shard_map/ppermute | solution.py:264
  28.0 0.9 %copy-start.8 = (s32[8,2]{0,1:T(2,128)S(1)}, s32[8,2]{0,1:T(2,128)}, u32[]{:S(2)}) copy-start(s32[8,2]{0,1:T(2,128)} %param.11) | copy-start | bytes 196
  28.0 10.0 %collective-permute-start.7 = (bf16[32,1280]{1,0:T(8,128)(2,1)}, bf16[32,1280]{1,0:T(8,128)(2,1)}, u32[]{:S(2)}, u32[]{:S(2)}) collective-permute-start(bf16[32,1280]{1,0:T(8,128)(2,1)} %get-tuple-element.41), channel_id=1, source_target_pairs={{0,6},{2,4},{4,2},{6,0},{8,14},{10,12},{12,10},{14,8},{1,7},{3,5},... | collective-permute-start | bytes 245768 | tf_op jit(solution)/shard_map/ppermute | solution.py:264
  29.0 0.9 %copy-start.12 = (bf16[32,1280]{1,0:T(8,128)(2,1)S(1)}, bf16[32,1280]{1,0:T(8,128)(2,1)}, u32[]{:S(2)}) copy-start(bf16[32,1280]{1,0:T(8,128)(2,1)} %copy-done.11) | copy-start | bytes 245764
  29.0 3.8 %copy-start.10 = (bf16[32,1280]{1,0:T(8,128)(2,1)S(1)}, bf16[32,1280]{1,0:T(8,128)(2,1)}, u32[]{:S(2)}) copy-start(bf16[32,1280]{1,0:T(8,128)(2,1)} %copy-done.9) | copy-start | bytes 245764
  29.8 12.0 %collective-permute-start.8 = (bf16[32,1280]{1,0:T(8,128)(2,1)S(1)}, bf16[32,1280]{1,0:T(8,128)(2,1)S(1)}, u32[]{:S(2)}, u32[]{:S(2)}) collective-permute-start(bf16[32,1280]{1,0:T(8,128)(2,1)S(1)} %copy-done.12), channel_id=1, source_target_pairs={{0,8},{2,10},{4,12},{6,14},{8,0},{10,2},{12,4},{14,6},{1,9},{3,11}... | collective-permute-start | bytes 245768 | tf_op jit(solution)/shard_map/ppermute | solution.py:264
  32.8 9.0 %collective-permute-start.9 = (bf16[32,1280]{1,0:T(8,128)(2,1)S(1)}, bf16[32,1280]{1,0:T(8,128)(2,1)S(1)}, u32[]{:S(2)}, u32[]{:S(2)}) collective-permute-start(bf16[32,1280]{1,0:T(8,128)(2,1)S(1)} %copy-done.10), channel_id=1, source_target_pairs={{0,12},{2,14},{4,8},{6,10},{8,4},{10,6},{12,0},{14,2},{1,13},{3,15... | collective-permute-start | bytes 245768 | tf_op jit(solution)/shard_map/ppermute | solution.py:264
  33.6 12.7 %collective-permute-start.10 = (bf16[32,1280]{1,0:T(8,128)(2,1)S(1)}, bf16[32,1280]{1,0:T(8,128)(2,1)S(1)}, u32[]{:S(2)}, u32[]{:S(2)}) collective-permute-start(bf16[32,1280]{1,0:T(8,128)(2,1)S(1)} %get-tuple-element.45), channel_id=1, source_target_pairs={{0,14},{2,12},{4,10},{6,8},{8,6},{10,4},{12,2},{14,0},{1,15},{3,13... | collective-permute-start | bytes 245768 | tf_op jit(solution)/shard_map/ppermute | solution.py:264
  37.5 10.6 %collective-permute-start.11 = (bf16[32,1280]{1,0:T(8,128)(2,1)S(1)}, bf16[32,1280]{1,0:T(8,128)(2,1)S(1)}, u32[]{:S(2)}, u32[]{:S(2)}) collective-permute-start(bf16[32,1280]{1,0:T(8,128)(2,1)S(1)} %get-tuple-element.46), channel_id=1, source_target_pairs={{0,2},{2,0},{4,6},{6,4},{8,10},{10,8},{12,14},{14,12},{1,3},{3,1},... | collective-permute-start | bytes 245768 | tf_op jit(solution)/shard_map/ppermute | solution.py:264
  38.1 10.6 %collective-permute-start.12 = (bf16[32,1280]{1,0:T(8,128)(2,1)S(1)}, bf16[32,1280]{1,0:T(8,128)(2,1)S(1)}, u32[]{:S(2)}, u32[]{:S(2)}) collective-permute-start(bf16[32,1280]{1,0:T(8,128)(2,1)S(1)} %get-tuple-element.47), channel_id=1, source_target_pairs={{0,4},{2,6},{4,0},{6,2},{8,12},{10,14},{12,8},{14,10},{1,5},{3,7},... | collective-permute-start | bytes 245768 | tf_op jit(solution)/shard_map/ppermute | solution.py:264
  41.8 8.3 %collective-permute-start.13 = (bf16[32,1280]{1,0:T(8,128)(2,1)S(1)}, bf16[32,1280]{1,0:T(8,128)(2,1)S(1)}, u32[]{:S(2)}, u32[]{:S(2)}) collective-permute-start(bf16[32,1280]{1,0:T(8,128)(2,1)S(1)} %get-tuple-element.48), channel_id=1, source_target_pairs={{0,10},{2,8},{4,14},{6,12},{8,2},{10,0},{12,6},{14,4},{1,11},{3,9}... | collective-permute-start | bytes 245768 | tf_op jit(solution)/shard_map/ppermute | solution.py:264
  41.8 8.5 %collective-permute-start.14 = (bf16[32,1280]{1,0:T(8,128)(2,1)S(1)}, bf16[32,1280]{1,0:T(8,128)(2,1)S(1)}, u32[]{:S(2)}, u32[]{:S(2)}) collective-permute-start(bf16[32,1280]{1,0:T(8,128)(2,1)S(1)} %get-tuple-element.49), channel_id=1, source_target_pairs={{0,6},{2,4},{4,2},{6,0},{8,14},{10,12},{12,10},{14,8},{1,7},{3,5},... | collective-permute-start | bytes 245768 | tf_op jit(solution)/shard_map/ppermute | solution.py:264
  46.3 7.0 %collective-permute-start.15 = (bf16[32,1280]{1,0:T(8,128)(2,1)S(1)}, bf16[32,1280]{1,0:T(8,128)(2,1)S(1)}, u32[]{:S(2)}, u32[]{:S(2)}) collective-permute-start(bf16[32,1280]{1,0:T(8,128)(2,1)S(1)} %get-tuple-element.50), channel_id=1, source_target_pairs={{0,8},{2,10},{4,12},{6,14},{8,0},{10,2},{12,4},{14,6},{1,9},{3,11}... | collective-permute-start | bytes 245768 | tf_op jit(solution)/shard_map/ppermute | solution.py:264
  48.1 6.3 %collective-permute-start.16 = (bf16[32,1280]{1,0:T(8,128)(2,1)S(1)}, bf16[32,1280]{1,0:T(8,128)(2,1)S(1)}, u32[]{:S(2)}, u32[]{:S(2)}) collective-permute-start(bf16[32,1280]{1,0:T(8,128)(2,1)S(1)} %get-tuple-element.51), channel_id=1, source_target_pairs={{0,12},{2,14},{4,8},{6,10},{8,4},{10,6},{12,0},{14,2},{1,13},{3,15... | collective-permute-start | bytes 245768 | tf_op jit(solution)/shard_map/ppermute | solution.py:264
  56.4 0.9 %copy-start = (bf16[256,1280]{1,0:T(8,128)(2,1)}, bf16[256,1280]{1,0:T(8,128)(2,1)S(1)}, u32[]{:S(2)}) copy-start(bf16[256,1280]{1,0:T(8,128)(2,1)S(1)} %get-tuple-element.58.refs_5_) | copy-start | bytes 1966084
  57.2 18.8 %all-to-all-start.1 = ((bf16[8,32,1280]{2,1,0:T(8,128)(2,1)}), bf16[8,32,1280]{2,1,0:T(8,128)(2,1)S(1)}, u32[]{:S(2)}, u32[]{:S(2)}) async-start(bf16[8,32,1280]{2,1,0:T(8,128)(2,1)} %get-tuple-element.52), calls=%async_computation.1 | async-start | bytes 1310720 | tf_op jit(solution)/shard_map/all_to_all | solution.py:260
  60.8 1.1 %copy-start.1 = (bf16[256,1280]{1,0:T(8,128)(2,1)S(1)}, bf16[256,1280]{1,0:T(8,128)(2,1)}, u32[]{:S(2)}) copy-start(bf16[256,1280]{1,0:T(8,128)(2,1)} %copy-done) | copy-start | bytes 1966084
  66.5 1.9 %collective-permute-start.17 = (bf16[192,1280]{1,0:T(8,128)(2,1)S(1)}, bf16[192,1280]{1,0:T(8,128)(2,1)S(1)}, u32[]{:S(2)}, u32[]{:S(2)}) collective-permute-start(bf16[192,1280]{1,0:T(8,128)(2,1)S(1)} %get-tuple-element.62), channel_id=1, source_target_pairs={{0,1},{1,0},{2,3},{3,2},{4,5},{5,4},{6,7},{7,6},{8,9},{9,8},{10,11... | collective-permute-start | bytes 1474568 | tf_op jit(solution)/shard_map/ppermute | solution.py:240
  66.5 2.6 %collective-permute-start.18 = (bf16[192,1280]{1,0:T(8,128)(2,1)S(1)}, bf16[192,1280]{1,0:T(8,128)(2,1)S(1)}, u32[]{:S(2)}, u32[]{:S(2)}) collective-permute-start(bf16[192,1280]{1,0:T(8,128)(2,1)S(1)} %get-tuple-element.63), channel_id=1, source_target_pairs={{0,1},{1,0},{2,3},{3,2},{4,5},{5,4},{6,7},{7,6},{8,9},{9,8},{10,11... | collective-permute-start | bytes 1474568 | tf_op jit(solution)/shard_map/ppermute | solution.py:240
  67.0 2.8 %collective-permute-start.19 = (bf16[192,1280]{1,0:T(8,128)(2,1)S(1)}, bf16[192,1280]{1,0:T(8,128)(2,1)S(1)}, u32[]{:S(2)}, u32[]{:S(2)}) collective-permute-start(bf16[192,1280]{1,0:T(8,128)(2,1)S(1)} %get-tuple-element.64), channel_id=1, source_target_pairs={{0,1},{1,0},{2,3},{3,2},{4,5},{5,4},{6,7},{7,6},{8,9},{9,8},{10,11... | collective-permute-start | bytes 1474568 | tf_op jit(solution)/shard_map/ppermute | solution.py:240

commit v5 on v4

--- a/solution.py
+++ b/solution.py
@@ -9,6 +9,7 @@
 HEAD_DIM = 80
 STRIP = 256
 STEPS = (0, 7, 1, 2, 5, 3, 4, 6)
+LAST = 2
 LARGE = pltpu.CompilerParams(vmem_limit_bytes=12 * 1024 * 1024)
 SMALL = pltpu.CompilerParams(vmem_limit_bytes=6 * 1024 * 1024)
 SMEM = pl.BlockSpec(memory_space=pltpu.SMEM)
@@ -78,11 +79,14 @@
     rank = lax.axis_index("dp")
     slot = lax.axis_index("seq")
     count = len(STEPS)
-    out_ref, grad_ref = refs[-2:]
+    o_refs, g_refs, (out_ref, grad_ref) = refs[:count], refs[count:-2], refs[-2:]
     rows = out_ref.shape[1]
-    for step, o_ref, g_ref in zip(STEPS, refs[:count], refs[count : 2 * count]):
+    for step, o_ref in zip(STEPS, o_refs):
         out_ref[dest_ref[slot, rank ^ step]] = o_ref[...]
+    for step, g_ref in zip(STEPS, g_refs):
         grad_ref[block_of(rank ^ step, rows), :] = g_ref[...]
+    for step in STEPS[len(g_refs) :]:
+        grad_ref[block_of(rank ^ step, rows), :] = jnp.zeros((rows, grad_ref.shape[1]), jnp.bfloat16)
 
 
 def store_kernel(in_ref, hbm_ref, sems):
@@ -167,7 +171,12 @@
 
 def backward_kernel(grid_ref, *refs):
     (k_img, v_img, qt_ref, ot_ref, lse_ref), refs = refs[:5], refs[5:]
-    g_img, own_refs, far_refs, (gt_ref, kt_ref, *grad_refs) = refs[0], refs[1:4], refs[4:7], refs[7:]
+    (g_ref, *last_refs), refs = refs[:-12], refs[-12:]
+    own_refs, far_refs, (g_img, gt_ref, kt_ref, *grad_refs) = refs[:3], refs[3:6], refs[6:]
+    g_img[...] = g_ref[...]
+    for step, last_ref in zip(STEPS[-LAST:], last_refs):
+        to = lax.axis_index("dp") ^ step
+        g_img[block_of(to, last_ref.shape[0]), :] = last_ref[...]
     rank = lax.axis_index("dp")
     slot = lax.axis_index("seq")
     start, length = image_place(grid_ref, rank, slot)
@@ -290,13 +299,15 @@
             SMALL,
             "to_lister",
         )
+        grad_blocks = exchange(messages)
         host_order, grad_slot = call(
             to_host_kernel,
-            (destination, *attended, *exchange(messages)),
+            (destination, *attended, *grad_blocks[:-LAST]),
             [bf16(ranks, block, width), bf16(slot_rows, width)],
             SMALL,
             "to_host",
         )
+        host_order, *last = lax.optimization_barrier((host_order, *grad_blocks[-LAST:]))
         (hosted_out,) = call(
             store_kernel,
             (spread(host_order),),
@@ -315,15 +326,15 @@
         both = spread(
             jnp.concatenate([grad_spread[dest], attended[0].reshape(ranks, block, width)], axis=1)
         )
-        grad_slot = both[:, :block].reshape(slot_rows, width)
+        grad_slot, last = both[:, :block].reshape(slot_rows, width), []
         hosted_out = spread(both[source, block:]).reshape(slot_rows, width)
     grads = call(
         backward_kernel,
-        (image_grid, k_img, v_img, q_turned, out_turned, lse, grad_slot),
+        (image_grid, k_img, v_img, q_turned, out_turned, lse, grad_slot, *last),
         [bf16(part_rows, width)] * 6,
         LARGE,
         "attend_back",
-        scratch=[(width, slot_rows)] * 5,
+        scratch=[(slot_rows, width)] + [(width, slot_rows)] * 5,
         work=5,
     )
     grad_query, grad_key, grad_value = call(

time: 77.4 us -> 75.9 us (0.981)
  waiting for transfers between devices: 20.1 us -> 11.9 us
  starting transfers between devices: 35.5 us -> 39.3 us
  local copies, waits for them, and re-layouts: 6.54 us -> 9.32 us
    ppermute x14, waiting for transfers between devices: 9.5 us -> 2.16 us  [exchange(): lax.ppermute(x, 'dp', [(rank, rank ^ step) for rank in range(ranks)])]
    unnamed x26 -> x34, local copies, waits for them, and re-layouts: 6.54 us -> 9.32 us
    ppermute x14, starting transfers between devices: 23.2 us -> 25.5 us  [exchange(): lax.ppermute(x, 'dp', [(rank, rank ^ step) for rank in range(ranks)])]
    all_to_all x2, starting transfers between devices: 10.9 us -> 12.6 us  [spread(): return lax.all_to_all(x, 'dp', 0, 0, tiled=True)]
    all_to_all x2, waiting for transfers between devices: 5.02 us -> 4.16 us  [spread(): return lax.all_to_all(x, 'dp', 0, 0, tiled=True)]
  transfers between devices with their start and end apart: 22 -> 22, of which waited for: 12 -> 9; matrix products, arithmetic and copies ran while one was open for 0% -> 0% of each run, Pallas kernels for 15% -> 17%
where the time goes in v5:
time: 75.9 us; the launch traced here: 75.3 us
  starting transfers between devices  39.3 us (52%)
  Pallas kernels  14 us (18%)
  waiting for transfers between devices  11.9 us (16%)
  local copies, waits for them, and re-layouts  9.32 us (12%)
  between operations  0.77 us (1%)
    ppermute x14, starting transfers between devices, exchange(): lax.ppermute(x, 'dp', [(rank, rank ^ step) for rank in range(ranks)])  25.5 us
    pallas_call x6, Pallas kernels, call(): pl.pallas_call(kernel, out_shape=outs, in_specs=[SMEM if x.dtype == jnp.i...  14 us
    all_to_all x2, starting transfers between devices, spread(): return lax.all_to_all(x, 'dp', 0, 0, tiled=True)  12.6 us
    unnamed x34, local copies, waits for them, and re-layouts  9.32 us
    ppermute x6, waiting for transfers between devices, swap(): return lax.ppermute(x, 'seq', [(0, 1), (1, 0)])  5.56 us
    all_to_all x2, waiting for transfers between devices, spread(): return lax.all_to_all(x, 'dp', 0, 0, tiled=True)  4.16 us
    ppermute x14, waiting for transfers between devices, exchange(): lax.ppermute(x, 'dp', [(rank, rank ^ step) for rank in range(ranks)])  2.16 us
  transfers between devices with their start and end apart: 22, of which 9 were waited for; matrix products, arithmetic and copies ran while one was open for 0% of the time, Pallas kernels for 17%

profile of v5, /device:TPU:0, one launch (start us, length us, event | category | flops | bytes accessed | tf_op | source)
XLA Modules:
  0.0 75.3 jit_solution(14222023571592193792)
XLA Ops:
  0.7 7.4 %all-to-all-start = ((bf16[8,32,1280]{2,1,0:T(8,128)(2,1)}), bf16[8,32,1280]{2,1,0:T(8,128)(2,1)S(1)}, u32[]{:S(2)}, u32[]{:S(2)}) async-start(bf16[8,32,1280]{2,1,0:T(8,128)(2,1)} %bitcast.7), calls=%async_computation | async-start | bytes 1310720 | tf_op jit(solution)/shard_map/all_to_all | solution.py:269
  8.1 0.1 collective-permute-start
  8.2 0.5 collective-permute-start.1
  8.6 0.1 collective-permute-start.2
  8.7 1.3 %collective-permute-done.refs_1_ = bf16[192,1280]{1,0:T(8,128)(2,1)S(1)} collective-permute-done((bf16[192,1280]{1,0:T(8,128)(2,1)S(1)}, bf16[192,1280]{1,0:T(8,128)(2,1)S(1)}, u32[]{:S(2)}, u32[]{:S(2)}) %collective-permute-start) | collective-permute-done | bytes 491552 | tf_op jit(solution)/shard_map/ppermute | solution.py:249
  10.0 1.4 %collective-permute-done.1.refs_3_ = bf16[192,1280]{1,0:T(8,128)(2,1)S(1)} collective-permute-done((bf16[192,1280]{1,0:T(8,128)(2,1)S(1)}, bf16[192,1280]{1,0:T(8,128)(2,1)S(1)}, u32[]{:S(2)}, u32[]{:S(2)}) %collective-permute-start.1) | collective-permute-done | bytes 491552 | tf_op jit(solution)/shard_map/ppermute | solution.py:249
  11.4 0.2 collective-permute-done.2.refs_5_
  11.6 1.0 %copy-done.3 = bf16[192,1280]{1,0:T(8,128)(2,1)S(1)} copy-done((bf16[192,1280]{1,0:T(8,128)(2,1)S(1)}, bf16[192,1280]{1,0:T(8,128)(2,1)}, u32[]{:S(2)}) %copy-start.3) | copy-done | bytes 491544
  12.6 1.0 %copy-done.5 = bf16[192,1280]{1,0:T(8,128)(2,1)S(1)} copy-done((bf16[192,1280]{1,0:T(8,128)(2,1)S(1)}, bf16[192,1280]{1,0:T(8,128)(2,1)}, u32[]{:S(2)}) %copy-start.5) | copy-done | bytes 491544
  13.7 1.0 %copy-done.6 = bf16[192,1280]{1,0:T(8,128)(2,1)S(1)} copy-done((bf16[192,1280]{1,0:T(8,128)(2,1)S(1)}, bf16[192,1280]{1,0:T(8,128)(2,1)}, u32[]{:S(2)}) %copy-start.6) | copy-done | bytes 491544
  14.7 4.8 %attend.1 = (bf16[256,1280]{1,0:T(8,128)(2,1)S(1)}, bf16[256,1280]{1,0:T(8,128)(2,1)S(1)}, bf16[1280,256]{1,0:T(8,128)(2,1)S(1)}, bf16[1280,256]{1,0:T(8,128)(2,...) custom-call(s32[2,2,8]{2,1,0:T(2,128)S(1)} %bitcast.3, ...), custom_call_target="tpu_custom_call" | custom-call | flops 335544320 | bytes 6242432 | tf_op jit(solution)/shard_map/attend/pallas_call | solution.py:252
  19.5 0.6 copy-done.13
  20.2 0.6 copy-done.15
  20.8 4.7 %collective-permute-start.3 = (bf16[32,1280]{1,0:T(8,128)(2,1)}, bf16[32,1280]{1,0:T(8,128)(2,1)S(1)}, u32[]{:S(2)}, u32[]{:S(2)}) collective-permute-start(bf16[32,1280]{1,0:T(8,128)(2,1)} %get-tuple-element.40), channel_id=1, source_target_pairs={{0,14},{2,12},{4,10},{6,8},{8,6},{10,4},{12,2},{14,0},{1,15},{3,13... | collective-permute-start | bytes 245768 | tf_op jit(solution)/shard_map/ppermute | solution.py:273
  25.5 0.6 collective-permute-start.4
  26.0 0.0 collective-permute-start.5
  26.0 2.0 %collective-permute-start.6 = (bf16[32,1280]{1,0:T(8,128)(2,1)}, bf16[32,1280]{1,0:T(8,128)(2,1)}, u32[]{:S(2)}, u32[]{:S(2)}) collective-permute-start(bf16[32,1280]{1,0:T(8,128)(2,1)} %get-tuple-element.43), channel_id=1, source_target_pairs={{0,10},{2,8},{4,14},{6,12},{8,2},{10,0},{12,6},{14,4},{1,11},{3,9}... | collective-permute-start | bytes 245768 | tf_op jit(solution)/shard_map/ppermute | solution.py:273
  28.1 0.9 %collective-permute-start.7 = (bf16[32,1280]{1,0:T(8,128)(2,1)}, bf16[32,1280]{1,0:T(8,128)(2,1)}, u32[]{:S(2)}, u32[]{:S(2)}) collective-permute-start(bf16[32,1280]{1,0:T(8,128)(2,1)} %get-tuple-element.44), channel_id=1, source_target_pairs={{0,6},{2,4},{4,2},{6,0},{8,14},{10,12},{12,10},{14,8},{1,7},{3,5},... | collective-permute-start | bytes 245768 | tf_op jit(solution)/shard_map/ppermute | solution.py:273
  29.0 0.6 to_lister.1
  29.6 0.0 copy-start.7
  29.6 0.6 copy-done.7
  30.2 2.9 %collective-permute-start.8 = (bf16[32,1280]{1,0:T(8,128)(2,1)S(1)}, bf16[32,1280]{1,0:T(8,128)(2,1)S(1)}, u32[]{:S(2)}, u32[]{:S(2)}) collective-permute-start(bf16[32,1280]{1,0:T(8,128)(2,1)S(1)} %copy-done.16), channel_id=1, source_target_pairs={{0,8},{2,10},{4,12},{6,14},{8,0},{10,2},{12,4},{14,6},{1,9},{3,11}... | collective-permute-start | bytes 245768 | tf_op jit(solution)/shard_map/ppermute | solution.py:273
  33.2 0.6 copy-done.9
  33.8 0.4 collective-permute-start.9
  34.3 4.3 %collective-permute-start.10 = (bf16[32,1280]{1,0:T(8,128)(2,1)S(1)}, bf16[32,1280]{1,0:T(8,128)(2,1)S(1)}, u32[]{:S(2)}, u32[]{:S(2)}) collective-permute-start(bf16[32,1280]{1,0:T(8,128)(2,1)S(1)} %get-tuple-element.48), channel_id=1, source_target_pairs={{0,14},{2,12},{4,10},{6,8},{8,6},{10,4},{12,2},{14,0},{1,15},{3,13... | collective-permute-start | bytes 245768 | tf_op jit(solution)/shard_map/ppermute | solution.py:273
  38.5 0.6 collective-permute-start.11
  39.1 1.0 %collective-permute-done.8.refs_6_ = bf16[32,1280]{1,0:T(8,128)(2,1)S(1)} collective-permute-done((bf16[32,1280]{1,0:T(8,128)(2,1)S(1)}, bf16[32,1280]{1,0:T(8,128)(2,1)S(1)}, u32[]{:S(2)}, u32[]{:S(2)}) %collective-permute-start.8) | collective-permute-done | bytes 81952 | tf_op jit(solution)/shard_map/ppermute | solution.py:273
  40.1 1.0 %collective-permute-start.13 = (bf16[32,1280]{1,0:T(8,128)(2,1)S(1)}, bf16[32,1280]{1,0:T(8,128)(2,1)S(1)}, u32[]{:S(2)}, u32[]{:S(2)}) collective-permute-start(bf16[32,1280]{1,0:T(8,128)(2,1)S(1)} %get-tuple-element.51), channel_id=1, source_target_pairs={{0,10},{2,8},{4,14},{6,12},{8,2},{10,0},{12,6},{14,4},{1,11},{3,9}... | collective-permute-start | bytes 245768 | tf_op jit(solution)/shard_map/ppermute | solution.py:273
  41.1 4.2 %collective-permute-start.14 = (bf16[32,1280]{1,0:T(8,128)(2,1)S(1)}, bf16[32,1280]{1,0:T(8,128)(2,1)S(1)}, u32[]{:S(2)}, u32[]{:S(2)}) collective-permute-start(bf16[32,1280]{1,0:T(8,128)(2,1)S(1)} %get-tuple-element.52), channel_id=1, source_target_pairs={{0,6},{2,4},{4,2},{6,0},{8,14},{10,12},{12,10},{14,8},{1,7},{3,5},... | collective-permute-start | bytes 245768 | tf_op jit(solution)/shard_map/ppermute | solution.py:273
  45.4 3.2 %collective-permute-start.15 = (bf16[32,1280]{1,0:T(8,128)(2,1)S(1)}, bf16[32,1280]{1,0:T(8,128)(2,1)S(1)}, u32[]{:S(2)}, u32[]{:S(2)}) collective-permute-start(bf16[32,1280]{1,0:T(8,128)(2,1)S(1)} %get-tuple-element.54), channel_id=1, source_target_pairs={{0,8},{2,10},{4,12},{6,14},{8,0},{10,2},{12,4},{14,6},{1,9},{3,11}... | collective-permute-start | bytes 245768 | tf_op jit(solution)/shard_map/ppermute | solution.py:273
  48.6 0.7 collective-permute-start.16
  49.3 0.9 %copy-done.8 = bf16[32,1280]{1,0:T(8,128)(2,1)S(1)} copy-done((bf16[32,1280]{1,0:T(8,128)(2,1)S(1)}, bf16[32,1280]{1,0:T(8,128)(2,1)}, u32[]{:S(2)}) %copy-start.8) | copy-done | bytes 81944
  50.2 0.9 %copy-done.10 = bf16[32,1280]{1,0:T(8,128)(2,1)S(1)} copy-done((bf16[32,1280]{1,0:T(8,128)(2,1)S(1)}, bf16[32,1280]{1,0:T(8,128)(2,1)}, u32[]{:S(2)}) %copy-start.10) | copy-done | bytes 81944
  51.0 1.9 %to_host.1 = (bf16[8,32,1280]{2,1,0:T(8,128)(2,1)}, bf16[256,1280]{1,0:T(8,128)(2,1)S(1)}) custom-call(s32[2,8]{1,0:T(2,128)S(1)} %bitcast.6, bf16[32,1280]{1,0:T(8,128)(2,1)S(1)} %get-tuple-element.39.refs_0_, bf16[32,1280]{1,0:T(8,128)(2,1)S(1)} %copy-done.8, bf16[32,1280]{1,0:T(8,128)(2,1)S(1)} %copy-done.10, ...), custom_call_target="tpu_custom_call" | custom-call | flops 1 | bytes 2457664 | tf_op jit(solution)/shard_map/to_host/pallas_call | solution.py:252
  53.0 0.8 %copy-done = bf16[256,1280]{1,0:T(8,128)(2,1)} copy-done((bf16[256,1280]{1,0:T(8,128)(2,1)}, bf16[256,1280]{1,0:T(8,128)(2,1)S(1)}, u32[]{:S(2)}) %copy-start) | copy-done | bytes 655384
  53.8 1.1 %collective-permute-done.16.refs_7_ = bf16[32,1280]{1,0:T(8,128)(2,1)S(1)} collective-permute-done((bf16[32,1280]{1,0:T(8,128)(2,1)S(1)}, bf16[32,1280]{1,0:T(8,128)(2,1)S(1)}, u32[]{:S(2)}, u32[]{:S(2)}) %collective-permute-start.16) | collective-permute-done | bytes 81952 | tf_op jit(solution)/shard_map/ppermute | solution.py:273
  54.9 5.2 %all-to-all-start.1 = ((bf16[8,32,1280]{2,1,0:T(8,128)(2,1)}), bf16[8,32,1280]{2,1,0:T(8,128)(2,1)S(1)}, u32[]{:S(2)}, u32[]{:S(2)}) async-start(bf16[8,32,1280]{2,1,0:T(8,128)(2,1)} %get-tuple-element.56), calls=%async_computation.1 | async-start | bytes 1310720 | tf_op jit(solution)/shard_map/all_to_all | solution.py:269
  60.1 1.1 %copy-done.1 = bf16[256,1280]{1,0:T(8,128)(2,1)S(1)} copy-done((bf16[256,1280]{1,0:T(8,128)(2,1)S(1)}, bf16[256,1280]{1,0:T(8,128)(2,1)}, u32[]{:S(2)}) %copy-start.1) | copy-done | bytes 655384
  61.2 4.6 %attend_back.1 = (bf16[192,1280]{1,0:T(8,128)(2,1)S(1)}, bf16[192,1280]{1,0:T(8,128)(2,1)S(1)}, bf16[192,1280]{1,0:T(8,128)(2,1)S(1)}, bf16[192,1280]{1,0:T(8,12...) custom-call(s32[2,2,8]{2,1,0:T(2,128)S(1)} %bitcast.4, ...), custom_call_target="tpu_custom_call" | custom-call | flops 838860800 | bytes 6406272 | tf_op jit(solution)/shard_map/attend_back/pallas_call | solution.py:252
  65.8 0.1 collective-permute-start.17
  65.8 0.5 collective-permute-start.18
  66.3 0.1 collective-permute-start.19
  66.4 1.3 %collective-permute-done.17.refs_3_ = bf16[192,1280]{1,0:T(8,128)(2,1)S(1)} collective-permute-done((bf16[192,1280]{1,0:T(8,128)(2,1)S(1)}, bf16[192,1280]{1,0:T(8,128)(2,1)S(1)}, u32[]{:S(2)}, u32[]{:S(2)}) %collective-permute-start.17) | collective-permute-done | bytes 491552 | tf_op jit(solution)/shard_map/ppermute | solution.py:249
  67.7 0.7 collective-permute-done.18.refs_4_
  68.4 0.7 collective-permute-done.19.refs_5_
  69.1 1.2 %join.1 = (bf16[192,1280]{1,0:T(8,128)(2,1)}, bf16[192,1280]{1,0:T(8,128)(2,1)}, bf16[192,1280]{1,0:T(8,128)(2,1)}) custom-call(bf16[192,1280]{1,0:T(8,128)(2,1)S(1)} %get-tuple-element.65.refs_0_, bf16[192,1280]{1,0:T(8,128)(2,1)S(1)} %get-tuple-element.66.refs_1_, bf16[192,1280]{1,0:T(8,128)(2,1)S(1)} %get-tuple-element.67.refs_2_, ...), custom_call_target="tpu_custom_call" | custom-call | flops 1 | bytes 4423680 | tf_op jit(solution)/shard_map/join/pallas_call | solution.py:252
  70.3 4.2 %all-to-all-done.1.in_ref = bf16[8,32,1280]{2,1,0:T(8,128)(2,1)S(1)} async-done(((bf16[8,32,1280]{2,1,0:T(8,128)(2,1)}), bf16[8,32,1280]{2,1,0:T(8,128)(2,1)S(1)}, u32[]{:S(2)}, u32[]{:S(2)}) %all-to-all-start.1) | async-done | bytes 655392 | tf_op jit(solution)/shard_map/all_to_all | solution.py:269
  74.4 0.9 %store.1 = bf16[256,1280]{1,0:T(8,128)(2,1)} custom-call(bf16[8,32,1280]{2,1,0:T(8,128)(2,1)S(1)} %all-to-all-done.1.in_ref), custom_call_target="tpu_custom_call" | custom-call | flops 1 | bytes 1310720 | tf_op jit(solution)/shard_map/store/pallas_call | solution.py:252
  (36 shorter events, 0.1 us)
Async XLA Ops:
  0.6 7.4 %copy-start.2 = (bf16[192,1280]{1,0:T(8,128)(2,1)S(1)}, bf16[192,1280]{1,0:T(8,128)(2,1)}, u32[]{:S(2)}) copy-start(bf16[192,1280]{1,0:T(8,128)(2,1)} %refs_0_.1) | copy-start | bytes 1474564
  0.6 7.5 %copy-start.4 = (bf16[192,1280]{1,0:T(8,128)(2,1)S(1)}, bf16[192,1280]{1,0:T(8,128)(2,1)}, u32[]{:S(2)}) copy-start(bf16[192,1280]{1,0:T(8,128)(2,1)} %refs_2_.1) | copy-start | bytes 1474564
  0.7 11.0 %copy-start.11 = (s32[8,2,2]{0,2,1:T(2,128)S(1)}, s32[8,2,2]{0,2,1:T(2,128)}, u32[]{:S(2)}) copy-start(s32[8,2,2]{0,2,1:T(2,128)} %param.10) | copy-start | bytes 388
  0.7 28.3 %all-to-all-start = ((bf16[8,32,1280]{2,1,0:T(8,128)(2,1)}), bf16[8,32,1280]{2,1,0:T(8,128)(2,1)S(1)}, u32[]{:S(2)}, u32[]{:S(2)}) async-start(bf16[8,32,1280]{2,1,0:T(8,128)(2,1)} %bitcast.7), calls=%async_computation | async-start | bytes 1310720 | tf_op jit(solution)/shard_map/all_to_all | solution.py:269
  8.1 1.9 %collective-permute-start = (bf16[192,1280]{1,0:T(8,128)(2,1)S(1)}, bf16[192,1280]{1,0:T(8,128)(2,1)S(1)}, u32[]{:S(2)}, u32[]{:S(2)}) collective-permute-start(bf16[192,1280]{1,0:T(8,128)(2,1)S(1)} %copy-done.2), channel_id=1, source_target_pairs={{0,1},{1,0},{2,3},{3,2},{4,5},{5,4},{6,7},{7,6},{8,9},{9,8},{10,11... | collective-permute-start | bytes 1474568 | tf_op jit(solution)/shard_map/ppermute | solution.py:249
  8.2 3.2 %collective-permute-start.1 = (bf16[192,1280]{1,0:T(8,128)(2,1)S(1)}, bf16[192,1280]{1,0:T(8,128)(2,1)S(1)}, u32[]{:S(2)}, u32[]{:S(2)}) collective-permute-start(bf16[192,1280]{1,0:T(8,128)(2,1)S(1)} %copy-done.4), channel_id=1, source_target_pairs={{0,1},{1,0},{2,3},{3,2},{4,5},{5,4},{6,7},{7,6},{8,9},{9,8},{10,11... | collective-permute-start | bytes 1474568 | tf_op jit(solution)/shard_map/ppermute | solution.py:249
  8.6 3.0 %collective-permute-start.2 = (bf16[192,1280]{1,0:T(8,128)(2,1)}, bf16[192,1280]{1,0:T(8,128)(2,1)S(1)}, u32[]{:S(2)}, u32[]{:S(2)}) collective-permute-start(bf16[192,1280]{1,0:T(8,128)(2,1)} %refs_4_.1), channel_id=1, source_target_pairs={{0,1},{1,0},{2,3},{3,2},{4,5},{5,4},{6,7},{7,6},{8,9},{9,8},{10,11... | collective-permute-start | bytes 1474568 | tf_op jit(solution)/shard_map/ppermute | solution.py:249
  11.6 1.0 %copy-start.3 = (bf16[192,1280]{1,0:T(8,128)(2,1)S(1)}, bf16[192,1280]{1,0:T(8,128)(2,1)}, u32[]{:S(2)}) copy-start(bf16[192,1280]{1,0:T(8,128)(2,1)} %refs_0_.1) | copy-start | bytes 1474564
  12.6 1.0 %copy-start.5 = (bf16[192,1280]{1,0:T(8,128)(2,1)S(1)}, bf16[192,1280]{1,0:T(8,128)(2,1)}, u32[]{:S(2)}) copy-start(bf16[192,1280]{1,0:T(8,128)(2,1)} %refs_2_.1) | copy-start | bytes 1474564
  13.7 1.0 %copy-start.6 = (bf16[192,1280]{1,0:T(8,128)(2,1)S(1)}, bf16[192,1280]{1,0:T(8,128)(2,1)}, u32[]{:S(2)}) copy-start(bf16[192,1280]{1,0:T(8,128)(2,1)} %refs_4_.1) | copy-start | bytes 1474564
  19.5 0.6 copy-start.13
  20.2 0.6 copy-start.15
  20.8 8.8 %collective-permute-start.3 = (bf16[32,1280]{1,0:T(8,128)(2,1)}, bf16[32,1280]{1,0:T(8,128)(2,1)S(1)}, u32[]{:S(2)}, u32[]{:S(2)}) collective-permute-start(bf16[32,1280]{1,0:T(8,128)(2,1)} %get-tuple-element.40), channel_id=1, source_target_pairs={{0,14},{2,12},{4,10},{6,8},{8,6},{10,4},{12,2},{14,0},{1,15},{3,13... | collective-permute-start | bytes 245768 | tf_op jit(solution)/shard_map/ppermute | solution.py:273
  25.5 7.7 %collective-permute-start.4 = (bf16[32,1280]{1,0:T(8,128)(2,1)}, bf16[32,1280]{1,0:T(8,128)(2,1)S(1)}, u32[]{:S(2)}, u32[]{:S(2)}) collective-permute-start(bf16[32,1280]{1,0:T(8,128)(2,1)} %get-tuple-element.41), channel_id=1, source_target_pairs={{0,2},{2,0},{4,6},{6,4},{8,10},{10,8},{12,14},{14,12},{1,3},{3,1},... | collective-permute-start | bytes 245768 | tf_op jit(solution)/shard_map/ppermute | solution.py:273
  26.0 8.2 %collective-permute-start.5 = (bf16[32,1280]{1,0:T(8,128)(2,1)}, bf16[32,1280]{1,0:T(8,128)(2,1)}, u32[]{:S(2)}, u32[]{:S(2)}) collective-permute-start(bf16[32,1280]{1,0:T(8,128)(2,1)} %get-tuple-element.42), channel_id=1, source_target_pairs={{0,4},{2,6},{4,0},{6,2},{8,12},{10,14},{12,8},{14,10},{1,5},{3,7},... | collective-permute-start | bytes 245768 | tf_op jit(solution)/shard_map/ppermute | solution.py:273
  26.0 12.5 %collective-permute-start.6 = (bf16[32,1280]{1,0:T(8,128)(2,1)}, bf16[32,1280]{1,0:T(8,128)(2,1)}, u32[]{:S(2)}, u32[]{:S(2)}) collective-permute-start(bf16[32,1280]{1,0:T(8,128)(2,1)} %get-tuple-element.43), channel_id=1, source_target_pairs={{0,10},{2,8},{4,14},{6,12},{8,2},{10,0},{12,6},{14,4},{1,11},{3,9}... | collective-permute-start | bytes 245768 | tf_op jit(solution)/shard_map/ppermute | solution.py:273
  28.0 0.9 %copy-start.12 = (s32[8,2]{0,1:T(2,128)S(1)}, s32[8,2]{0,1:T(2,128)}, u32[]{:S(2)}) copy-start(s32[8,2]{0,1:T(2,128)} %param.11) | copy-start | bytes 196
  28.1 11.1 %collective-permute-start.7 = (bf16[32,1280]{1,0:T(8,128)(2,1)}, bf16[32,1280]{1,0:T(8,128)(2,1)}, u32[]{:S(2)}, u32[]{:S(2)}) collective-permute-start(bf16[32,1280]{1,0:T(8,128)(2,1)} %get-tuple-element.44), channel_id=1, source_target_pairs={{0,6},{2,4},{4,2},{6,0},{8,14},{10,12},{12,10},{14,8},{1,7},{3,5},... | collective-permute-start | bytes 245768 | tf_op jit(solution)/shard_map/ppermute | solution.py:273
  29.0 1.3 %copy-start.16 = (bf16[32,1280]{1,0:T(8,128)(2,1)S(1)}, bf16[32,1280]{1,0:T(8,128)(2,1)}, u32[]{:S(2)}) copy-start(bf16[32,1280]{1,0:T(8,128)(2,1)} %copy-done.15) | copy-start | bytes 245764
  29.0 4.8 %copy-start.14 = (bf16[32,1280]{1,0:T(8,128)(2,1)S(1)}, bf16[32,1280]{1,0:T(8,128)(2,1)}, u32[]{:S(2)}) copy-start(bf16[32,1280]{1,0:T(8,128)(2,1)} %copy-done.13) | copy-start | bytes 245764
  29.6 0.6 copy-start.7
  30.2 9.9 %collective-permute-start.8 = (bf16[32,1280]{1,0:T(8,128)(2,1)S(1)}, bf16[32,1280]{1,0:T(8,128)(2,1)S(1)}, u32[]{:S(2)}, u32[]{:S(2)}) collective-permute-start(bf16[32,1280]{1,0:T(8,128)(2,1)S(1)} %copy-done.16), channel_id=1, source_target_pairs={{0,8},{2,10},{4,12},{6,14},{8,0},{10,2},{12,4},{14,6},{1,9},{3,11}... | collective-permute-start | bytes 245768 | tf_op jit(solution)/shard_map/ppermute | solution.py:273
  33.2 0.6 copy-start.9
  33.8 7.3 %collective-permute-start.9 = (bf16[32,1280]{1,0:T(8,128)(2,1)S(1)}, bf16[32,1280]{1,0:T(8,128)(2,1)S(1)}, u32[]{:S(2)}, u32[]{:S(2)}) collective-permute-start(bf16[32,1280]{1,0:T(8,128)(2,1)S(1)} %copy-done.14), channel_id=1, source_target_pairs={{0,12},{2,14},{4,8},{6,10},{8,4},{10,6},{12,0},{14,2},{1,13},{3,15... | collective-permute-start | bytes 245768 | tf_op jit(solution)/shard_map/ppermute | solution.py:273
  34.3 11.1 %collective-permute-start.10 = (bf16[32,1280]{1,0:T(8,128)(2,1)S(1)}, bf16[32,1280]{1,0:T(8,128)(2,1)S(1)}, u32[]{:S(2)}, u32[]{:S(2)}) collective-permute-start(bf16[32,1280]{1,0:T(8,128)(2,1)S(1)} %get-tuple-element.48), channel_id=1, source_target_pairs={{0,14},{2,12},{4,10},{6,8},{8,6},{10,4},{12,2},{14,0},{1,15},{3,13... | collective-permute-start | bytes 245768 | tf_op jit(solution)/shard_map/ppermute | solution.py:273
  38.5 10.0 %collective-permute-start.11 = (bf16[32,1280]{1,0:T(8,128)(2,1)S(1)}, bf16[32,1280]{1,0:T(8,128)(2,1)S(1)}, u32[]{:S(2)}, u32[]{:S(2)}) collective-permute-start(bf16[32,1280]{1,0:T(8,128)(2,1)S(1)} %get-tuple-element.49), channel_id=1, source_target_pairs={{0,2},{2,0},{4,6},{6,4},{8,10},{10,8},{12,14},{14,12},{1,3},{3,1},... | collective-permute-start | bytes 245768 | tf_op jit(solution)/shard_map/ppermute | solution.py:273
  39.1 10.2 %collective-permute-start.12 = (bf16[32,1280]{1,0:T(8,128)(2,1)S(1)}, bf16[32,1280]{1,0:T(8,128)(2,1)S(1)}, u32[]{:S(2)}, u32[]{:S(2)}) collective-permute-start(bf16[32,1280]{1,0:T(8,128)(2,1)S(1)} %get-tuple-element.50), channel_id=1, source_target_pairs={{0,4},{2,6},{4,0},{6,2},{8,12},{10,14},{12,8},{14,10},{1,5},{3,7},... | collective-permute-start | bytes 245768 | tf_op jit(solution)/shard_map/ppermute | solution.py:273
  40.1 9.1 %collective-permute-start.13 = (bf16[32,1280]{1,0:T(8,128)(2,1)S(1)}, bf16[32,1280]{1,0:T(8,128)(2,1)S(1)}, u32[]{:S(2)}, u32[]{:S(2)}) collective-permute-start(bf16[32,1280]{1,0:T(8,128)(2,1)S(1)} %get-tuple-element.51), channel_id=1, source_target_pairs={{0,10},{2,8},{4,14},{6,12},{8,2},{10,0},{12,6},{14,4},{1,11},{3,9}... | collective-permute-start | bytes 245768 | tf_op jit(solution)/shard_map/ppermute | solution.py:273
  41.1 8.1 %collective-permute-start.14 = (bf16[32,1280]{1,0:T(8,128)(2,1)S(1)}, bf16[32,1280]{1,0:T(8,128)(2,1)S(1)}, u32[]{:S(2)}, u32[]{:S(2)}) collective-permute-start(bf16[32,1280]{1,0:T(8,128)(2,1)S(1)} %get-tuple-element.52), channel_id=1, source_target_pairs={{0,6},{2,4},{4,2},{6,0},{8,14},{10,12},{12,10},{14,8},{1,7},{3,5},... | collective-permute-start | bytes 245768 | tf_op jit(solution)/shard_map/ppermute | solution.py:273
  45.4 8.5 %collective-permute-start.15 = (bf16[32,1280]{1,0:T(8,128)(2,1)S(1)}, bf16[32,1280]{1,0:T(8,128)(2,1)S(1)}, u32[]{:S(2)}, u32[]{:S(2)}) collective-permute-start(bf16[32,1280]{1,0:T(8,128)(2,1)S(1)} %get-tuple-element.54), channel_id=1, source_target_pairs={{0,8},{2,10},{4,12},{6,14},{8,0},{10,2},{12,4},{14,6},{1,9},{3,11}... | collective-permute-start | bytes 245768 | tf_op jit(solution)/shard_map/ppermute | solution.py:273
  48.6 6.3 %collective-permute-start.16 = (bf16[32,1280]{1,0:T(8,128)(2,1)S(1)}, bf16[32,1280]{1,0:T(8,128)(2,1)S(1)}, u32[]{:S(2)}, u32[]{:S(2)}) collective-permute-start(bf16[32,1280]{1,0:T(8,128)(2,1)S(1)} %get-tuple-element.55), channel_id=1, source_target_pairs={{0,12},{2,14},{4,8},{6,10},{8,4},{10,6},{12,0},{14,2},{1,13},{3,15... | collective-permute-start | bytes 245768 | tf_op jit(solution)/shard_map/ppermute | solution.py:273
  49.3 0.9 %copy-start.8 = (bf16[32,1280]{1,0:T(8,128)(2,1)S(1)}, bf16[32,1280]{1,0:T(8,128)(2,1)}, u32[]{:S(2)}) copy-start(bf16[32,1280]{1,0:T(8,128)(2,1)} %copy-done.7) | copy-start | bytes 245764
  50.2 0.9 %copy-start.10 = (bf16[32,1280]{1,0:T(8,128)(2,1)S(1)}, bf16[32,1280]{1,0:T(8,128)(2,1)}, u32[]{:S(2)}) copy-start(bf16[32,1280]{1,0:T(8,128)(2,1)} %copy-done.9) | copy-start | bytes 245764
  53.0 0.8 %copy-start = (bf16[256,1280]{1,0:T(8,128)(2,1)}, bf16[256,1280]{1,0:T(8,128)(2,1)S(1)}, u32[]{:S(2)}) copy-start(bf16[256,1280]{1,0:T(8,128)(2,1)S(1)} %get-tuple-element.62.refs_5_) | copy-start | bytes 1966084
  54.9 19.5 %all-to-all-start.1 = ((bf16[8,32,1280]{2,1,0:T(8,128)(2,1)}), bf16[8,32,1280]{2,1,0:T(8,128)(2,1)S(1)}, u32[]{:S(2)}, u32[]{:S(2)}) async-start(bf16[8,32,1280]{2,1,0:T(8,128)(2,1)} %get-tuple-element.56), calls=%async_computation.1 | async-start | bytes 1310720 | tf_op jit(solution)/shard_map/all_to_all | solution.py:269
  60.1 1.1 %copy-start.1 = (bf16[256,1280]{1,0:T(8,128)(2,1)S(1)}, bf16[256,1280]{1,0:T(8,128)(2,1)}, u32[]{:S(2)}) copy-start(bf16[256,1280]{1,0:T(8,128)(2,1)} %copy-done) | copy-start | bytes 1966084
  65.8 1.9 %collective-permute-start.17 = (bf16[192,1280]{1,0:T(8,128)(2,1)S(1)}, bf16[192,1280]{1,0:T(8,128)(2,1)S(1)}, u32[]{:S(2)}, u32[]{:S(2)}) collective-permute-start(bf16[192,1280]{1,0:T(8,128)(2,1)S(1)} %get-tuple-element.68), channel_id=1, source_target_pairs={{0,1},{1,0},{2,3},{3,2},{4,5},{5,4},{6,7},{7,6},{8,9},{9,8},{10,11... | collective-permute-start | bytes 1474568 | tf_op jit(solution)/shard_map/ppermute | solution.py:249
  65.8 2.6 %collective-permute-start.18 = (bf16[192,1280]{1,0:T(8,128)(2,1)S(1)}, bf16[192,1280]{1,0:T(8,128)(2,1)S(1)}, u32[]{:S(2)}, u32[]{:S(2)}) collective-permute-start(bf16[192,1280]{1,0:T(8,128)(2,1)S(1)} %get-tuple-element.69), channel_id=1, source_target_pairs={{0,1},{1,0},{2,3},{3,2},{4,5},{5,4},{6,7},{7,6},{8,9},{9,8},{10,11... | collective-permute-start | bytes 1474568 | tf_op jit(solution)/shard_map/ppermute | solution.py:249
  66.3 2.8 %collective-permute-start.19 = (bf16[192,1280]{1,0:T(8,128)(2,1)S(1)}, bf16[192,1280]{1,0:T(8,128)(2,1)S(1)}, u32[]{:S(2)}, u32[]{:S(2)}) collective-permute-start(bf16[192,1280]{1,0:T(8,128)(2,1)S(1)} %get-tuple-element.70), channel_id=1, source_target_pairs={{0,1},{1,0},{2,3},{3,2},{4,5},{5,4},{6,7},{7,6},{8,9},{9,8},{10,11... | collective-permute-start | bytes 1474568 | tf_op jit(solution)/shard_map/ppermute | solution.py:249

commit v6 on v5

--- a/solution.py
+++ b/solution.py
@@ -8,7 +8,7 @@
 
 HEAD_DIM = 80
 STRIP = 256
-STEPS = (0, 7, 1, 2, 5, 3, 4, 6)
+STEPS = (0, 6, 2, 5, 1, 3, 4, 7)
 LAST = 2
 LARGE = pltpu.CompilerParams(vmem_limit_bytes=12 * 1024 * 1024)
 SMALL = pltpu.CompilerParams(vmem_limit_bytes=6 * 1024 * 1024)

time: 75.9 us -> 74.1 us (0.976)
  waiting for transfers between devices: 11.9 us -> 10.6 us
    all_to_all x2, starting transfers between devices: 12.6 us -> 11.4 us  [spread(): return lax.all_to_all(x, 'dp', 0, 0, tiled=True)]
    all_to_all x2, waiting for transfers between devices: 4.16 us -> 3.31 us  [spread(): return lax.all_to_all(x, 'dp', 0, 0, tiled=True)]
  transfers between devices with their start and end apart: 22 -> 22, of which waited for: 9 -> 9; matrix products, arithmetic and copies ran while one was open for 0% -> 0% of each run, Pallas kernels for 17% -> 18%
where the time goes in v6:
time: 74.1 us; the launch traced here: 73.6 us
  starting transfers between devices  38.8 us (52%)
  Pallas kernels  14 us (19%)
  waiting for transfers between devices  10.6 us (14%)
  local copies, waits for them, and re-layouts  9.32 us (13%)
  between operations  0.78 us (1%)
    ppermute x14, starting transfers between devices, exchange(): lax.ppermute(x, 'dp', [(rank, rank ^ step) for rank in range(ranks)])  26.2 us
    pallas_call x6, Pallas kernels, call(): pl.pallas_call(kernel, out_shape=outs, in_specs=[SMEM if x.dtype == jnp.i...  14 us
    all_to_all x2, starting transfers between devices, spread(): return lax.all_to_all(x, 'dp', 0, 0, tiled=True)  11.4 us
    unnamed x34, local copies, waits for them, and re-layouts  9.32 us
    ppermute x6, waiting for transfers between devices, swap(): return lax.ppermute(x, 'seq', [(0, 1), (1, 0)])  5.56 us
    all_to_all x2, waiting for transfers between devices, spread(): return lax.all_to_all(x, 'dp', 0, 0, tiled=True)  3.31 us
    ppermute x14, waiting for transfers between devices, exchange(): lax.ppermute(x, 'dp', [(rank, rank ^ step) for rank in range(ranks)])  1.71 us
  transfers between devices with their start and end apart: 22, of which 9 were waited for; matrix products, arithmetic and copies ran while one was open for 0% of the time, Pallas kernels for 18%

profile of v6, /device:TPU:0, one launch (start us, length us, event | category | flops | bytes accessed | tf_op | source)
XLA Modules:
  0.0 73.6 jit_solution(4846997564168525432)
XLA Ops:
  0.7 7.4 %all-to-all-start = ((bf16[8,32,1280]{2,1,0:T(8,128)(2,1)}), bf16[8,32,1280]{2,1,0:T(8,128)(2,1)S(1)}, u32[]{:S(2)}, u32[]{:S(2)}) async-start(bf16[8,32,1280]{2,1,0:T(8,128)(2,1)} %bitcast.7), calls=%async_computation | async-start | bytes 1310720 | tf_op jit(solution)/shard_map/all_to_all | solution.py:269
  8.1 0.1 collective-permute-start
  8.2 0.5 collective-permute-start.1
  8.6 0.1 collective-permute-start.2
  8.7 1.3 %collective-permute-done.refs_1_ = bf16[192,1280]{1,0:T(8,128)(2,1)S(1)} collective-permute-done((bf16[192,1280]{1,0:T(8,128)(2,1)S(1)}, bf16[192,1280]{1,0:T(8,128)(2,1)S(1)}, u32[]{:S(2)}, u32[]{:S(2)}) %collective-permute-start) | collective-permute-done | bytes 491552 | tf_op jit(solution)/shard_map/ppermute | solution.py:249
  10.0 1.4 %collective-permute-done.1.refs_3_ = bf16[192,1280]{1,0:T(8,128)(2,1)S(1)} collective-permute-done((bf16[192,1280]{1,0:T(8,128)(2,1)S(1)}, bf16[192,1280]{1,0:T(8,128)(2,1)S(1)}, u32[]{:S(2)}, u32[]{:S(2)}) %collective-permute-start.1) | collective-permute-done | bytes 491552 | tf_op jit(solution)/shard_map/ppermute | solution.py:249
  11.4 0.2 collective-permute-done.2.refs_5_
  11.6 1.0 %copy-done.3 = bf16[192,1280]{1,0:T(8,128)(2,1)S(1)} copy-done((bf16[192,1280]{1,0:T(8,128)(2,1)S(1)}, bf16[192,1280]{1,0:T(8,128)(2,1)}, u32[]{:S(2)}) %copy-start.3) | copy-done | bytes 491544
  12.6 1.0 %copy-done.5 = bf16[192,1280]{1,0:T(8,128)(2,1)S(1)} copy-done((bf16[192,1280]{1,0:T(8,128)(2,1)S(1)}, bf16[192,1280]{1,0:T(8,128)(2,1)}, u32[]{:S(2)}) %copy-start.5) | copy-done | bytes 491544
  13.7 1.0 %copy-done.6 = bf16[192,1280]{1,0:T(8,128)(2,1)S(1)} copy-done((bf16[192,1280]{1,0:T(8,128)(2,1)S(1)}, bf16[192,1280]{1,0:T(8,128)(2,1)}, u32[]{:S(2)}) %copy-start.6) | copy-done | bytes 491544
  14.7 4.8 %attend.1 = (bf16[256,1280]{1,0:T(8,128)(2,1)S(1)}, bf16[256,1280]{1,0:T(8,128)(2,1)S(1)}, bf16[1280,256]{1,0:T(8,128)(2,1)S(1)}, bf16[1280,256]{1,0:T(8,128)(2,...) custom-call(s32[2,2,8]{2,1,0:T(2,128)S(1)} %bitcast.3, ...), custom_call_target="tpu_custom_call" | custom-call | flops 335544320 | bytes 6242432 | tf_op jit(solution)/shard_map/attend/pallas_call | solution.py:252
  19.5 0.6 copy-done.13
  20.2 0.6 copy-done.15
  20.8 3.8 %collective-permute-start.3 = (bf16[32,1280]{1,0:T(8,128)(2,1)}, bf16[32,1280]{1,0:T(8,128)(2,1)S(1)}, u32[]{:S(2)}, u32[]{:S(2)}) collective-permute-start(bf16[32,1280]{1,0:T(8,128)(2,1)} %get-tuple-element.40), channel_id=1, source_target_pairs={{0,12},{2,14},{4,8},{6,10},{8,4},{10,6},{12,0},{14,2},{1,13},{3,15... | collective-permute-start | bytes 245768 | tf_op jit(solution)/shard_map/ppermute | solution.py:273
  24.6 0.0 collective-permute-start.4
  24.6 2.0 %collective-permute-start.5 = (bf16[32,1280]{1,0:T(8,128)(2,1)}, bf16[32,1280]{1,0:T(8,128)(2,1)}, u32[]{:S(2)}, u32[]{:S(2)}) collective-permute-start(bf16[32,1280]{1,0:T(8,128)(2,1)} %get-tuple-element.42), channel_id=1, source_target_pairs={{0,10},{2,8},{4,14},{6,12},{8,2},{10,0},{12,6},{14,4},{1,11},{3,9}... | collective-permute-start | bytes 245768 | tf_op jit(solution)/shard_map/ppermute | solution.py:273
  26.6 0.1 collective-permute-start.6
  26.7 2.0 %collective-permute-start.7 = (bf16[32,1280]{1,0:T(8,128)(2,1)}, bf16[32,1280]{1,0:T(8,128)(2,1)}, u32[]{:S(2)}, u32[]{:S(2)}) collective-permute-start(bf16[32,1280]{1,0:T(8,128)(2,1)} %get-tuple-element.44), channel_id=1, source_target_pairs={{0,6},{2,4},{4,2},{6,0},{8,14},{10,12},{12,10},{14,8},{1,7},{3,5},... | collective-permute-start | bytes 245768 | tf_op jit(solution)/shard_map/ppermute | solution.py:273
  28.6 0.6 to_lister.1
  29.3 0.0 copy-start.7
  29.3 0.6 copy-done.7
  29.9 3.3 %collective-permute-start.8 = (bf16[32,1280]{1,0:T(8,128)(2,1)S(1)}, bf16[32,1280]{1,0:T(8,128)(2,1)S(1)}, u32[]{:S(2)}, u32[]{:S(2)}) collective-permute-start(bf16[32,1280]{1,0:T(8,128)(2,1)S(1)} %copy-done.16), channel_id=1, source_target_pairs={{0,8},{2,10},{4,12},{6,14},{8,0},{10,2},{12,4},{14,6},{1,9},{3,11}... | collective-permute-start | bytes 245768 | tf_op jit(solution)/shard_map/ppermute | solution.py:273
  33.2 0.6 copy-done.9
  33.8 1.1 %collective-permute-start.9 = (bf16[32,1280]{1,0:T(8,128)(2,1)S(1)}, bf16[32,1280]{1,0:T(8,128)(2,1)S(1)}, u32[]{:S(2)}, u32[]{:S(2)}) collective-permute-start(bf16[32,1280]{1,0:T(8,128)(2,1)S(1)} %copy-done.14), channel_id=1, source_target_pairs={{0,14},{2,12},{4,10},{6,8},{8,6},{10,4},{12,2},{14,0},{1,15},{3,13... | collective-permute-start | bytes 245768 | tf_op jit(solution)/shard_map/ppermute | solution.py:273
  34.9 2.7 %collective-permute-start.10 = (bf16[32,1280]{1,0:T(8,128)(2,1)S(1)}, bf16[32,1280]{1,0:T(8,128)(2,1)S(1)}, u32[]{:S(2)}, u32[]{:S(2)}) collective-permute-start(bf16[32,1280]{1,0:T(8,128)(2,1)S(1)} %get-tuple-element.48), channel_id=1, source_target_pairs={{0,12},{2,14},{4,8},{6,10},{8,4},{10,6},{12,0},{14,2},{1,13},{3,15... | collective-permute-start | bytes 245768 | tf_op jit(solution)/shard_map/ppermute | solution.py:273
  37.6 2.0 %collective-permute-start.12 = (bf16[32,1280]{1,0:T(8,128)(2,1)S(1)}, bf16[32,1280]{1,0:T(8,128)(2,1)S(1)}, u32[]{:S(2)}, u32[]{:S(2)}) collective-permute-start(bf16[32,1280]{1,0:T(8,128)(2,1)S(1)} %get-tuple-element.50), channel_id=1, source_target_pairs={{0,10},{2,8},{4,14},{6,12},{8,2},{10,0},{12,6},{14,4},{1,11},{3,9}... | collective-permute-start | bytes 245768 | tf_op jit(solution)/shard_map/ppermute | solution.py:273
  39.7 1.1 %collective-permute-start.13 = (bf16[32,1280]{1,0:T(8,128)(2,1)S(1)}, bf16[32,1280]{1,0:T(8,128)(2,1)S(1)}, u32[]{:S(2)}, u32[]{:S(2)}) collective-permute-start(bf16[32,1280]{1,0:T(8,128)(2,1)S(1)} %get-tuple-element.51), channel_id=1, source_target_pairs={{0,2},{2,0},{4,6},{6,4},{8,10},{10,8},{12,14},{14,12},{1,3},{3,1},... | collective-permute-start | bytes 245768 | tf_op jit(solution)/shard_map/ppermute | solution.py:273
  40.8 0.5 collective-permute-done.9.refs_7_
  41.3 3.4 %collective-permute-start.14 = (bf16[32,1280]{1,0:T(8,128)(2,1)S(1)}, bf16[32,1280]{1,0:T(8,128)(2,1)S(1)}, u32[]{:S(2)}, u32[]{:S(2)}) collective-permute-start(bf16[32,1280]{1,0:T(8,128)(2,1)S(1)} %get-tuple-element.52), channel_id=1, source_target_pairs={{0,6},{2,4},{4,2},{6,0},{8,14},{10,12},{12,10},{14,8},{1,7},{3,5},... | collective-permute-start | bytes 245768 | tf_op jit(solution)/shard_map/ppermute | solution.py:273
  44.7 3.3 %collective-permute-start.15 = (bf16[32,1280]{1,0:T(8,128)(2,1)S(1)}, bf16[32,1280]{1,0:T(8,128)(2,1)S(1)}, u32[]{:S(2)}, u32[]{:S(2)}) collective-permute-start(bf16[32,1280]{1,0:T(8,128)(2,1)S(1)} %get-tuple-element.54), channel_id=1, source_target_pairs={{0,8},{2,10},{4,12},{6,14},{8,0},{10,2},{12,4},{14,6},{1,9},{3,11}... | collective-permute-start | bytes 245768 | tf_op jit(solution)/shard_map/ppermute | solution.py:273
  48.0 1.4 %collective-permute-start.16 = (bf16[32,1280]{1,0:T(8,128)(2,1)S(1)}, bf16[32,1280]{1,0:T(8,128)(2,1)S(1)}, u32[]{:S(2)}, u32[]{:S(2)}) collective-permute-start(bf16[32,1280]{1,0:T(8,128)(2,1)S(1)} %get-tuple-element.55), channel_id=1, source_target_pairs={{0,14},{2,12},{4,10},{6,8},{8,6},{10,4},{12,2},{14,0},{1,15},{3,13... | collective-permute-start | bytes 245768 | tf_op jit(solution)/shard_map/ppermute | solution.py:273
  49.4 0.9 %copy-done.8 = bf16[32,1280]{1,0:T(8,128)(2,1)S(1)} copy-done((bf16[32,1280]{1,0:T(8,128)(2,1)S(1)}, bf16[32,1280]{1,0:T(8,128)(2,1)}, u32[]{:S(2)}) %copy-start.8) | copy-done | bytes 81944
  50.3 0.9 %copy-done.10 = bf16[32,1280]{1,0:T(8,128)(2,1)S(1)} copy-done((bf16[32,1280]{1,0:T(8,128)(2,1)S(1)}, bf16[32,1280]{1,0:T(8,128)(2,1)}, u32[]{:S(2)}) %copy-start.10) | copy-done | bytes 81944
  51.2 1.9 %to_host.1 = (bf16[8,32,1280]{2,1,0:T(8,128)(2,1)}, bf16[256,1280]{1,0:T(8,128)(2,1)S(1)}) custom-call(s32[2,8]{1,0:T(2,128)S(1)} %bitcast.6, bf16[32,1280]{1,0:T(8,128)(2,1)S(1)} %get-tuple-element.39.refs_0_, bf16[32,1280]{1,0:T(8,128)(2,1)S(1)} %copy-done.8, bf16[32,1280]{1,0:T(8,128)(2,1)S(1)} %copy-done.10, ...), custom_call_target="tpu_custom_call" | custom-call | flops 1 | bytes 2457664 | tf_op jit(solution)/shard_map/to_host/pallas_call | solution.py:252
  53.1 0.8 %copy-done = bf16[256,1280]{1,0:T(8,128)(2,1)} copy-done((bf16[256,1280]{1,0:T(8,128)(2,1)}, bf16[256,1280]{1,0:T(8,128)(2,1)S(1)}, u32[]{:S(2)}) %copy-start) | copy-done | bytes 655384
  54.0 1.2 %collective-permute-done.16.refs_7_ = bf16[32,1280]{1,0:T(8,128)(2,1)S(1)} collective-permute-done((bf16[32,1280]{1,0:T(8,128)(2,1)S(1)}, bf16[32,1280]{1,0:T(8,128)(2,1)S(1)}, u32[]{:S(2)}, u32[]{:S(2)}) %collective-permute-start.16) | collective-permute-done | bytes 81952 | tf_op jit(solution)/shard_map/ppermute | solution.py:273
  55.2 4.0 %all-to-all-start.1 = ((bf16[8,32,1280]{2,1,0:T(8,128)(2,1)}), bf16[8,32,1280]{2,1,0:T(8,128)(2,1)S(1)}, u32[]{:S(2)}, u32[]{:S(2)}) async-start(bf16[8,32,1280]{2,1,0:T(8,128)(2,1)} %get-tuple-element.56), calls=%async_computation.1 | async-start | bytes 1310720 | tf_op jit(solution)/shard_map/all_to_all | solution.py:269
  59.2 1.1 %copy-done.1 = bf16[256,1280]{1,0:T(8,128)(2,1)S(1)} copy-done((bf16[256,1280]{1,0:T(8,128)(2,1)S(1)}, bf16[256,1280]{1,0:T(8,128)(2,1)}, u32[]{:S(2)}) %copy-start.1) | copy-done | bytes 655384
  60.2 4.6 %attend_back.1 = (bf16[192,1280]{1,0:T(8,128)(2,1)S(1)}, bf16[192,1280]{1,0:T(8,128)(2,1)S(1)}, bf16[192,1280]{1,0:T(8,128)(2,1)S(1)}, bf16[192,1280]{1,0:T(8,12...) custom-call(s32[2,2,8]{2,1,0:T(2,128)S(1)} %bitcast.4, ...), custom_call_target="tpu_custom_call" | custom-call | flops 838860800 | bytes 6406272 | tf_op jit(solution)/shard_map/attend_back/pallas_call | solution.py:252
  64.8 0.1 collective-permute-start.17
  64.9 0.5 collective-permute-start.18
  65.4 0.1 collective-permute-start.19
  65.5 1.3 %collective-permute-done.17.refs_3_ = bf16[192,1280]{1,0:T(8,128)(2,1)S(1)} collective-permute-done((bf16[192,1280]{1,0:T(8,128)(2,1)S(1)}, bf16[192,1280]{1,0:T(8,128)(2,1)S(1)}, u32[]{:S(2)}, u32[]{:S(2)}) %collective-permute-start.17) | collective-permute-done | bytes 491552 | tf_op jit(solution)/shard_map/ppermute | solution.py:249
  66.8 0.7 collective-permute-done.18.refs_4_
  67.5 0.7 collective-permute-done.19.refs_5_
  68.2 1.2 %join.1 = (bf16[192,1280]{1,0:T(8,128)(2,1)}, bf16[192,1280]{1,0:T(8,128)(2,1)}, bf16[192,1280]{1,0:T(8,128)(2,1)}) custom-call(bf16[192,1280]{1,0:T(8,128)(2,1)S(1)} %get-tuple-element.65.refs_0_, bf16[192,1280]{1,0:T(8,128)(2,1)S(1)} %get-tuple-element.66.refs_1_, bf16[192,1280]{1,0:T(8,128)(2,1)S(1)} %get-tuple-element.67.refs_2_, ...), custom_call_target="tpu_custom_call" | custom-call | flops 1 | bytes 4423680 | tf_op jit(solution)/shard_map/join/pallas_call | solution.py:252
  69.3 3.3 %all-to-all-done.1.in_ref = bf16[8,32,1280]{2,1,0:T(8,128)(2,1)S(1)} async-done(((bf16[8,32,1280]{2,1,0:T(8,128)(2,1)}), bf16[8,32,1280]{2,1,0:T(8,128)(2,1)S(1)}, u32[]{:S(2)}, u32[]{:S(2)}) %all-to-all-start.1) | async-done | bytes 655392 | tf_op jit(solution)/shard_map/all_to_all | solution.py:269
  72.7 0.9 %store.1 = bf16[256,1280]{1,0:T(8,128)(2,1)} custom-call(bf16[8,32,1280]{2,1,0:T(8,128)(2,1)S(1)} %all-to-all-done.1.in_ref), custom_call_target="tpu_custom_call" | custom-call | flops 1 | bytes 1310720 | tf_op jit(solution)/shard_map/store/pallas_call | solution.py:252
  (36 shorter events, 0.1 us)
Async XLA Ops:
  0.6 7.4 %copy-start.2 = (bf16[192,1280]{1,0:T(8,128)(2,1)S(1)}, bf16[192,1280]{1,0:T(8,128)(2,1)}, u32[]{:S(2)}) copy-start(bf16[192,1280]{1,0:T(8,128)(2,1)} %refs_0_.1) | copy-start | bytes 1474564
  0.6 7.5 %copy-start.4 = (bf16[192,1280]{1,0:T(8,128)(2,1)S(1)}, bf16[192,1280]{1,0:T(8,128)(2,1)}, u32[]{:S(2)}) copy-start(bf16[192,1280]{1,0:T(8,128)(2,1)} %refs_2_.1) | copy-start | bytes 1474564
  0.7 11.0 %copy-start.11 = (s32[8,2,2]{0,2,1:T(2,128)S(1)}, s32[8,2,2]{0,2,1:T(2,128)}, u32[]{:S(2)}) copy-start(s32[8,2,2]{0,2,1:T(2,128)} %param.10) | copy-start | bytes 388
  0.7 28.0 %all-to-all-start = ((bf16[8,32,1280]{2,1,0:T(8,128)(2,1)}), bf16[8,32,1280]{2,1,0:T(8,128)(2,1)S(1)}, u32[]{:S(2)}, u32[]{:S(2)}) async-start(bf16[8,32,1280]{2,1,0:T(8,128)(2,1)} %bitcast.7), calls=%async_computation | async-start | bytes 1310720 | tf_op jit(solution)/shard_map/all_to_all | solution.py:269
  8.1 1.9 %collective-permute-start = (bf16[192,1280]{1,0:T(8,128)(2,1)S(1)}, bf16[192,1280]{1,0:T(8,128)(2,1)S(1)}, u32[]{:S(2)}, u32[]{:S(2)}) collective-permute-start(bf16[192,1280]{1,0:T(8,128)(2,1)S(1)} %copy-done.2), channel_id=1, source_target_pairs={{0,1},{1,0},{2,3},{3,2},{4,5},{5,4},{6,7},{7,6},{8,9},{9,8},{10,11... | collective-permute-start | bytes 1474568 | tf_op jit(solution)/shard_map/ppermute | solution.py:249
  8.2 3.2 %collective-permute-start.1 = (bf16[192,1280]{1,0:T(8,128)(2,1)S(1)}, bf16[192,1280]{1,0:T(8,128)(2,1)S(1)}, u32[]{:S(2)}, u32[]{:S(2)}) collective-permute-start(bf16[192,1280]{1,0:T(8,128)(2,1)S(1)} %copy-done.4), channel_id=1, source_target_pairs={{0,1},{1,0},{2,3},{3,2},{4,5},{5,4},{6,7},{7,6},{8,9},{9,8},{10,11... | collective-permute-start | bytes 1474568 | tf_op jit(solution)/shard_map/ppermute | solution.py:249
  8.6 3.0 %collective-permute-start.2 = (bf16[192,1280]{1,0:T(8,128)(2,1)}, bf16[192,1280]{1,0:T(8,128)(2,1)S(1)}, u32[]{:S(2)}, u32[]{:S(2)}) collective-permute-start(bf16[192,1280]{1,0:T(8,128)(2,1)} %refs_4_.1), channel_id=1, source_target_pairs={{0,1},{1,0},{2,3},{3,2},{4,5},{5,4},{6,7},{7,6},{8,9},{9,8},{10,11... | collective-permute-start | bytes 1474568 | tf_op jit(solution)/shard_map/ppermute | solution.py:249
  11.6 1.0 %copy-start.3 = (bf16[192,1280]{1,0:T(8,128)(2,1)S(1)}, bf16[192,1280]{1,0:T(8,128)(2,1)}, u32[]{:S(2)}) copy-start(bf16[192,1280]{1,0:T(8,128)(2,1)} %refs_0_.1) | copy-start | bytes 1474564
  12.6 1.0 %copy-start.5 = (bf16[192,1280]{1,0:T(8,128)(2,1)S(1)}, bf16[192,1280]{1,0:T(8,128)(2,1)}, u32[]{:S(2)}) copy-start(bf16[192,1280]{1,0:T(8,128)(2,1)} %refs_2_.1) | copy-start | bytes 1474564
  13.7 1.0 %copy-start.6 = (bf16[192,1280]{1,0:T(8,128)(2,1)S(1)}, bf16[192,1280]{1,0:T(8,128)(2,1)}, u32[]{:S(2)}) copy-start(bf16[192,1280]{1,0:T(8,128)(2,1)} %refs_4_.1) | copy-start | bytes 1474564
  19.5 0.6 copy-start.13
  20.2 0.6 copy-start.15
  20.8 8.4 %collective-permute-start.3 = (bf16[32,1280]{1,0:T(8,128)(2,1)}, bf16[32,1280]{1,0:T(8,128)(2,1)S(1)}, u32[]{:S(2)}, u32[]{:S(2)}) collective-permute-start(bf16[32,1280]{1,0:T(8,128)(2,1)} %get-tuple-element.40), channel_id=1, source_target_pairs={{0,12},{2,14},{4,8},{6,10},{8,4},{10,6},{12,0},{14,2},{1,13},{3,15... | collective-permute-start | bytes 245768 | tf_op jit(solution)/shard_map/ppermute | solution.py:273
  24.6 8.6 %collective-permute-start.4 = (bf16[32,1280]{1,0:T(8,128)(2,1)}, bf16[32,1280]{1,0:T(8,128)(2,1)S(1)}, u32[]{:S(2)}, u32[]{:S(2)}) collective-permute-start(bf16[32,1280]{1,0:T(8,128)(2,1)} %get-tuple-element.41), channel_id=1, source_target_pairs={{0,4},{2,6},{4,0},{6,2},{8,12},{10,14},{12,8},{14,10},{1,5},{3,7},... | collective-permute-start | bytes 245768 | tf_op jit(solution)/shard_map/ppermute | solution.py:273
  24.6 10.3 %collective-permute-start.5 = (bf16[32,1280]{1,0:T(8,128)(2,1)}, bf16[32,1280]{1,0:T(8,128)(2,1)}, u32[]{:S(2)}, u32[]{:S(2)}) collective-permute-start(bf16[32,1280]{1,0:T(8,128)(2,1)} %get-tuple-element.42), channel_id=1, source_target_pairs={{0,10},{2,8},{4,14},{6,12},{8,2},{10,0},{12,6},{14,4},{1,11},{3,9}... | collective-permute-start | bytes 245768 | tf_op jit(solution)/shard_map/ppermute | solution.py:273
  26.6 11.1 %collective-permute-start.6 = (bf16[32,1280]{1,0:T(8,128)(2,1)}, bf16[32,1280]{1,0:T(8,128)(2,1)}, u32[]{:S(2)}, u32[]{:S(2)}) collective-permute-start(bf16[32,1280]{1,0:T(8,128)(2,1)} %get-tuple-element.43), channel_id=1, source_target_pairs={{0,2},{2,0},{4,6},{6,4},{8,10},{10,8},{12,14},{14,12},{1,3},{3,1},... | collective-permute-start | bytes 245768 | tf_op jit(solution)/shard_map/ppermute | solution.py:273
  26.7 2.0 %copy-start.12 = (s32[8,2]{0,1:T(2,128)S(1)}, s32[8,2]{0,1:T(2,128)}, u32[]{:S(2)}) copy-start(s32[8,2]{0,1:T(2,128)} %param.11) | copy-start | bytes 196
  26.7 11.0 %collective-permute-start.7 = (bf16[32,1280]{1,0:T(8,128)(2,1)}, bf16[32,1280]{1,0:T(8,128)(2,1)}, u32[]{:S(2)}, u32[]{:S(2)}) collective-permute-start(bf16[32,1280]{1,0:T(8,128)(2,1)} %get-tuple-element.44), channel_id=1, source_target_pairs={{0,6},{2,4},{4,2},{6,0},{8,14},{10,12},{12,10},{14,8},{1,7},{3,5},... | collective-permute-start | bytes 245768 | tf_op jit(solution)/shard_map/ppermute | solution.py:273
  28.6 1.3 %copy-start.16 = (bf16[32,1280]{1,0:T(8,128)(2,1)S(1)}, bf16[32,1280]{1,0:T(8,128)(2,1)}, u32[]{:S(2)}) copy-start(bf16[32,1280]{1,0:T(8,128)(2,1)} %copy-done.15) | copy-start | bytes 245764
  28.6 5.2 %copy-start.14 = (bf16[32,1280]{1,0:T(8,128)(2,1)S(1)}, bf16[32,1280]{1,0:T(8,128)(2,1)}, u32[]{:S(2)}) copy-start(bf16[32,1280]{1,0:T(8,128)(2,1)} %copy-done.13) | copy-start | bytes 245764
  29.3 0.6 copy-start.7
  29.9 9.8 %collective-permute-start.8 = (bf16[32,1280]{1,0:T(8,128)(2,1)S(1)}, bf16[32,1280]{1,0:T(8,128)(2,1)S(1)}, u32[]{:S(2)}, u32[]{:S(2)}) collective-permute-start(bf16[32,1280]{1,0:T(8,128)(2,1)S(1)} %copy-done.16), channel_id=1, source_target_pairs={{0,8},{2,10},{4,12},{6,14},{8,0},{10,2},{12,4},{14,6},{1,9},{3,11}... | collective-permute-start | bytes 245768 | tf_op jit(solution)/shard_map/ppermute | solution.py:273
  33.2 0.6 copy-start.9
  33.8 7.5 %collective-permute-start.9 = (bf16[32,1280]{1,0:T(8,128)(2,1)S(1)}, bf16[32,1280]{1,0:T(8,128)(2,1)S(1)}, u32[]{:S(2)}, u32[]{:S(2)}) collective-permute-start(bf16[32,1280]{1,0:T(8,128)(2,1)S(1)} %copy-done.14), channel_id=1, source_target_pairs={{0,14},{2,12},{4,10},{6,8},{8,6},{10,4},{12,2},{14,0},{1,15},{3,13... | collective-permute-start | bytes 245768 | tf_op jit(solution)/shard_map/ppermute | solution.py:273
  34.9 9.8 %collective-permute-start.10 = (bf16[32,1280]{1,0:T(8,128)(2,1)S(1)}, bf16[32,1280]{1,0:T(8,128)(2,1)S(1)}, u32[]{:S(2)}, u32[]{:S(2)}) collective-permute-start(bf16[32,1280]{1,0:T(8,128)(2,1)S(1)} %get-tuple-element.48), channel_id=1, source_target_pairs={{0,12},{2,14},{4,8},{6,10},{8,4},{10,6},{12,0},{14,2},{1,13},{3,15... | collective-permute-start | bytes 245768 | tf_op jit(solution)/shard_map/ppermute | solution.py:273
  37.6 10.4 %collective-permute-start.11 = (bf16[32,1280]{1,0:T(8,128)(2,1)S(1)}, bf16[32,1280]{1,0:T(8,128)(2,1)S(1)}, u32[]{:S(2)}, u32[]{:S(2)}) collective-permute-start(bf16[32,1280]{1,0:T(8,128)(2,1)S(1)} %get-tuple-element.49), channel_id=1, source_target_pairs={{0,4},{2,6},{4,0},{6,2},{8,12},{10,14},{12,8},{14,10},{1,5},{3,7},... | collective-permute-start | bytes 245768 | tf_op jit(solution)/shard_map/ppermute | solution.py:273
  37.6 11.8 %collective-permute-start.12 = (bf16[32,1280]{1,0:T(8,128)(2,1)S(1)}, bf16[32,1280]{1,0:T(8,128)(2,1)S(1)}, u32[]{:S(2)}, u32[]{:S(2)}) collective-permute-start(bf16[32,1280]{1,0:T(8,128)(2,1)S(1)} %get-tuple-element.50), channel_id=1, source_target_pairs={{0,10},{2,8},{4,14},{6,12},{8,2},{10,0},{12,6},{14,4},{1,11},{3,9}... | collective-permute-start | bytes 245768 | tf_op jit(solution)/shard_map/ppermute | solution.py:273
  39.7 9.8 %collective-permute-start.13 = (bf16[32,1280]{1,0:T(8,128)(2,1)S(1)}, bf16[32,1280]{1,0:T(8,128)(2,1)S(1)}, u32[]{:S(2)}, u32[]{:S(2)}) collective-permute-start(bf16[32,1280]{1,0:T(8,128)(2,1)S(1)} %get-tuple-element.51), channel_id=1, source_target_pairs={{0,2},{2,0},{4,6},{6,4},{8,10},{10,8},{12,14},{14,12},{1,3},{3,1},... | collective-permute-start | bytes 245768 | tf_op jit(solution)/shard_map/ppermute | solution.py:273
  41.3 8.2 %collective-permute-start.14 = (bf16[32,1280]{1,0:T(8,128)(2,1)S(1)}, bf16[32,1280]{1,0:T(8,128)(2,1)S(1)}, u32[]{:S(2)}, u32[]{:S(2)}) collective-permute-start(bf16[32,1280]{1,0:T(8,128)(2,1)S(1)} %get-tuple-element.52), channel_id=1, source_target_pairs={{0,6},{2,4},{4,2},{6,0},{8,14},{10,12},{12,10},{14,8},{1,7},{3,5},... | collective-permute-start | bytes 245768 | tf_op jit(solution)/shard_map/ppermute | solution.py:273
  44.7 9.3 %collective-permute-start.15 = (bf16[32,1280]{1,0:T(8,128)(2,1)S(1)}, bf16[32,1280]{1,0:T(8,128)(2,1)S(1)}, u32[]{:S(2)}, u32[]{:S(2)}) collective-permute-start(bf16[32,1280]{1,0:T(8,128)(2,1)S(1)} %get-tuple-element.54), channel_id=1, source_target_pairs={{0,8},{2,10},{4,12},{6,14},{8,0},{10,2},{12,4},{14,6},{1,9},{3,11}... | collective-permute-start | bytes 245768 | tf_op jit(solution)/shard_map/ppermute | solution.py:273
  48.0 7.1 %collective-permute-start.16 = (bf16[32,1280]{1,0:T(8,128)(2,1)S(1)}, bf16[32,1280]{1,0:T(8,128)(2,1)S(1)}, u32[]{:S(2)}, u32[]{:S(2)}) collective-permute-start(bf16[32,1280]{1,0:T(8,128)(2,1)S(1)} %get-tuple-element.55), channel_id=1, source_target_pairs={{0,14},{2,12},{4,10},{6,8},{8,6},{10,4},{12,2},{14,0},{1,15},{3,13... | collective-permute-start | bytes 245768 | tf_op jit(solution)/shard_map/ppermute | solution.py:273
  49.4 0.9 %copy-start.8 = (bf16[32,1280]{1,0:T(8,128)(2,1)S(1)}, bf16[32,1280]{1,0:T(8,128)(2,1)}, u32[]{:S(2)}) copy-start(bf16[32,1280]{1,0:T(8,128)(2,1)} %copy-done.7) | copy-start | bytes 245764
  50.3 0.9 %copy-start.10 = (bf16[32,1280]{1,0:T(8,128)(2,1)S(1)}, bf16[32,1280]{1,0:T(8,128)(2,1)}, u32[]{:S(2)}) copy-start(bf16[32,1280]{1,0:T(8,128)(2,1)} %copy-done.9) | copy-start | bytes 245764
  53.1 0.8 %copy-start = (bf16[256,1280]{1,0:T(8,128)(2,1)}, bf16[256,1280]{1,0:T(8,128)(2,1)S(1)}, u32[]{:S(2)}) copy-start(bf16[256,1280]{1,0:T(8,128)(2,1)S(1)} %get-tuple-element.62.refs_5_) | copy-start | bytes 1966084
  55.2 17.5 %all-to-all-start.1 = ((bf16[8,32,1280]{2,1,0:T(8,128)(2,1)}), bf16[8,32,1280]{2,1,0:T(8,128)(2,1)S(1)}, u32[]{:S(2)}, u32[]{:S(2)}) async-start(bf16[8,32,1280]{2,1,0:T(8,128)(2,1)} %get-tuple-element.56), calls=%async_computation.1 | async-start | bytes 1310720 | tf_op jit(solution)/shard_map/all_to_all | solution.py:269
  59.2 1.1 %copy-start.1 = (bf16[256,1280]{1,0:T(8,128)(2,1)S(1)}, bf16[256,1280]{1,0:T(8,128)(2,1)}, u32[]{:S(2)}) copy-start(bf16[256,1280]{1,0:T(8,128)(2,1)} %copy-done) | copy-start | bytes 1966084
  64.8 1.9 %collective-permute-start.17 = (bf16[192,1280]{1,0:T(8,128)(2,1)S(1)}, bf16[192,1280]{1,0:T(8,128)(2,1)S(1)}, u32[]{:S(2)}, u32[]{:S(2)}) collective-permute-start(bf16[192,1280]{1,0:T(8,128)(2,1)S(1)} %get-tuple-element.68), channel_id=1, source_target_pairs={{0,1},{1,0},{2,3},{3,2},{4,5},{5,4},{6,7},{7,6},{8,9},{9,8},{10,11... | collective-permute-start | bytes 1474568 | tf_op jit(solution)/shard_map/ppermute | solution.py:249
  64.9 2.6 %collective-permute-start.18 = (bf16[192,1280]{1,0:T(8,128)(2,1)S(1)}, bf16[192,1280]{1,0:T(8,128)(2,1)S(1)}, u32[]{:S(2)}, u32[]{:S(2)}) collective-permute-start(bf16[192,1280]{1,0:T(8,128)(2,1)S(1)} %get-tuple-element.69), channel_id=1, source_target_pairs={{0,1},{1,0},{2,3},{3,2},{4,5},{5,4},{6,7},{7,6},{8,9},{9,8},{10,11... | collective-permute-start | bytes 1474568 | tf_op jit(solution)/shard_map/ppermute | solution.py:249
  65.4 2.8 %collective-permute-start.19 = (bf16[192,1280]{1,0:T(8,128)(2,1)S(1)}, bf16[192,1280]{1,0:T(8,128)(2,1)S(1)}, u32[]{:S(2)}, u32[]{:S(2)}) collective-permute-start(bf16[192,1280]{1,0:T(8,128)(2,1)S(1)} %get-tuple-element.70), channel_id=1, source_target_pairs={{0,1},{1,0},{2,3},{3,2},{4,5},{5,4},{6,7},{7,6},{8,9},{9,8},{10,11... | collective-permute-start | bytes 1474568 | tf_op jit(solution)/shard_map/ppermute | solution.py:249

commit v7 on v6

--- a/solution.py
+++ b/solution.py
@@ -10,6 +10,7 @@
 STRIP = 256
 STEPS = (0, 6, 2, 5, 1, 3, 4, 7)
 LAST = 2
+HELD = 2
 LARGE = pltpu.CompilerParams(vmem_limit_bytes=12 * 1024 * 1024)
 SMALL = pltpu.CompilerParams(vmem_limit_bytes=6 * 1024 * 1024)
 SMEM = pl.BlockSpec(memory_space=pltpu.SMEM)
@@ -68,11 +69,14 @@
     return pl.ds(pl.multiple_of(to * rows, rows), rows)
 
 
-def to_lister_kernel(dest_ref, in_ref, *out_refs):
+def to_lister_kernel(dest_ref, in_ref, *refs):
     rank = lax.axis_index("dp")
     slot = lax.axis_index("seq")
+    o_refs, out_refs = refs[:HELD], refs[HELD:]
     for step, out_ref in zip(STEPS, out_refs):
         out_ref[...] = in_ref[dest_ref[slot, rank ^ step]]
+    for o_ref, out_ref in zip(o_refs, out_refs[len(STEPS) :]):
+        out_ref[...] = o_ref[...]
 
 
 def to_host_kernel(dest_ref, *refs):
@@ -291,15 +295,15 @@
         work=2,
     )
     if by_pairs:
-        attended = exchange(attended)
         messages = call(
             to_lister_kernel,
-            (destination, grad_spread),
-            [bf16(block, width)] * ranks,
+            (destination, grad_spread, *attended[ranks - HELD :]),
+            [bf16(block, width)] * (ranks + HELD),
             SMALL,
             "to_lister",
         )
-        grad_blocks = exchange(messages)
+        attended = exchange([*attended[: ranks - HELD], *messages[ranks:]])
+        grad_blocks = exchange(messages[:ranks])
         host_order, grad_slot = call(
             to_host_kernel,
             (destination, *attended, *grad_blocks[:-LAST]),

time: 74.1 us -> 73 us (0.985)
  local copies, waits for them, and re-layouts: 9.32 us -> 5.71 us
  starting transfers between devices: 38.8 us -> 40.1 us
  waiting for transfers between devices: 10.6 us -> 11.8 us
    unnamed x34 -> x18, local copies, waits for them, and re-layouts: 9.32 us -> 5.71 us
    ppermute x14, starting transfers between devices: 26.2 us -> 27 us  [exchange(): lax.ppermute(x, 'dp', [(rank, rank ^ step) for rank in range(ranks)])]
    all_to_all x2, waiting for transfers between devices: 3.31 us -> 4.06 us  [spread(): return lax.all_to_all(x, 'dp', 0, 0, tiled=True)]
  transfers between devices with their start and end apart: 22 -> 22, of which waited for: 9 -> 11; matrix products, arithmetic and copies ran while one was open for 0% -> 0% of each run, Pallas kernels for 18% -> 18%
where the time goes in v7:
time: 73 us; the launch traced here: 72.5 us
  starting transfers between devices  40.1 us (55%)
  Pallas kernels  14.1 us (19%)
  waiting for transfers between devices  11.8 us (16%)
  local copies, waits for them, and re-layouts  5.71 us (8%)
  between operations  0.76 us (1%)
    ppermute x14, starting transfers between devices, exchange(): lax.ppermute(x, 'dp', [(rank, rank ^ step) for rank in range(ranks)])  27 us
    pallas_call x6, Pallas kernels, call(): pl.pallas_call(kernel, out_shape=outs, in_specs=[SMEM if x.dtype == jnp.i...  14.1 us
    all_to_all x2, starting transfers between devices, spread(): return lax.all_to_all(x, 'dp', 0, 0, tiled=True)  11.8 us
    unnamed x18, local copies, waits for them, and re-layouts  5.71 us
    ppermute x6, waiting for transfers between devices, swap(): return lax.ppermute(x, 'seq', [(0, 1), (1, 0)])  5.56 us
    all_to_all x2, waiting for transfers between devices, spread(): return lax.all_to_all(x, 'dp', 0, 0, tiled=True)  4.06 us
    ppermute x14, waiting for transfers between devices, exchange(): lax.ppermute(x, 'dp', [(rank, rank ^ step) for rank in range(ranks)])  2.21 us
  transfers between devices with their start and end apart: 22, of which 11 were waited for; matrix products, arithmetic and copies ran while one was open for 0% of the time, Pallas kernels for 18%

profile of v7, /device:TPU:0, one launch (start us, length us, event | category | flops | bytes accessed | tf_op | source)
XLA Modules:
  0.0 72.5 jit_solution(14877537880215432921)
XLA Ops:
  0.7 7.4 %all-to-all-start = ((bf16[8,32,1280]{2,1,0:T(8,128)(2,1)}), bf16[8,32,1280]{2,1,0:T(8,128)(2,1)S(1)}, u32[]{:S(2)}, u32[]{:S(2)}) async-start(bf16[8,32,1280]{2,1,0:T(8,128)(2,1)} %bitcast.7), calls=%async_computation | async-start | bytes 1310720 | tf_op jit(solution)/shard_map/all_to_all | solution.py:273
  8.1 0.1 collective-permute-start
  8.2 0.5 collective-permute-start.1
  8.6 0.1 collective-permute-start.2
  8.7 1.3 %collective-permute-done.refs_1_ = bf16[192,1280]{1,0:T(8,128)(2,1)S(1)} collective-permute-done((bf16[192,1280]{1,0:T(8,128)(2,1)S(1)}, bf16[192,1280]{1,0:T(8,128)(2,1)S(1)}, u32[]{:S(2)}, u32[]{:S(2)}) %collective-permute-start) | collective-permute-done | bytes 491552 | tf_op jit(solution)/shard_map/ppermute | solution.py:253
  10.0 1.4 %collective-permute-done.1.refs_3_ = bf16[192,1280]{1,0:T(8,128)(2,1)S(1)} collective-permute-done((bf16[192,1280]{1,0:T(8,128)(2,1)S(1)}, bf16[192,1280]{1,0:T(8,128)(2,1)S(1)}, u32[]{:S(2)}, u32[]{:S(2)}) %collective-permute-start.1) | collective-permute-done | bytes 491552 | tf_op jit(solution)/shard_map/ppermute | solution.py:253
  11.4 0.2 collective-permute-done.2.refs_5_
  11.6 1.0 %copy-done.3 = bf16[192,1280]{1,0:T(8,128)(2,1)S(1)} copy-done((bf16[192,1280]{1,0:T(8,128)(2,1)S(1)}, bf16[192,1280]{1,0:T(8,128)(2,1)}, u32[]{:S(2)}) %copy-start.3) | copy-done | bytes 491544
  12.6 1.0 %copy-done.5 = bf16[192,1280]{1,0:T(8,128)(2,1)S(1)} copy-done((bf16[192,1280]{1,0:T(8,128)(2,1)S(1)}, bf16[192,1280]{1,0:T(8,128)(2,1)}, u32[]{:S(2)}) %copy-start.5) | copy-done | bytes 491544
  13.7 1.0 %copy-done.6 = bf16[192,1280]{1,0:T(8,128)(2,1)S(1)} copy-done((bf16[192,1280]{1,0:T(8,128)(2,1)S(1)}, bf16[192,1280]{1,0:T(8,128)(2,1)}, u32[]{:S(2)}) %copy-start.6) | copy-done | bytes 491544
  14.7 4.8 %attend.1 = (bf16[256,1280]{1,0:T(8,128)(2,1)S(1)}, bf16[256,1280]{1,0:T(8,128)(2,1)S(1)}, bf16[1280,256]{1,0:T(8,128)(2,1)S(1)}, bf16[1280,256]{1,0:T(8,128)(2,...) custom-call(s32[2,2,8]{2,1,0:T(2,128)S(1)} %bitcast.3, ...), custom_call_target="tpu_custom_call" | custom-call | flops 335544320 | bytes 6242432 | tf_op jit(solution)/shard_map/attend/pallas_call | solution.py:256
  19.5 3.8 %collective-permute-start.3 = (bf16[32,1280]{1,0:T(8,128)(2,1)}, bf16[32,1280]{1,0:T(8,128)(2,1)}, u32[]{:S(2)}, u32[]{:S(2)}) collective-permute-start(bf16[32,1280]{1,0:T(8,128)(2,1)} %get-tuple-element.42), channel_id=1, source_target_pairs={{0,12},{2,14},{4,8},{6,10},{8,4},{10,6},{12,0},{14,2},{1,13},{3,15... | collective-permute-start | bytes 245768 | tf_op jit(solution)/shard_map/ppermute | solution.py:277
  23.3 0.0 collective-permute-start.4
  23.3 2.0 %collective-permute-start.5 = (bf16[32,1280]{1,0:T(8,128)(2,1)}, bf16[32,1280]{1,0:T(8,128)(2,1)}, u32[]{:S(2)}, u32[]{:S(2)}) collective-permute-start(bf16[32,1280]{1,0:T(8,128)(2,1)} %get-tuple-element.44), channel_id=1, source_target_pairs={{0,10},{2,8},{4,14},{6,12},{8,2},{10,0},{12,6},{14,4},{1,11},{3,9}... | collective-permute-start | bytes 245768 | tf_op jit(solution)/shard_map/ppermute | solution.py:277
  25.3 0.1 collective-permute-start.6
  25.4 2.0 %collective-permute-start.7 = (bf16[32,1280]{1,0:T(8,128)(2,1)}, bf16[32,1280]{1,0:T(8,128)(2,1)}, u32[]{:S(2)}, u32[]{:S(2)}) collective-permute-start(bf16[32,1280]{1,0:T(8,128)(2,1)} %get-tuple-element.46), channel_id=1, source_target_pairs={{0,6},{2,4},{4,2},{6,0},{8,14},{10,12},{12,10},{14,8},{1,7},{3,5},... | collective-permute-start | bytes 245768 | tf_op jit(solution)/shard_map/ppermute | solution.py:277
  27.4 0.8 %all-to-all-done.in_ref = bf16[8,32,1280]{2,1,0:T(8,128)(2,1)S(1)} async-done(((bf16[8,32,1280]{2,1,0:T(8,128)(2,1)}), bf16[8,32,1280]{2,1,0:T(8,128)(2,1)S(1)}, u32[]{:S(2)}, u32[]{:S(2)}) %all-to-all-start) | async-done | bytes 655392 | tf_op jit(solution)/shard_map/all_to_all | solution.py:273
  28.2 0.7 copy-done.8
  28.9 0.6 to_lister.1
  29.5 0.0 collective-permute-done.3.refs_1_
  29.5 2.5 %collective-permute-start.8 = (bf16[32,1280]{1,0:T(8,128)(2,1)S(1)}, bf16[32,1280]{1,0:T(8,128)(2,1)S(1)}, u32[]{:S(2)}, u32[]{:S(2)}) collective-permute-start(bf16[32,1280]{1,0:T(8,128)(2,1)S(1)} %get-tuple-element.49), channel_id=1, source_target_pairs={{0,8},{2,10},{4,12},{6,14},{8,0},{10,2},{12,4},{14,6},{1,9},{3,11}... | collective-permute-start | bytes 245768 | tf_op jit(solution)/shard_map/ppermute | solution.py:277
  32.0 0.0 collective-permute-done.4.refs_2_
  32.0 4.0 %collective-permute-start.9 = (bf16[32,1280]{1,0:T(8,128)(2,1)S(1)}, bf16[32,1280]{1,0:T(8,128)(2,1)S(1)}, u32[]{:S(2)}, u32[]{:S(2)}) collective-permute-start(bf16[32,1280]{1,0:T(8,128)(2,1)S(1)} %get-tuple-element.50), channel_id=1, source_target_pairs={{0,14},{2,12},{4,10},{6,8},{8,6},{10,4},{12,2},{14,0},{1,15},{3,13... | collective-permute-start | bytes 245768 | tf_op jit(solution)/shard_map/ppermute | solution.py:277
  36.0 0.1 collective-permute-start.11
  36.1 3.1 %collective-permute-start.12 = (bf16[32,1280]{1,0:T(8,128)(2,1)S(1)}, bf16[32,1280]{1,0:T(8,128)(2,1)S(1)}, u32[]{:S(2)}, u32[]{:S(2)}) collective-permute-start(bf16[32,1280]{1,0:T(8,128)(2,1)S(1)} %get-tuple-element.54), channel_id=1, source_target_pairs={{0,10},{2,8},{4,14},{6,12},{8,2},{10,0},{12,6},{14,4},{1,11},{3,9}... | collective-permute-start | bytes 245768 | tf_op jit(solution)/shard_map/ppermute | solution.py:277
  39.2 1.0 %collective-permute-done.8.refs_6_ = bf16[32,1280]{1,0:T(8,128)(2,1)S(1)} collective-permute-done((bf16[32,1280]{1,0:T(8,128)(2,1)S(1)}, bf16[32,1280]{1,0:T(8,128)(2,1)S(1)}, u32[]{:S(2)}, u32[]{:S(2)}) %collective-permute-start.8) | collective-permute-done | bytes 81952 | tf_op jit(solution)/shard_map/ppermute | solution.py:277
  40.3 2.5 %collective-permute-start.13 = (bf16[32,1280]{1,0:T(8,128)(2,1)S(1)}, bf16[32,1280]{1,0:T(8,128)(2,1)S(1)}, u32[]{:S(2)}, u32[]{:S(2)}) collective-permute-start(bf16[32,1280]{1,0:T(8,128)(2,1)S(1)} %get-tuple-element.55), channel_id=1, source_target_pairs={{0,2},{2,0},{4,6},{6,4},{8,10},{10,8},{12,14},{14,12},{1,3},{3,1},... | collective-permute-start | bytes 245768 | tf_op jit(solution)/shard_map/ppermute | solution.py:277
  42.8 1.6 %collective-permute-start.14 = (bf16[32,1280]{1,0:T(8,128)(2,1)S(1)}, bf16[32,1280]{1,0:T(8,128)(2,1)S(1)}, u32[]{:S(2)}, u32[]{:S(2)}) collective-permute-start(bf16[32,1280]{1,0:T(8,128)(2,1)S(1)} %get-tuple-element.56), channel_id=1, source_target_pairs={{0,6},{2,4},{4,2},{6,0},{8,14},{10,12},{12,10},{14,8},{1,7},{3,5},... | collective-permute-start | bytes 245768 | tf_op jit(solution)/shard_map/ppermute | solution.py:277
  44.4 2.2 %collective-permute-start.15 = (bf16[32,1280]{1,0:T(8,128)(2,1)S(1)}, bf16[32,1280]{1,0:T(8,128)(2,1)S(1)}, u32[]{:S(2)}, u32[]{:S(2)}) collective-permute-start(bf16[32,1280]{1,0:T(8,128)(2,1)S(1)} %get-tuple-element.58), channel_id=1, source_target_pairs={{0,8},{2,10},{4,12},{6,14},{8,0},{10,2},{12,4},{14,6},{1,9},{3,11}... | collective-permute-start | bytes 245768 | tf_op jit(solution)/shard_map/ppermute | solution.py:277
  46.6 3.2 %collective-permute-start.16 = (bf16[32,1280]{1,0:T(8,128)(2,1)S(1)}, bf16[32,1280]{1,0:T(8,128)(2,1)S(1)}, u32[]{:S(2)}, u32[]{:S(2)}) collective-permute-start(bf16[32,1280]{1,0:T(8,128)(2,1)S(1)} %get-tuple-element.59), channel_id=1, source_target_pairs={{0,14},{2,12},{4,10},{6,8},{8,6},{10,4},{12,2},{14,0},{1,15},{3,13... | collective-permute-start | bytes 245768 | tf_op jit(solution)/shard_map/ppermute | solution.py:277
  49.8 0.6 collective-permute-done.12.refs_11_
  50.4 0.0 collective-permute-done.13.refs_12_
  50.4 0.0 collective-permute-done.14.refs_13_
  50.4 2.0 %to_host.1 = (bf16[8,32,1280]{2,1,0:T(8,128)(2,1)}, bf16[256,1280]{1,0:T(8,128)(2,1)S(1)}) custom-call(s32[2,8]{1,0:T(2,128)S(1)} %bitcast.6, bf16[32,1280]{1,0:T(8,128)(2,1)S(1)} %get-tuple-element.41.refs_0_, bf16[32,1280]{1,0:T(8,128)(2,1)} %collective-permute-done.3.refs_1_, bf16[32,1280]{1,0:T(8,128)(2,1)} %collective-permute-done.4.refs_2_, ...), custom_call_target="tpu_custom_call" | custom-call | flops 1 | bytes 2457664 | tf_op jit(solution)/shard_map/to_host/pallas_call | solution.py:256
  52.4 0.8 %copy-done = bf16[256,1280]{1,0:T(8,128)(2,1)} copy-done((bf16[256,1280]{1,0:T(8,128)(2,1)}, bf16[256,1280]{1,0:T(8,128)(2,1)S(1)}, u32[]{:S(2)}) %copy-start) | copy-done | bytes 655384
  53.3 0.6 collective-permute-done.16.refs_7_
  53.8 4.4 %all-to-all-start.1 = ((bf16[8,32,1280]{2,1,0:T(8,128)(2,1)}), bf16[8,32,1280]{2,1,0:T(8,128)(2,1)S(1)}, u32[]{:S(2)}, u32[]{:S(2)}) async-start(bf16[8,32,1280]{2,1,0:T(8,128)(2,1)} %get-tuple-element.60), calls=%async_computation.1 | async-start | bytes 1310720 | tf_op jit(solution)/shard_map/all_to_all | solution.py:273
  58.2 1.1 %copy-done.1 = bf16[256,1280]{1,0:T(8,128)(2,1)S(1)} copy-done((bf16[256,1280]{1,0:T(8,128)(2,1)S(1)}, bf16[256,1280]{1,0:T(8,128)(2,1)}, u32[]{:S(2)}) %copy-start.1) | copy-done | bytes 655384
  59.3 4.6 %attend_back.1 = (bf16[192,1280]{1,0:T(8,128)(2,1)S(1)}, bf16[192,1280]{1,0:T(8,128)(2,1)S(1)}, bf16[192,1280]{1,0:T(8,128)(2,1)S(1)}, bf16[192,1280]{1,0:T(8,12...) custom-call(s32[2,2,8]{2,1,0:T(2,128)S(1)} %bitcast.4, ...), custom_call_target="tpu_custom_call" | custom-call | flops 838860800 | bytes 6406272 | tf_op jit(solution)/shard_map/attend_back/pallas_call | solution.py:256
  63.9 0.1 collective-permute-start.17
  64.0 0.5 collective-permute-start.18
  64.5 0.1 collective-permute-start.19
  64.5 1.3 %collective-permute-done.17.refs_3_ = bf16[192,1280]{1,0:T(8,128)(2,1)S(1)} collective-permute-done((bf16[192,1280]{1,0:T(8,128)(2,1)S(1)}, bf16[192,1280]{1,0:T(8,128)(2,1)S(1)}, u32[]{:S(2)}, u32[]{:S(2)}) %collective-permute-start.17) | collective-permute-done | bytes 491552 | tf_op jit(solution)/shard_map/ppermute | solution.py:253
  65.8 0.7 collective-permute-done.18.refs_4_
  66.5 0.7 collective-permute-done.19.refs_5_
  67.2 1.2 %join.1 = (bf16[192,1280]{1,0:T(8,128)(2,1)}, bf16[192,1280]{1,0:T(8,128)(2,1)}, bf16[192,1280]{1,0:T(8,128)(2,1)}) custom-call(bf16[192,1280]{1,0:T(8,128)(2,1)S(1)} %get-tuple-element.69.refs_0_, bf16[192,1280]{1,0:T(8,128)(2,1)S(1)} %get-tuple-element.70.refs_1_, bf16[192,1280]{1,0:T(8,128)(2,1)S(1)} %get-tuple-element.71.refs_2_, ...), custom_call_target="tpu_custom_call" | custom-call | flops 1 | bytes 4423680 | tf_op jit(solution)/shard_map/join/pallas_call | solution.py:256
  68.4 3.2 %all-to-all-done.1.in_ref = bf16[8,32,1280]{2,1,0:T(8,128)(2,1)S(1)} async-done(((bf16[8,32,1280]{2,1,0:T(8,128)(2,1)}), bf16[8,32,1280]{2,1,0:T(8,128)(2,1)S(1)}, u32[]{:S(2)}, u32[]{:S(2)}) %all-to-all-start.1) | async-done | bytes 655392 | tf_op jit(solution)/shard_map/all_to_all | solution.py:273
  71.6 0.9 %store.1 = bf16[256,1280]{1,0:T(8,128)(2,1)} custom-call(bf16[8,32,1280]{2,1,0:T(8,128)(2,1)S(1)} %all-to-all-done.1.in_ref), custom_call_target="tpu_custom_call" | custom-call | flops 1 | bytes 1310720 | tf_op jit(solution)/shard_map/store/pallas_call | solution.py:256
  (20 shorter events, 0.0 us)
Async XLA Ops:
  0.6 7.4 %copy-start.2 = (bf16[192,1280]{1,0:T(8,128)(2,1)S(1)}, bf16[192,1280]{1,0:T(8,128)(2,1)}, u32[]{:S(2)}) copy-start(bf16[192,1280]{1,0:T(8,128)(2,1)} %refs_0_.1) | copy-start | bytes 1474564
  0.6 7.5 %copy-start.4 = (bf16[192,1280]{1,0:T(8,128)(2,1)S(1)}, bf16[192,1280]{1,0:T(8,128)(2,1)}, u32[]{:S(2)}) copy-start(bf16[192,1280]{1,0:T(8,128)(2,1)} %refs_2_.1) | copy-start | bytes 1474564
  0.7 11.0 %copy-start.7 = (s32[8,2,2]{0,2,1:T(2,128)S(1)}, s32[8,2,2]{0,2,1:T(2,128)}, u32[]{:S(2)}) copy-start(s32[8,2,2]{0,2,1:T(2,128)} %param.10) | copy-start | bytes 388
  0.7 27.5 %all-to-all-start = ((bf16[8,32,1280]{2,1,0:T(8,128)(2,1)}), bf16[8,32,1280]{2,1,0:T(8,128)(2,1)S(1)}, u32[]{:S(2)}, u32[]{:S(2)}) async-start(bf16[8,32,1280]{2,1,0:T(8,128)(2,1)} %bitcast.7), calls=%async_computation | async-start | bytes 1310720 | tf_op jit(solution)/shard_map/all_to_all | solution.py:273
  8.1 1.9 %collective-permute-start = (bf16[192,1280]{1,0:T(8,128)(2,1)S(1)}, bf16[192,1280]{1,0:T(8,128)(2,1)S(1)}, u32[]{:S(2)}, u32[]{:S(2)}) collective-permute-start(bf16[192,1280]{1,0:T(8,128)(2,1)S(1)} %copy-done.2), channel_id=1, source_target_pairs={{0,1},{1,0},{2,3},{3,2},{4,5},{5,4},{6,7},{7,6},{8,9},{9,8},{10,11... | collective-permute-start | bytes 1474568 | tf_op jit(solution)/shard_map/ppermute | solution.py:253
  8.2 3.2 %collective-permute-start.1 = (bf16[192,1280]{1,0:T(8,128)(2,1)S(1)}, bf16[192,1280]{1,0:T(8,128)(2,1)S(1)}, u32[]{:S(2)}, u32[]{:S(2)}) collective-permute-start(bf16[192,1280]{1,0:T(8,128)(2,1)S(1)} %copy-done.4), channel_id=1, source_target_pairs={{0,1},{1,0},{2,3},{3,2},{4,5},{5,4},{6,7},{7,6},{8,9},{9,8},{10,11... | collective-permute-start | bytes 1474568 | tf_op jit(solution)/shard_map/ppermute | solution.py:253
  8.6 3.0 %collective-permute-start.2 = (bf16[192,1280]{1,0:T(8,128)(2,1)}, bf16[192,1280]{1,0:T(8,128)(2,1)S(1)}, u32[]{:S(2)}, u32[]{:S(2)}) collective-permute-start(bf16[192,1280]{1,0:T(8,128)(2,1)} %refs_4_.1), channel_id=1, source_target_pairs={{0,1},{1,0},{2,3},{3,2},{4,5},{5,4},{6,7},{7,6},{8,9},{9,8},{10,11... | collective-permute-start | bytes 1474568 | tf_op jit(solution)/shard_map/ppermute | solution.py:253
  11.6 1.0 %copy-start.3 = (bf16[192,1280]{1,0:T(8,128)(2,1)S(1)}, bf16[192,1280]{1,0:T(8,128)(2,1)}, u32[]{:S(2)}) copy-start(bf16[192,1280]{1,0:T(8,128)(2,1)} %refs_0_.1) | copy-start | bytes 1474564
  12.6 1.0 %copy-start.5 = (bf16[192,1280]{1,0:T(8,128)(2,1)S(1)}, bf16[192,1280]{1,0:T(8,128)(2,1)}, u32[]{:S(2)}) copy-start(bf16[192,1280]{1,0:T(8,128)(2,1)} %refs_2_.1) | copy-start | bytes 1474564
  13.7 1.0 %copy-start.6 = (bf16[192,1280]{1,0:T(8,128)(2,1)S(1)}, bf16[192,1280]{1,0:T(8,128)(2,1)}, u32[]{:S(2)}) copy-start(bf16[192,1280]{1,0:T(8,128)(2,1)} %refs_4_.1) | copy-start | bytes 1474564
  19.5 10.0 %collective-permute-start.3 = (bf16[32,1280]{1,0:T(8,128)(2,1)}, bf16[32,1280]{1,0:T(8,128)(2,1)}, u32[]{:S(2)}, u32[]{:S(2)}) collective-permute-start(bf16[32,1280]{1,0:T(8,128)(2,1)} %get-tuple-element.42), channel_id=1, source_target_pairs={{0,12},{2,14},{4,8},{6,10},{8,4},{10,6},{12,0},{14,2},{1,13},{3,15... | collective-permute-start | bytes 245768 | tf_op jit(solution)/shard_map/ppermute | solution.py:277
  23.3 8.7 %collective-permute-start.4 = (bf16[32,1280]{1,0:T(8,128)(2,1)}, bf16[32,1280]{1,0:T(8,128)(2,1)}, u32[]{:S(2)}, u32[]{:S(2)}) collective-permute-start(bf16[32,1280]{1,0:T(8,128)(2,1)} %get-tuple-element.43), channel_id=1, source_target_pairs={{0,4},{2,6},{4,0},{6,2},{8,12},{10,14},{12,8},{14,10},{1,5},{3,7},... | collective-permute-start | bytes 245768 | tf_op jit(solution)/shard_map/ppermute | solution.py:277
  23.3 12.7 %collective-permute-start.5 = (bf16[32,1280]{1,0:T(8,128)(2,1)}, bf16[32,1280]{1,0:T(8,128)(2,1)}, u32[]{:S(2)}, u32[]{:S(2)}) collective-permute-start(bf16[32,1280]{1,0:T(8,128)(2,1)} %get-tuple-element.44), channel_id=1, source_target_pairs={{0,10},{2,8},{4,14},{6,12},{8,2},{10,0},{12,6},{14,4},{1,11},{3,9}... | collective-permute-start | bytes 245768 | tf_op jit(solution)/shard_map/ppermute | solution.py:277
  25.3 10.7 %collective-permute-start.6 = (bf16[32,1280]{1,0:T(8,128)(2,1)}, bf16[32,1280]{1,0:T(8,128)(2,1)}, u32[]{:S(2)}, u32[]{:S(2)}) collective-permute-start(bf16[32,1280]{1,0:T(8,128)(2,1)} %get-tuple-element.45), channel_id=1, source_target_pairs={{0,2},{2,0},{4,6},{6,4},{8,10},{10,8},{12,14},{14,12},{1,3},{3,1},... | collective-permute-start | bytes 245768 | tf_op jit(solution)/shard_map/ppermute | solution.py:277
  25.4 10.7 %collective-permute-start.7 = (bf16[32,1280]{1,0:T(8,128)(2,1)}, bf16[32,1280]{1,0:T(8,128)(2,1)}, u32[]{:S(2)}, u32[]{:S(2)}) collective-permute-start(bf16[32,1280]{1,0:T(8,128)(2,1)} %get-tuple-element.46), channel_id=1, source_target_pairs={{0,6},{2,4},{4,2},{6,0},{8,14},{10,12},{12,10},{14,8},{1,7},{3,5},... | collective-permute-start | bytes 245768 | tf_op jit(solution)/shard_map/ppermute | solution.py:277
  28.2 0.7 copy-start.8
  29.5 10.8 %collective-permute-start.8 = (bf16[32,1280]{1,0:T(8,128)(2,1)S(1)}, bf16[32,1280]{1,0:T(8,128)(2,1)S(1)}, u32[]{:S(2)}, u32[]{:S(2)}) collective-permute-start(bf16[32,1280]{1,0:T(8,128)(2,1)S(1)} %get-tuple-element.49), channel_id=1, source_target_pairs={{0,8},{2,10},{4,12},{6,14},{8,0},{10,2},{12,4},{14,6},{1,9},{3,11}... | collective-permute-start | bytes 245768 | tf_op jit(solution)/shard_map/ppermute | solution.py:277
  32.0 10.8 %collective-permute-start.9 = (bf16[32,1280]{1,0:T(8,128)(2,1)S(1)}, bf16[32,1280]{1,0:T(8,128)(2,1)S(1)}, u32[]{:S(2)}, u32[]{:S(2)}) collective-permute-start(bf16[32,1280]{1,0:T(8,128)(2,1)S(1)} %get-tuple-element.50), channel_id=1, source_target_pairs={{0,14},{2,12},{4,10},{6,8},{8,6},{10,4},{12,2},{14,0},{1,15},{3,13... | collective-permute-start | bytes 245768 | tf_op jit(solution)/shard_map/ppermute | solution.py:277
  36.0 8.4 %collective-permute-start.10 = (bf16[32,1280]{1,0:T(8,128)(2,1)S(1)}, bf16[32,1280]{1,0:T(8,128)(2,1)S(1)}, u32[]{:S(2)}, u32[]{:S(2)}) collective-permute-start(bf16[32,1280]{1,0:T(8,128)(2,1)S(1)} %get-tuple-element.52), channel_id=1, source_target_pairs={{0,12},{2,14},{4,8},{6,10},{8,4},{10,6},{12,0},{14,2},{1,13},{3,15... | collective-permute-start | bytes 245768 | tf_op jit(solution)/shard_map/ppermute | solution.py:277
  36.0 10.6 %collective-permute-start.11 = (bf16[32,1280]{1,0:T(8,128)(2,1)S(1)}, bf16[32,1280]{1,0:T(8,128)(2,1)S(1)}, u32[]{:S(2)}, u32[]{:S(2)}) collective-permute-start(bf16[32,1280]{1,0:T(8,128)(2,1)S(1)} %get-tuple-element.53), channel_id=1, source_target_pairs={{0,4},{2,6},{4,0},{6,2},{8,12},{10,14},{12,8},{14,10},{1,5},{3,7},... | collective-permute-start | bytes 245768 | tf_op jit(solution)/shard_map/ppermute | solution.py:277
  36.1 14.3 %collective-permute-start.12 = (bf16[32,1280]{1,0:T(8,128)(2,1)S(1)}, bf16[32,1280]{1,0:T(8,128)(2,1)S(1)}, u32[]{:S(2)}, u32[]{:S(2)}) collective-permute-start(bf16[32,1280]{1,0:T(8,128)(2,1)S(1)} %get-tuple-element.54), channel_id=1, source_target_pairs={{0,10},{2,8},{4,14},{6,12},{8,2},{10,0},{12,6},{14,4},{1,11},{3,9}... | collective-permute-start | bytes 245768 | tf_op jit(solution)/shard_map/ppermute | solution.py:277
  40.3 10.1 %collective-permute-start.13 = (bf16[32,1280]{1,0:T(8,128)(2,1)S(1)}, bf16[32,1280]{1,0:T(8,128)(2,1)S(1)}, u32[]{:S(2)}, u32[]{:S(2)}) collective-permute-start(bf16[32,1280]{1,0:T(8,128)(2,1)S(1)} %get-tuple-element.55), channel_id=1, source_target_pairs={{0,2},{2,0},{4,6},{6,4},{8,10},{10,8},{12,14},{14,12},{1,3},{3,1},... | collective-permute-start | bytes 245768 | tf_op jit(solution)/shard_map/ppermute | solution.py:277
  42.8 7.6 %collective-permute-start.14 = (bf16[32,1280]{1,0:T(8,128)(2,1)S(1)}, bf16[32,1280]{1,0:T(8,128)(2,1)S(1)}, u32[]{:S(2)}, u32[]{:S(2)}) collective-permute-start(bf16[32,1280]{1,0:T(8,128)(2,1)S(1)} %get-tuple-element.56), channel_id=1, source_target_pairs={{0,6},{2,4},{4,2},{6,0},{8,14},{10,12},{12,10},{14,8},{1,7},{3,5},... | collective-permute-start | bytes 245768 | tf_op jit(solution)/shard_map/ppermute | solution.py:277
  44.4 8.9 %collective-permute-start.15 = (bf16[32,1280]{1,0:T(8,128)(2,1)S(1)}, bf16[32,1280]{1,0:T(8,128)(2,1)S(1)}, u32[]{:S(2)}, u32[]{:S(2)}) collective-permute-start(bf16[32,1280]{1,0:T(8,128)(2,1)S(1)} %get-tuple-element.58), channel_id=1, source_target_pairs={{0,8},{2,10},{4,12},{6,14},{8,0},{10,2},{12,4},{14,6},{1,9},{3,11}... | collective-permute-start | bytes 245768 | tf_op jit(solution)/shard_map/ppermute | solution.py:277
  46.6 7.2 %collective-permute-start.16 = (bf16[32,1280]{1,0:T(8,128)(2,1)S(1)}, bf16[32,1280]{1,0:T(8,128)(2,1)S(1)}, u32[]{:S(2)}, u32[]{:S(2)}) collective-permute-start(bf16[32,1280]{1,0:T(8,128)(2,1)S(1)} %get-tuple-element.59), channel_id=1, source_target_pairs={{0,14},{2,12},{4,10},{6,8},{8,6},{10,4},{12,2},{14,0},{1,15},{3,13... | collective-permute-start | bytes 245768 | tf_op jit(solution)/shard_map/ppermute | solution.py:277
  52.4 0.8 %copy-start = (bf16[256,1280]{1,0:T(8,128)(2,1)}, bf16[256,1280]{1,0:T(8,128)(2,1)S(1)}, u32[]{:S(2)}) copy-start(bf16[256,1280]{1,0:T(8,128)(2,1)S(1)} %get-tuple-element.66.refs_5_) | copy-start | bytes 1966084
  53.8 17.8 %all-to-all-start.1 = ((bf16[8,32,1280]{2,1,0:T(8,128)(2,1)}), bf16[8,32,1280]{2,1,0:T(8,128)(2,1)S(1)}, u32[]{:S(2)}, u32[]{:S(2)}) async-start(bf16[8,32,1280]{2,1,0:T(8,128)(2,1)} %get-tuple-element.60), calls=%async_computation.1 | async-start | bytes 1310720 | tf_op jit(solution)/shard_map/all_to_all | solution.py:273
  58.2 1.1 %copy-start.1 = (bf16[256,1280]{1,0:T(8,128)(2,1)S(1)}, bf16[256,1280]{1,0:T(8,128)(2,1)}, u32[]{:S(2)}) copy-start(bf16[256,1280]{1,0:T(8,128)(2,1)} %copy-done) | copy-start | bytes 1966084
  63.9 1.9 %collective-permute-start.17 = (bf16[192,1280]{1,0:T(8,128)(2,1)S(1)}, bf16[192,1280]{1,0:T(8,128)(2,1)S(1)}, u32[]{:S(2)}, u32[]{:S(2)}) collective-permute-start(bf16[192,1280]{1,0:T(8,128)(2,1)S(1)} %get-tuple-element.72), channel_id=1, source_target_pairs={{0,1},{1,0},{2,3},{3,2},{4,5},{5,4},{6,7},{7,6},{8,9},{9,8},{10,11... | collective-permute-start | bytes 1474568 | tf_op jit(solution)/shard_map/ppermute | solution.py:253
  64.0 2.6 %collective-permute-start.18 = (bf16[192,1280]{1,0:T(8,128)(2,1)S(1)}, bf16[192,1280]{1,0:T(8,128)(2,1)S(1)}, u32[]{:S(2)}, u32[]{:S(2)}) collective-permute-start(bf16[192,1280]{1,0:T(8,128)(2,1)S(1)} %get-tuple-element.73), channel_id=1, source_target_pairs={{0,1},{1,0},{2,3},{3,2},{4,5},{5,4},{6,7},{7,6},{8,9},{9,8},{10,11... | collective-permute-start | bytes 1474568 | tf_op jit(solution)/shard_map/ppermute | solution.py:253
  64.5 2.8 %collective-permute-start.19 = (bf16[192,1280]{1,0:T(8,128)(2,1)S(1)}, bf16[192,1280]{1,0:T(8,128)(2,1)S(1)}, u32[]{:S(2)}, u32[]{:S(2)}) collective-permute-start(bf16[192,1280]{1,0:T(8,128)(2,1)S(1)} %get-tuple-element.74), channel_id=1, source_target_pairs={{0,1},{1,0},{2,3},{3,2},{4,5},{5,4},{6,7},{7,6},{8,9},{9,8},{10,11... | collective-permute-start | bytes 1474568 | tf_op jit(solution)/shard_map/ppermute | solution.py:253
